TPU v7x, 32 devices: a whole 2x2x4 slice. The times are simulated.
32 devices in a mesh: parts: 2 (over x), img: 16 (over z, y, core).
Axes of the slice: x: 2, y: 2, z: 4, core: 2. Of those that a mesh axis runs over, the one named last changes fastest.
Arguments:
- images: bfloat16 [2048, 16384], P(('parts', 'img')), parts along dimension 0, may hold values from -28 to 28
- groups: int32 [2048], P(('parts', 'img')), parts along dimension 0, may hold values from 0 to 7
- shifts: int32 [18, 2], P('parts'), parts along dimension 0, may hold values from -3 to 3
- volume: bfloat16 [32768, 256], P(('parts', 'img')), parts along dimension 0, may hold values from -6 to 6
- owner: int32 [8192, 1], P('parts'), parts along dimension 0, may hold values from 0 to 15; in each aligned block of 4096 rows (0 to 4095, 4096 to 8191, ...) at most 384 rows name the same one
- local: int32 [8192], P('parts'), parts along dimension 0, may hold values from 0 to 1023
- table_id: int32 [8192], P('parts'), parts along dimension 0, may hold values from 0 to 7
- interp: bfloat16 [8, 128, 128], replicated, may hold values from -0.5 to 0.5
- ctf: float32 [16, 8192], P('parts'), parts along dimension 0, may hold values from 0.2 to 1
Outputs:
- new_map: float32 [32768, 256], P(('parts', 'img')), parts along dimension 0
- evidence: float32 [2048], P(('parts', 'img')), parts along dimension 0
There are 2 independent parts, one for each index of `parts`. A program takes and returns all parts, laid end to end along the dimension named above; an argument that names none is the same for every part. Nothing has to cross between parts.
Inputs may be any that keep to these rules, and one draw needn't show every extreme that they name: `owner`: no slab is named by more than 384 slice blocks, a bound that some block reaches.
All inputs are finite; a program needn't handle non-finite values.
Results may differ from a plain program's by a relative error of at most 0.012.
The roundings to bfloat16 on the way count: a program that leaves them out, or rounds other values in their place, can miss the bound.
Values may be sent and summed in bfloat16 or wider, within the bound.
No kernel may reach another device: no remote copies, remote signals or barrier semaphores. Data moves between devices by JAX's collectives and lax.ppermute only.
A program may use at most 128 MiB of HBM per device.

v0:
```python
import math

import jax
import jax.numpy as jnp
from jax import lax
from jax.sharding import PartitionSpec as P

BW = 128
KB = 64
R = 64


exact_mode = lax.Precision.HIGHEST


def phases(shifts):
    freq_x = (jnp.arange(BW) - BW // 2).astype(jnp.float32)
    freq_y = jnp.arange(KB).astype(jnp.float32)
    shift_x = shifts[:, 0].astype(jnp.float32)
    shift_y = shifts[:, 1].astype(jnp.float32)
    angles = (
        2.0
        * math.pi
        / BW
        * (
            shift_x[:, None, None] * freq_x[None, None, :]
            + shift_y[:, None, None] * freq_y[None, :, None]
        )
    )
    return (jnp.cos(angles), jnp.sin(angles))


def pick_table(blocks_in, table_ids, interp, adjoint):
    tables = interp.astype(jnp.float32)
    if adjoint:
        expanded = jnp.einsum("ncj,tjv->ntcv", blocks_in, tables, precision=exact_mode)
    else:
        expanded = jnp.einsum("ncv,tjv->ntcj", blocks_in, tables, precision=exact_mode)
    one_hot = (table_ids[:, None] == jnp.arange(interp.shape[0])[None, :]).astype(jnp.float32)
    return jnp.sum(expanded * one_hot[:, :, None, None], axis=1)


def score_images(image_rows, group_ids, slices, shifts, ctf):
    refs = slices.shape[0]
    count = image_rows.shape[0]
    cosine, sine_values = phases(shifts)
    slice_values = slices.astype(jnp.float32)
    powers = (slice_values[:, :, 0] ** 2 + slice_values[:, :, 1] ** 2).reshape(refs, KB * BW)
    norm_terms = jnp.dot(ctf * ctf, powers.T, precision=exact_mode)
    one_hot = (group_ids[:, None] == jnp.arange(ctf.shape[0])[None, :]).astype(jnp.float32)
    image_ctf = jnp.dot(one_hot, ctf, precision=exact_mode).reshape(count, KB, 1, BW)
    weighted = (
        (image_rows.astype(jnp.float32).reshape(count, KB, 2, BW) * image_ctf)
        .astype(jnp.bfloat16)
        .reshape(count, KB * 2 * BW)
    )
    image_norms = jnp.dot(one_hot, norm_terms, precision=exact_mode)
    scale_factor = 1.0 / math.sqrt(KB * BW)
    score_list = []
    for number in range(cosine.shape[0]):
        real_part = (
            slice_values[:, :, 0] * cosine[number] - slice_values[:, :, 1] * sine_values[number]
        )
        imag_part = (
            slice_values[:, :, 0] * sine_values[number] + slice_values[:, :, 1] * cosine[number]
        )
        rotated = (
            jnp.stack([real_part, imag_part], axis=2)
            .astype(jnp.bfloat16)
            .reshape(refs, KB * 2 * BW)
        )
        intersection = lax.dot_general(
            weighted, rotated, (((1,), (1,)), ((), ())), preferred_element_type=jnp.float32
        )
        score_list.append((intersection - 0.5 * image_norms) * scale_factor)
    scores = jnp.stack(score_list, axis=1)
    maximum = jnp.max(scores, axis=(1, 2))
    exponent = jnp.exp(scores - maximum[:, None, None])
    summed = jnp.sum(exponent, axis=(1, 2))
    evidence = maximum + jnp.log(summed)
    weights = (exponent / summed[:, None, None]).astype(jnp.bfloat16)
    accumulated = jnp.zeros((refs, KB, 2, BW), jnp.float32)
    for number in range(cosine.shape[0]):
        partial_sum = lax.dot_general(
            weights[:, number, :],
            weighted,
            (((0,), (0,)), ((), ())),
            preferred_element_type=jnp.float32,
        ).reshape(refs, KB, 2, BW)
        back_real = (
            partial_sum[:, :, 0] * cosine[number] + partial_sum[:, :, 1] * sine_values[number]
        )
        back_imag = (
            partial_sum[:, :, 1] * cosine[number] - partial_sum[:, :, 0] * sine_values[number]
        )
        accumulated = accumulated + jnp.stack([back_real, back_imag], axis=2)
    return (accumulated, evidence)


def per_device(images, groups, shifts, volume, owner, local, table_id, interp, ctf):
    devices = lax.axis_size("img")
    myself = lax.axis_index("img")
    block_count = R * KB
    capacity = max(2, 3 * block_count // (2 * devices))
    owners = owner[:, 0]
    member = (owners[:, None] == jnp.arange(devices, dtype=jnp.int32)[None, :]).astype(jnp.int32)
    position = jnp.sum(jnp.cumsum(member, axis=0) * member, axis=1) - 1
    target = owners * capacity + position
    owned = owners == myself
    slot_source = (
        jnp.full((capacity,), block_count, jnp.int32)
        .at[jnp.where(owned, position, capacity)]
        .set(jnp.arange(block_count, dtype=jnp.int32), mode="drop")
    )
    local_padded = jnp.concatenate([local, jnp.zeros((1,), jnp.int32)])
    table_padded = jnp.concatenate([table_id, jnp.zeros((1,), jnp.int32)])
    slot_local = local_padded[slot_source]
    slot_table = table_padded[slot_source]
    volume_rows = volume[slot_local].astype(jnp.float32).reshape(capacity, 2, BW)
    own_slices = (
        pick_table(volume_rows, slot_table, interp, False)
        .astype(jnp.bfloat16)
        .reshape(capacity, 2 * BW)
    )
    gathered = lax.all_gather(own_slices, "img", axis=0, tiled=True)
    slices = gathered[target].reshape(R, KB, 2, BW)
    accumulated, evidence = score_images(images, groups, slices, shifts, ctf)
    acc_rows = accumulated.reshape(block_count, 2 * BW)
    outbound = jnp.zeros((devices * capacity, 2 * BW), jnp.float32).at[target].set(acc_rows)
    received = lax.psum_scatter(outbound, "img", scatter_dimension=0, tiled=True)
    contrib = pick_table(received.reshape(capacity, 2, BW), slot_table, interp, True).reshape(
        capacity, 2 * BW
    )
    new_map = volume.astype(jnp.float32).at[slot_local].add(contrib)
    return (new_map, evidence)


def solution(mesh):
    return jax.shard_map(
        per_device,
        mesh=mesh,
        in_specs=(
            P(("parts", "img"), None),
            P(("parts", "img")),
            P("parts", None),
            P(("parts", "img"), None),
            P("parts", None),
            P("parts"),
            P("parts"),
            P(),
            P("parts", None),
        ),
        out_specs=(P(("parts", "img"), None), P(("parts", "img"))),
        check_vma=False,
    )
```

profile of v0, /device:TPU:0, one launch (start us, length us, event | category | flops | bytes accessed | tf_op | source)
XLA Modules:
  0.0 340.5 jit_solution(2389398079491741984)
XLA Ops:
  8.0 4.6 %reduce-window.6 = s32[16,32,128]{2,1,0:T(8,128)S(1)} reduce-window(s32[16,32,128]{2,1,0:T(8,128)S(1)} %fusion.140, s32[]{:T(128)} %constant.18.clone.1), window={size=1x1x128 pad=0_0x0_0x127_0}, to_apply=%region_0.0 | reduce-window | flops 8323072 | bytes 524292 | tf_op jit(solution)/shard_map/reduce-window
  15.2 15.5 %scatter_custom_fusion = s32[384]{0:T(512)S(1)} fusion(s32[4096]{0:T(1024)S(1)} %bitcast.279, s32[4096]{0:T(1024)S(1)} %iota.31, s32[]{:T(128)} %constant.16.clone.1), kind=kCustom, calls=%fused_computation.224 | custom fusion | bytes 1540 | tf_op jit(solution)/shard_map/scatter | solution.py:113
  31.4 2.5 gather_fusion
  34.5 2.0 gather_fusion.1
  36.6 2.5 gather_fusion.2
  40.8 5.2 %reshape.246 = f32[64,64,2,128]{3,2,1,0:T(2,128)} reshape(bf16[64,16384]{1,0:T(8,128)(2,1)S(1)} %copy-done.5) | data formatting | bytes 6291456 | tf_op jit(solution)/shard_map/reshape | solution.py:53
  48.3 3.5 %mul.700.clone = f32[64,64,2,128]{3,2,1,0:T(2,128)} broadcast(f32[64,64,128]{2,1,0:T(8,128)S(1)} %bitcast.267), dimensions={0,1,3} | broadcast | bytes 6291456 | tf_op jit(solution)/shard_map/mul | solution.py:53
  51.7 6.5 %mul.795 = f32[64,16384]{1,0:T(8,128)} reshape(f32[64,64,2,128]{3,2,1,0:T(2,128)} %mul.700.clone) | data formatting | bytes 8388608 | tf_op jit(solution)/shard_map/mul | solution.py:53
  58.2 3.9 %fusion.12 = bf16[16384,64]{0,1:T(8,128)(2,1)} fusion(f32[64,16384]{1,0:T(8,128)} %mul.795, bf16[64,16384]{1,0:T(8,128)(2,1)S(1)} %copy-done.5), kind=kLoop, calls=%fused_computation.24 | loop fusion | flops 3145728 | bytes 8388608 | tf_op jit(solution)/shard_map/dot_general | solution.py:84
  62.1 3.3 dot_general.87
  66.2 1.1 fusion.134
  68.0 2.3 copy_bitcast_fusion
  71.2 3.8 %fusion.10 = bf16[64,64,2,128]{3,0,2,1:T(8,128)(2,1)} fusion(f32[64,64,2,128]{3,2,1,0:T(2,128)S(1)} %copy-done.3, f32[64,64,128]{2,0,1:T(8,128)S(1)} %copy_bitcast_fusion), kind=kLoop, calls=%fused_computation.19 | loop fusion | flops 2097152 | bytes 8388608 | tf_op jit(solution)/shard_map/convert_element_type | solution.py:54
  75.0 13.6 %all-gather.2.cloned.1.call-done = bf16[6144,256]{1,0:T(8,128)(2,1)} async-done(((bf16[384,256]{1,0:T(8,128)(2,1)}), bf16[6144,256]{1,0:T(8,128)(2,1)}) %all-gather.2.cloned.1.call-update) | async-done | bytes 3145744 | tf_op jit(solution)/shard_map/all_gather | solution.py:125
  88.6 19.5 %gather_fusion.3 = bf16[4096,256]{1,0:T(8,128)(2,1)} fusion(bf16[6144,256]{1,0:T(8,128)(2,1)} %all-gather.2.cloned.1.call-done, s32[4096]{0:T(1024)} %broadcast_clamp_fusion), kind=kCustom, calls=%fused_computation.3 | custom fusion | bytes 4210688 | tf_op jit(solution)/shard_map/gather | solution.py:126
  108.1 5.3 %reshape.250 = f32[64,64,2,128]{3,2,1,0:T(2,128)} reshape(bf16[4096,256]{1,0:T(8,128)(2,1)} %gather_fusion.3) | data formatting | bytes 6291456 | tf_op jit(solution)/shard_map/convert_element_type | solution.py:47
  113.4 7.9 %fusion.177 = (f32[64,64,1,128]{3,2,1,0:T(1,128)S(1)}, f32[64,64,1,128]{3,2,1,0:T(1,128)S(1)}) fusion(f32[64,64,2,128]{3,2,1,0:T(2,128)} %reshape.250), kind=kLoop, calls=%fused_computation.241 | loop fusion | bytes 8388608 | tf_op jit(solution)/shard_map/slice | solution.py:62
  121.4 8.2 %subtract_convert_fusion = (bf16[64,64,1,128]{3,0,2,1:T(8,128)(2,1)S(1)}, bf16[64,64,1,128]{3,0,2,1:T(8,128)(2,1)S(1)}, f32[64,64,1,128]{3,0,2,1:T(8,128)S(1)}, ...) fusion(f32[64,128]{1,0:T(8,128)S(1)} %copy-done.11, ...), kind=kLoop, calls=%fused_computation.84 | loop fusion | flops 35127296 | bytes 23592960 | tf_op jit(solution)/shard_map/convert.1
  129.5 1.2 copy.87
  130.8 2.5 fusion.13
  133.6 2.7 subtract_convert_fusion.8
  136.3 1.3 bitcast_dynamic-update-slice_fusion.8
  137.6 1.3 bitcast_dynamic-update-slice_fusion.7
  138.9 1.3 bitcast_dynamic-update-slice_fusion.6
  140.2 1.3 bitcast_dynamic-update-slice_fusion.5
  141.5 1.3 bitcast_dynamic-update-slice_fusion.4
  142.8 1.3 bitcast_dynamic-update-slice_fusion.3
  144.1 1.3 bitcast_dynamic-update-slice_fusion.2
  145.4 1.3 bitcast_dynamic-update-slice_fusion.1
  146.7 1.3 bitcast_dynamic-update-slice_fusion
  148.0 1.3 reduce_max.120
  149.3 1.4 reduce_max.118
  150.7 1.3 reduce_max.116
  151.9 1.4 reduce_max.114
  153.3 1.3 reduce_max.112
  154.6 1.4 reduce_max.110
  155.9 1.3 reduce_max.108
  157.3 1.3 reduce_max.106
  158.6 1.4 reduce_max.105
  160.8 3.8 %fusion.151 = f32[64,64,2,128]{3,0,2,1:T(8,128)} fusion(bf16[64,2,128,64]{2,1,0,3:T(2,128)(2,1)S(1)} %dot_general.87, bf16[64,9,64]{0,2,1:T(8,128)(2,1)S(1)} %divide_convert_fusion), kind=kOutput, calls=%fused_computation.158 | convolution fusion | flops 134217728 | bytes 6307840 | tf_op jit(solution)/shard_map/dot_general | solution.py:84
  164.6 1.7 fusion.153
  166.3 1.7 fusion.143
  168.0 1.7 fusion.145
  169.7 1.7 fusion.147
  171.4 1.7 fusion.149
  173.1 1.7 fusion.155
  174.9 1.7 fusion.157
  176.6 1.7 fusion.159
  178.3 3.1 multiply_add_fusion.4
  181.5 2.6 multiply_add_fusion.5
  184.0 2.6 multiply_add_fusion
  186.7 2.6 multiply_add_fusion.1
  189.2 2.6 multiply_add_fusion.2
  191.8 2.6 multiply_add_fusion.3
  194.4 2.6 multiply_add_fusion.6
  197.0 2.6 multiply_add_fusion.7
  199.6 2.6 multiply_add_fusion.8
  202.2 12.3 %fusion.9 = f32[64,64,2,128]{3,0,2,1:T(8,128)S(1)} fusion(f32[64,64,1,128]{3,0,2,1:T(8,128)} %get-tuple-element.19, f32[64,64,1,128]{3,0,2,1:T(8,128)} %get-tuple-element.18, f32[64,64,1,128]{3,0,2,1:T(8,128)} %get-tuple-element.17, f32[64,64,1,128]{3,0,2,1:T(8,128)} %get-tuple-element.16, f32[64,64,1,128]{3,0,2,1:T(8,128)} %get-tuple-element.15, ...), kind=kLoop, calls=%fused_computation.17 | loop fusion | flops 17825792 | bytes 41943040 | tf_op jit(solution)/shard_map/add | solution.py:96
  214.5 5.3 %copy.98 = f32[64,64,2,128]{3,2,1,0:T(2,128)} copy(f32[64,64,2,128]{3,0,2,1:T(8,128)S(1)} %fusion.9) | data formatting | bytes 8388608 | tf_op jit(solution)/shard_map/add | solution.py:96
  219.8 22.2 %scatter_custom_fusion.1 = f32[6144,256]{1,0:T(8,128)} fusion(s32[4096]{0:T(1024)S(1)} %bitcast.276, f32[512,8,2,128]{3,2,1,0:T(2,128)} %bitcast.266, f32[]{:T(128)} %constant.8.clone.1), kind=kCustom, calls=%fused_computation.7 | custom fusion | bytes 10485764 | tf_op jit(solution)/shard_map/scatter | solution.py:129
  243.2 83.0 %reduce-scatter.2.cloned.1.call-done = f32[384,256]{1,0:T(8,128)} async-done(((f32[6144,256]{1,0:T(8,128)}), f32[384,256]{1,0:T(8,128)}) %reduce-scatter.2.cloned.1.call-update) | async-done | bytes 393232 | tf_op jit(solution)/shard_map/reduce_scatter | solution.py:130
  326.2 1.2 copy.99
  327.3 1.6 multiply_reduce_fusion
  329.3 3.2 scatter_fusion
  (106 shorter events, 14.5 us)
Async XLA Ops:
  7.2 32.1 %copy-start = (bf16[8,128,128]{2,1,0:T(8,128)(2,1)S(1)}, bf16[8,128,128]{2,1,0:T(8,128)(2,1)}, u32[]{:S(2)}) copy-start(bf16[8,128,128]{2,1,0:T(8,128)(2,1)} %param.16) | copy-start | bytes 786436
  7.2 81.4 %all-gather.2.cloned.1.call-start = ((), (), s32[]{:S(2)}) async-start(), calls=%async_computation.1 | async-start | bytes 3342336 | tf_op jit(solution)/shard_map/all_gather | solution.py:125
  7.2 27.3 %copy-start.4 = (bf16[1024,256]{1,0:T(8,128)(2,1)S(1)}, bf16[1024,256]{1,0:T(8,128)(2,1)}, u32[]{:S(2)}) copy-start(bf16[1024,256]{1,0:T(8,128)(2,1)} %param.12) | copy-start | bytes 1572868
  34.0 0.5 copy-start.23
  39.2 1.6 copy-start.5
  39.2 1.3 copy-start.25
  40.6 5.4 %copy-start.8 = (f32[8,8192]{1,0:T(8,128)S(1)}, f32[8,8192]{1,0:T(8,128)}, u32[]{:S(2)}) copy-start(f32[8,8192]{1,0:T(8,128)} %param.17) | copy-start | bytes 786436
  40.6 5.4 %copy-start.32 = (s32[64]{0:T(128)S(1)}, s32[64]{0:T(128)}, u32[]{:S(2)}) copy-start(s32[64]{0:T(128)} %param.10) | copy-start | bytes 772
  40.6 285.6 %reduce-scatter.2.cloned.1.call-start = ((), (), s32[]{:S(2)}) async-start(), calls=%async_computation.2 | async-start | bytes 6684672 | tf_op jit(solution)/shard_map/reduce_scatter | solution.py:130
  47.0 1.3 copy-start.1
  62.1 3.3 copy-start.31
  68.0 53.3 %copy-start.9 = (f32[64,128]{1,0:T(8,128)}, f32[64,128]{1,0:T(8,128)S(1)}, u32[]{:S(2)}) copy-start(f32[64,128]{1,0:T(8,128)S(1)} %get-tuple-element.106) | copy-start | bytes 98308
  68.0 3.2 copy-start.3
  113.3 8.0 %copy-start.11 = (f32[64,128]{1,0:T(8,128)S(1)}, f32[64,128]{1,0:T(8,128)}, u32[]{:S(2)}) copy-start(f32[64,128]{1,0:T(8,128)} %get-tuple-element.64) | copy-start | bytes 98308
  113.4 8.0 %copy-start.13 = (f32[64,128]{1,0:T(8,128)S(1)}, f32[64,128]{1,0:T(8,128)}, u32[]{:S(2)}) copy-start(f32[64,128]{1,0:T(8,128)} %get-tuple-element.107) | copy-start | bytes 98308
  113.4 8.0 %copy-start.15 = (f32[64,128]{1,0:T(8,128)S(1)}, f32[64,128]{1,0:T(8,128)}, u32[]{:S(2)}) copy-start(f32[64,128]{1,0:T(8,128)} %get-tuple-element.69) | copy-start | bytes 98308
  113.4 8.0 %copy-start.17 = (f32[64,128]{1,0:T(8,128)S(1)}, f32[64,128]{1,0:T(8,128)}, u32[]{:S(2)}) copy-start(f32[64,128]{1,0:T(8,128)} %get-tuple-element.102) | copy-start | bytes 98308
  113.4 8.0 %copy-start.19 = (f32[64,128]{1,0:T(8,128)S(1)}, f32[64,128]{1,0:T(8,128)}, u32[]{:S(2)}) copy-start(f32[64,128]{1,0:T(8,128)} %get-tuple-element.68) | copy-start | bytes 98308
  113.4 8.0 %copy-start.21 = (f32[64,128]{1,0:T(8,128)S(1)}, f32[64,128]{1,0:T(8,128)}, u32[]{:S(2)}) copy-start(f32[64,128]{1,0:T(8,128)} %get-tuple-element.103) | copy-start | bytes 98308
  130.8 2.6 copy-start.33
  133.6 2.7 copy-start.7
  160.6 4.0 %copy-start.27 = (f32[64]{0:T(128)}, f32[64]{0:T(128)S(1)}, u32[]{:S(2)}) copy-start(f32[64]{0:T(128)S(1)} %maximum_maximum_fusion) | copy-start | bytes 772
  160.7 3.9 %copy-start.29 = (f32[64]{0:T(128)}, f32[64]{0:T(128)S(1)}, u32[]{:S(2)}) copy-start(f32[64]{0:T(128)S(1)} %fusion.141) | copy-start | bytes 772
  176.6 1.7 copy-start.20
  176.6 1.7 copy-start.22
  178.3 3.1 copy-start.16
  178.3 3.1 copy-start.18
  181.4 2.6 copy-start.12
  181.4 2.6 copy-start.14
  184.0 2.6 copy-start.10
  199.6 2.6 copy-start.6
  242.0 0.7 copy-start.28
  242.0 0.7 copy-start.30
  242.0 85.4 %copy-start.26 = (f32[384,8]{0,1:T(8,128)S(1)}, f32[384,8]{0,1:T(8,128)}, u32[]{:S(2)}) copy-start(f32[384,8]{0,1:T(8,128)} %copy-done.25) | copy-start | bytes 36868
  242.6 86.6 %copy-start.24 = (s32[384]{0:T(512)S(1)}, s32[384]{0:T(512)}, u32[]{:S(2)}) copy-start(s32[384]{0:T(512)} %copy-done.23) | copy-start | bytes 4612
  332.5 1.0 copy-start.2
Sparse Core Ops, SparseCore 0:
  40.7 47.8 all-gather.1
  242.1 84.0 reduce-scatter.1
where the time goes:
time: 346 us; the launch traced here: 341 us
  local copies, waits for them, and re-layouts  112 us (32%)
  waiting for transfers between devices  96.7 us (28%)
  other arithmetic  81.3 us (23%)
  matrix products  35.1 us (10%)
  between operations  14.9 us (4%)
    reduce_scatter x1, waiting for transfers between devices, per_device(): lax.psum_scatter(outbound, 'img', scatter_dimension=0, tiled=True)  83 us
    add x9, other arithmetic, score_images(): partial_sum[:, :, 0] * cosine[number]  23.8 us
    scatter x1, local copies, waits for them, and re-layouts, per_device(): jnp.zeros((devices * capacity, 2 * BW), jnp.float32).at[target]  22.2 us
    gather x1, local copies, waits for them, and re-layouts, per_device(): slices = gathered[target].reshape(R, KB, 2, BW)  19.5 us
    dot_general x9, matrix products, score_images(): lax.dot_general(weights[:, number, :], weighted, (((0,), (0,)), ((), ()))...  17.4 us
    another operation x5, other arithmetic  15.8 us
    scatter x1, local copies, waits for them, and re-layouts, per_device(): slot_source = jnp.full((capacity,), block_count, jnp.int32).at[jnp.where(...  15.5 us
    all_gather x1, waiting for transfers between devices, per_device(): gathered = lax.all_gather(own_slices, 'img', axis=0, tiled=True)  13.6 us
  transfers between devices with their start and end apart: 2, of which 2 were waited for; matrix products, arithmetic and copies ran while one was open for 10% of the time, Pallas kernels for 0%

commit v1 on v0

v1 whole, which is shorter than its diff:
```python
import functools
import math

import jax
import jax.numpy as jnp
from jax import lax
from jax.experimental import pallas as pl
from jax.experimental.pallas import tpu as pltpu
from jax.sharding import PartitionSpec as P

BW = 128
KB = 64
R = 64
HALF = BW // 2
BLOCKS = R * KB
GROUP = 8

F32 = jnp.float32
BF16 = jnp.bfloat16
NT = (((1,), (1,)), ((), ()))
NN = (((1,), (0,)), ((), ()))


def dot(a, b, dims=NN):
    return lax.dot_general(a, b, dims, preferred_element_type=F32)


def iota(shape, axis):
    return lax.broadcasted_iota(jnp.int32, shape, axis)


def swap_halves(x):
    return pltpu.roll(x, HALF, 1)


def split_halves(real, imag):
    first = iota(real.shape, 1) < HALF
    return (
        jnp.where(first, real, swap_halves(imag)),
        jnp.where(first, swap_halves(real), imag),
    )


def slice_kernel(
    devices, ny, nz, cap, meta, owner, local, table, volume, interp, target, slots, keep, send
):
    me = meta[0]
    z, y, core = meta[1], meta[2], meta[3]
    own = owner[...]
    rows = own.shape[0]
    upper = jnp.where(iota((BW, BW), 0) <= iota((BW, BW), 1), 1.0, 0.0).astype(BF16)
    ones = jnp.ones((BW, BW), BF16)
    lower = jnp.where(iota((rows, rows), 1) < iota((rows, rows), 0), 1.0, 0.0).astype(BF16)

    def rank(d, pos):
        member = jnp.where(own == d, 1.0, 0.0)
        bits = member.astype(BF16)
        inclusive = dot(bits, upper)
        before = dot(lower, dot(bits, ones).astype(BF16))
        return pos + member * (inclusive - 1.0 + before)

    pos = jnp.zeros(own.shape, F32)
    if devices <= 16:
        for d in range(devices):
            pos = rank(d, pos)
    else:
        pos = lax.fori_loop(0, devices, rank, pos)
    pos = pos.astype(jnp.int32)
    shift_y = 1
    shift_z = 1 + (ny.bit_length() - 1)
    rel_core = (own & 1) ^ core
    rel_y = (lax.shift_right_logical(own, shift_y) - y) & (ny - 1)
    rel_z = (lax.shift_right_logical(own, shift_z) - z) & (nz - 1)
    target[...] = ((rel_z * ny + rel_y) * 2 + rel_core) * cap + pos

    mine = jnp.where(own == me, pos, -1)
    slot = iota((cap, BW), 0)
    kind = iota((8, BW), 0)
    loc, tab = local[...], table[...]
    high = lax.shift_right_logical(loc, 8).astype(F32)
    low = (loc & 255).astype(F32)
    tab = tab.astype(F32)
    found = jnp.zeros((cap, 8), F32)
    for g in range(rows):
        row = slice(g, g + 1)
        hot = jnp.where(slot == mine[row], 1.0, 0.0).astype(BF16)
        values = jnp.where(
            kind == 0,
            high[row],
            jnp.where(kind == 1, low[row], jnp.where(kind == 2, tab[row], 1.0)),
        ).astype(BF16)
        found = found + dot(hot, values, NT)
    valid = found[:, 3:4] > 0.5
    place = jnp.where(valid, found[:, 0:1] * 256.0 + found[:, 1:2], -1.0)
    which = found[:, 2:3]
    column = iota((cap, 8), 1)
    slots[...] = jnp.where(column == 0, place, jnp.where(column == 1, which, 0.0))

    depth = volume.shape[0]
    pick = jnp.where(iota((cap, depth), 1) == place.astype(jnp.int32), 1.0, 0.0).astype(BF16)
    voxels = dot(pick, volume[...])
    voxels = jnp.concatenate([voxels[:, :BW], voxels[:, BW:]], axis=0)
    which = jnp.concatenate([which, which], axis=0)
    out = jnp.zeros((2 * cap, BW), F32)
    for t in range(interp.shape[0]):
        out = out + dot(jnp.where(which == float(t), voxels, 0.0).astype(BF16), interp[t], NT)
    left, right = split_halves(out[:cap], out[cap:])
    keep[...] = jnp.where(core == 0, left, right).astype(BF16)
    send[...] = jnp.where(core == 0, right, left).astype(BF16)


def weigh_kernel(meta, images, group, ctf, keep, send, squares):
    core = meta[3]
    count = images.shape[0]
    groups = ctf.shape[0]
    number = jnp.broadcast_to(group[...], (count, BW))

    def body(b, carry):
        lanes = pl.ds(pl.multiple_of(b * BW, BW), BW)
        scale = ctf[:, lanes]
        factor = jnp.zeros((count, BW), F32)
        for g in range(groups):
            factor = jnp.where(number == g, scale[g : g + 1], factor)
        real = images[:, pl.ds(pl.multiple_of(b * 2 * BW, BW), BW)].astype(F32) * factor
        imag = images[:, pl.ds(pl.multiple_of(b * 2 * BW + BW, BW), BW)].astype(F32) * factor
        left, right = split_halves(real, imag)
        keep[:, lanes] = jnp.where(core == 0, left, right).astype(BF16)
        send[:, lanes] = jnp.where(core == 0, right, left).astype(BF16)
        square = scale * scale
        left, right = split_halves(square, square)
        square = jnp.where(core == 0, left, right)
        high = square.astype(BF16)
        rest = square - high.astype(F32)
        squares[:, lanes] = jnp.concatenate([high.astype(F32), rest], axis=0).astype(BF16)
        return carry

    lax.fori_loop(0, KB, body, 0, unroll=2)


def score_kernel(
    order, rows, target, group, cosine, sine, keep, other, squares, *rest
):
    pieces = rest[: len(order)]
    scores, gathered, block, left, power, norms = rest[len(order) :]
    shifts = cosine.shape[1]
    for number, piece in zip(order, pieces):
        gathered[pl.ds(number * rows, rows), :] = piece[...].astype(F32)
    scores[...] = jnp.zeros(scores.shape, F32)
    norms[...] = jnp.zeros(norms.shape, F32)

    def body(group_index, carry):
        for part in range(GROUP):
            b = group_index * GROUP + part
            lanes = slice(part * BW, (part + 1) * BW)
            for r in range(R):
                block[part, r : r + 1, :] = gathered[pl.ds(target[r * KB + b], 1), :]
            value = block[part]
            swapped = swap_halves(value)
            for s in range(shifts):
                turned = value * cosine[b, s : s + 1, :] + swapped * sine[b, s : s + 1, :]
                left[s * R : (s + 1) * R, lanes] = turned.astype(BF16)
            square = value * value
            high = square.astype(BF16)
            power[0:R, lanes] = high
            power[R : 2 * R, lanes] = (square - high.astype(F32)).astype(BF16)
        lanes = pl.ds(pl.multiple_of(group_index * GROUP * BW, BW), GROUP * BW)
        right = jnp.concatenate([keep[:, lanes], other[:, lanes]], axis=0)
        scores[...] += dot(left[...], right, NT)
        norms[...] += dot(power[...], squares[:, lanes], NT)
        return carry

    lax.fori_loop(0, KB // GROUP, body, 0)
    half = squares.shape[0] // 2
    total = norms[...]
    total = total[:R, :half] + total[:R, half:] + total[R:, :half] + total[R:, half:]
    norm = jnp.zeros((R, scores.shape[1]), F32)
    for g in range(half):
        norm = jnp.where(group[...] == g, total[:, g : g + 1], norm)
    for s in range(shifts):
        scores[s * R : (s + 1) * R, :] -= 0.5 * norm


def back_kernel(ny, nz, rows, first, target, mine, theirs, cosine, sine, keep, other, *rest):
    evidence = rest[0]
    by_y = rest[1 : 1 + ny]
    by_z = rest[1 + ny : 1 + ny + nz]
    placed, block = rest[1 + ny + nz :]
    shifts = cosine.shape[1]
    scale = 1.0 / math.sqrt(KB * BW)
    placed[...] = jnp.zeros(placed.shape, F32)
    scores = (mine[...] + swap_halves(theirs[...])) * scale
    top = jnp.max(scores, axis=0, keepdims=True)
    exponent = jnp.exp(scores - top)
    total = jnp.sum(exponent, axis=0, keepdims=True)
    evidence[...] = top + jnp.log(total)
    weights = (exponent / total).astype(BF16)

    def body(pair, carry):
        lanes = pl.ds(pl.multiple_of(pair * 2 * BW, BW), 2 * BW)
        right = jnp.concatenate([keep[:, lanes], other[:, lanes]], axis=0)
        sums = dot(weights, right)
        for part in range(2):
            b = pair * 2 + part
            straight = jnp.zeros((R, BW), F32)
            crossed = jnp.zeros((R, BW), F32)
            for s in range(shifts):
                term = sums[s * R : (s + 1) * R, part * BW : (part + 1) * BW]
                straight = straight + term * cosine[b, s : s + 1, :]
                crossed = crossed + term * sine[b, s : s + 1, :]
            block[part] = straight + swap_halves(crossed)
            for r in range(R):
                placed[pl.ds(target[r * KB + b], 1), :] = block[part, r : r + 1, :]
        return carry

    lax.fori_loop(0, KB // 2, body, 0)
    for kz in range(nz):
        for ky in range(ny):
            start = (kz * ny + ky) * rows
            by_y[ky][kz * first : (kz + 1) * first, :] = placed[start : start + first, :].astype(BF16)
            rest_rows = rows - first
            by_z[kz][ky * rest_rows : (ky + 1) * rest_rows, :] = placed[
                start + first : start + rows, :
            ].astype(BF16)


def adjoint_kernel(meta, place, slots, volume, interp, keep, other, new_map):
    core = meta[3]
    cap = keep.shape[0]
    mine, theirs = keep[...], other[...]
    left = jnp.where(core == 0, mine, theirs)
    right = jnp.where(core == 0, theirs, mine)
    real, imag = split_halves(left, right)
    value = jnp.concatenate([real, imag], axis=0)
    which = slots[:, 1:2]
    which = jnp.concatenate([which, which], axis=0)
    high = value.astype(BF16).astype(F32)
    rest = value - high
    out = jnp.zeros((2 * cap, BW), F32)
    for t in range(interp.shape[0]):
        chosen = which == float(t)
        out = out + dot(jnp.where(chosen, high, 0.0).astype(BF16), interp[t])
        out = out + dot(jnp.where(chosen, rest, 0.0).astype(BF16), interp[t])
    out = jnp.concatenate([out[:cap], out[cap:]], axis=1)
    depth = volume.shape[0]
    spread = jnp.where(
        iota((depth, cap), 0) == place[0:1, :].astype(jnp.int32), 1.0, 0.0
    ).astype(BF16)
    high = out.astype(BF16)
    rest = out - high.astype(F32)
    middle = rest.astype(BF16)
    low = (rest - middle.astype(F32)).astype(BF16)
    new_map[...] = volume[...].astype(F32) + (
        dot(spread, high) + (dot(spread, middle) + dot(spread, low))
    )


SMEM = pl.BlockSpec(memory_space=pltpu.SMEM)
VMEM = pl.BlockSpec(memory_space=pltpu.VMEM)


def call(kernel, in_specs, out_shapes, scratch, flops, touched, name):
    return pl.pallas_call(
        kernel,
        in_specs=in_specs,
        out_specs=[VMEM] * len(out_shapes),
        out_shape=out_shapes,
        scratch_shapes=scratch,
        compiler_params=pltpu.CompilerParams(vmem_limit_bytes=40 * 1024 * 1024),
        cost_estimate=pl.CostEstimate(flops=flops, bytes_accessed=touched, transcendentals=0),
        name=name,
    )


def per_device(images, groups, shifts, volume, owner, local, table_id, interp, ctf):
    devices = lax.axis_size("img")
    chips = devices // 2
    ny = 1 << ((chips.bit_length() - 1) // 2)
    nz = chips // ny
    me = lax.axis_index("img")
    core = me % 2
    y = (me // 2) % ny
    z = me // (2 * ny)
    meta = jnp.stack([me, z, y, core]).astype(jnp.int32)
    cap = max(2, 3 * BLOCKS // (2 * devices))
    rows = 2 * cap
    count = images.shape[0]
    shift_count = shifts.shape[0]
    struct = jax.ShapeDtypeStruct

    def device(dz, dy, dc):
        return (dz * ny + dy) * 2 + dc

    everyone = [(dz, dy, dc) for dz in range(nz) for dy in range(ny) for dc in range(2)]
    core_pairs = [(device(*d), device(d[0], d[1], 1 - d[2])) for d in everyone]

    def along_z(k):
        return [(device(a, b, c), device((a + k) % nz, b, c)) for a, b, c in everyone]

    def along_y(k):
        return [(device(a, b, c), device(a, (b + k) % ny, c)) for a, b, c in everyone]

    def to(array, pairs):
        return lax.ppermute(array, "img", pairs)

    wide = (BLOCKS // BW, BW)
    target, slots, slice_keep, slice_send = call(
        functools.partial(slice_kernel, devices, ny, nz, cap),
        [SMEM] + [VMEM] * 5,
        [
            struct(wide, jnp.int32),
            struct((cap, 8), F32),
            struct((cap, BW), BF16),
            struct((cap, BW), BF16),
        ],
        [],
        10**9,
        10**6,
        "own_slices",
    )(meta, owner.reshape(wide), local.reshape(wide), table_id.reshape(wide), volume, interp)
    target = target.reshape(BLOCKS)
    own_piece = jnp.concatenate([slice_keep, to(slice_send, core_pairs)], axis=0)

    pieces = {(0, 0): own_piece}
    near = sorted(range(1, nz), key=lambda k: min(k, nz - k))
    for ky in range(1, ny):
        pieces[0, ky] = to(own_piece, along_y(-ky))
    for kz in near:
        pieces[kz, 0] = to(own_piece, along_z(-kz))
    for kz in near:
        for ky in range(1, ny):
            pieces[kz, ky] = to(pieces[kz, 0], along_y(-ky))

    weight_keep, weight_send, squares = call(
        weigh_kernel,
        [SMEM] + [VMEM] * 3,
        [
            struct((count, KB * BW), BF16),
            struct((count, KB * BW), BF16),
            struct((2 * ctf.shape[0], KB * BW), BF16),
        ],
        [],
        10**9,
        4 * 10**6,
        "weigh",
    )(meta, images, groups.reshape(count, 1), ctf)
    weight_other = to(weight_send, core_pairs)
    group_row = groups.astype(F32).reshape(1, count)
    group_row = jnp.concatenate([group_row, to(group_row, core_pairs)], axis=1).astype(jnp.int32)
    place = slots.T

    lane = jnp.arange(BW)
    freq_x = (lane % HALF + core * HALF - BW // 2).astype(F32)
    freq_y = jnp.arange(KB).astype(F32)
    shift_x = shifts[:, 0].astype(F32)
    shift_y = shifts[:, 1].astype(F32)
    angles = (
        2.0
        * math.pi
        / BW
        * (
            shift_x[None, :, None] * freq_x[None, None, :]
            + shift_y[None, :, None] * freq_y[:, None, None]
        )
    )
    cosine = jnp.cos(angles)
    sine = jnp.sin(angles) * jnp.where(lane < HALF, -1.0, 1.0)

    order = tuple(kz * ny + ky for kz, ky in pieces)
    (partial,) = call(
        functools.partial(score_kernel, order, rows),
        [SMEM] + [VMEM] * (6 + len(order)),
        [struct((shift_count * R, 2 * count), F32)],
        [
            pltpu.VMEM((chips * rows, BW), F32),
            pltpu.VMEM((GROUP, R, BW), F32),
            pltpu.VMEM((shift_count * R, GROUP * BW), BF16),
            pltpu.VMEM((2 * R, GROUP * BW), BF16),
            pltpu.VMEM((2 * R, 2 * ctf.shape[0]), F32),
        ],
        4 * 10**9,
        10**7,
        "score",
    )(target, group_row, cosine, sine, weight_keep, weight_other, squares, *pieces.values())

    theirs = to(partial, core_pairs)
    first = rows * 2 // 3
    later = rows - first
    outs = call(
        functools.partial(back_kernel, ny, nz, rows, first),
        [SMEM] + [VMEM] * 6,
        [struct((1, 2 * count), F32)]
        + [struct((nz * first, BW), BF16)] * ny
        + [struct((ny * later, BW), BF16)] * nz,
        [pltpu.VMEM((chips * rows, BW), F32), pltpu.VMEM((2, R, BW), F32)],
        4 * 10**9,
        10**7,
        "back",
    )(target, partial, theirs, cosine, sine, weight_keep, weight_other)
    evidence = outs[0][0, :count]
    by_y, by_z = outs[1 : 1 + ny], outs[1 + ny :]

    from_y = [to(by_y[ky], along_y(ky)) for ky in range(1, ny)]
    from_z = [to(by_z[kz], along_z(kz)) for kz in near]
    summed_y = by_y[0].astype(F32)
    for part in from_y:
        summed_y = summed_y + part.astype(F32)
    packed_y = summed_y.astype(BF16)
    final_first = summed_y[:first]
    for kz in near:
        part = to(packed_y[kz * first : (kz + 1) * first], along_z(kz))
        final_first = final_first + part.astype(F32)
    summed_z = by_z[0].astype(F32)
    for part in from_z:
        summed_z = summed_z + part.astype(F32)
    packed_z = summed_z.astype(BF16)
    final_later = summed_z[:later]
    for ky in range(1, ny):
        part = to(packed_z[ky * later : (ky + 1) * later], along_y(ky))
        final_later = final_later + part.astype(F32)
    final = jnp.concatenate([final_first, final_later], axis=0)
    sum_keep = final[:cap]
    sum_other = to(final[cap:], core_pairs)

    (new_map,) = call(
        adjoint_kernel,
        [SMEM] + [VMEM] * 6,
        [struct(volume.shape, F32)],
        [],
        10**9,
        2 * 10**6,
        "adjoint",
    )(meta, place, slots, volume, interp, sum_keep, sum_other)
    return (new_map, evidence)


def solution(mesh):
    return jax.shard_map(
        per_device,
        mesh=mesh,
        in_specs=(
            P(("parts", "img"), None),
            P(("parts", "img")),
            P("parts", None),
            P(("parts", "img"), None),
            P("parts", None),
            P("parts"),
            P("parts"),
            P(),
            P("parts", None),
        ),
        out_specs=(P(("parts", "img"), None), P(("parts", "img"))),
        check_vma=False,
    )
```

time: 346 us -> 116 us (0.34); the launches traced: 341 us -> 115 us
  local copies, waits for them, and re-layouts: 112 us -> 8.59 us
  other arithmetic: 81.3 us -> 3.6 us
  waiting for transfers between devices: 96.7 us -> 37.4 us
  Pallas kernels: 0 us -> 41.8 us
  matrix products: 35.1 us -> 0 us
  starting transfers between devices: 0.25 us -> 22.9 us
  between operations: 14.9 us -> 0.87 us
    reduce_scatter x1 -> x0, waiting for transfers between devices: 83 us -> none  [per_device(): lax.psum_scatter(outbound, 'img', scatter_dimension=0, tiled=True)]
    pallas_call x0 -> x5, Pallas kernels: none -> 41.8 us  [the longest x1 15.1 us: per_device(): call(functools.partial(back_kernel, ny, nz, rows, first), [SMEM] + [VMEM]...]
    scatter x2 -> x0, local copies, waits for them, and re-layouts: 37.7 us -> none  [the longest x1 22.2 us: per_device(): jnp.zeros((devices * capacity, 2 * BW), jnp.float32).at[target]]
    ppermute x0 -> x20, waiting for transfers between devices: none -> 37.4 us  [to(): return lax.ppermute(array, 'img', pairs)]
    add x11 -> x3, other arithmetic: 36.6 us -> 0.13 us  [the longest x1 0.06 us: per_device(): summed_z = summed_z + part.astype(F32)]
    dot_general x23 -> x0, matrix products: 35.1 us -> none  [the longest x9 17.4 us: score_images(): lax.dot_general(weights[:, number, :], weighted, (((0,), (0,)), ((), ()))...]
    gather x4 -> x0, local copies, waits for them, and re-layouts: 26.6 us -> none  [the longest x1 19.5 us: per_device(): slices = gathered[target].reshape(R, KB, 2, BW)]
    ppermute x0 -> x20, starting transfers between devices: none -> 22.9 us  [to(): return lax.ppermute(array, 'img', pairs)]
  transfers between devices with their start and end apart: 2 -> 20, of which waited for: 2 -> 11; matrix products, arithmetic and copies ran while one was open for 10% -> 4% of each run, Pallas kernels for 0% -> 5%
where the time goes in v1:
time: 116 us; the launch traced here: 115 us
  Pallas kernels  41.8 us (36%)
  waiting for transfers between devices  37.4 us (32%)
  starting transfers between devices  22.9 us (20%)
  local copies, waits for them, and re-layouts  8.59 us (7%)
  other arithmetic  3.6 us (3%)
    ppermute x20, waiting for transfers between devices, to(): return lax.ppermute(array, 'img', pairs)  37.4 us
    ppermute x20, starting transfers between devices, to(): return lax.ppermute(array, 'img', pairs)  22.9 us
    pallas_call x1, Pallas kernels, per_device(): call(functools.partial(back_kernel, ny, nz, rows, first), [SMEM] + [VMEM]...  15.1 us
    pallas_call x1, Pallas kernels, per_device(): call(functools.partial(score_kernel, order, rows), [SMEM] + [VMEM] * (6 +...  11 us
    unnamed x31, local copies, waits for them, and re-layouts  7.21 us
    pallas_call x1, Pallas kernels, per_device(): call(functools.partial(slice_kernel, devices, ny, nz, cap), [SMEM] + [VME...  6.1 us
    pallas_call x1, Pallas kernels, per_device(): call(adjoint_kernel, [SMEM] + [VMEM] * 6, [struct(volume.shape, F32)], []...  5.09 us
    pallas_call x1, Pallas kernels, per_device(): call(weigh_kernel, [SMEM] + [VMEM] * 3, [struct((count, KB * BW), BF16),...  4.48 us
  transfers between devices with their start and end apart: 20, of which 11 were waited for; matrix products, arithmetic and copies ran while one was open for 4% of the time, Pallas kernels for 5%

profile of v1, /device:TPU:0, one launch (start us, length us, event | category | flops | bytes accessed | tf_op | source)
XLA Modules:
  0.0 115.2 jit_solution(8169328906447930315)
XLA Ops:
  0.7 0.7 copy.12.group
  1.4 0.1 pad_add_fusion.meta
  1.5 1.6 %copy-done = bf16[64,16384]{1,0:T(8,128)(2,1)S(1)} copy-done((bf16[64,16384]{1,0:T(8,128)(2,1)S(1)}, bf16[64,16384]{1,0:T(8,128)(2,1)}, u32[]{:S(2)}) %copy-start) | copy-done | bytes 2097176
  3.1 0.9 copy-done.2
  4.1 4.5 %weigh.1 = (bf16[64,8192]{1,0:T(8,128)(2,1)S(1)}, bf16[64,8192]{1,0:T(8,128)(2,1)S(1)}, bf16[16,8192]{1,0:T(8,128)(2,1)S(1)}) custom-call(s32[4]{0:T(128)S(1)} %pad_add_fusion.meta, bf16[64,16384]{1,0:T(8,128)(2,1)S(1)} %copy-done, s32[64,1]{1,0:T(8,128)S(1)} %copy.12.group, f32[8,8192]{1,0:T(8,128)S(1)} %copy-done.2), custom_call_target="tpu_custom_call" | custom-call | flops 1000000000 | bytes 4000000 | tf_op jit(solution)/shard_map/weigh/pallas_call | solution.py:333
  8.6 0.0 copy-start.8
  8.6 1.0 copy-done.8
  9.5 0.7 copy-done.10
  10.2 0.5 collective-permute-start.1
  10.7 6.1 %own_slices.1 = (s32[32,128]{1,0:T(8,128)S(1)}, f32[384,8]{1,0:T(8,128)S(1)}, bf16[384,128]{1,0:T(8,128)(2,1)S(1)}, bf16[384,128]{1,0:T(8,128)(2,1)S(1)}) custom-call(s32[4]{0:T(128)S(1)} %pad_add_fusion.meta, s32[32,128]{1,0:T(8,128)S(1)} %bitcast.19, s32[32,128]{1,0:T(8,128)S(1)} %bitcast.20, s32[32,128]{1,0:T(8,128)S(1)} %bitcast.21, ...), custom_call_target="tpu_custom_call" | custom-call | flops 1000000000 | bytes 1000000 | tf_op jit(solution)/shard_map/own_slices/pallas_call | solution.py:306
  16.8 0.1 collective-permute-start.2
  16.9 0.5 collective-permute-start
  17.4 0.1 broadcast_multiply_fusion
  17.5 0.7 collective-permute-done.2
  18.2 4.8 %collective-permute-start.4 = (bf16[768,128]{1,0:T(8,128)(2,1)S(1)}, bf16[768,128]{1,0:T(8,128)(2,1)S(1)}, u32[]{:S(2)}, u32[]{:S(2)}) collective-permute-start(bf16[768,128]{1,0:T(8,128)(2,1)S(1)} %constant_dynamic-update-slice_fusion.rest_0_), channel_id=1, source_target_pairs={{0,12},{1,13},{2,14},{3,15},{4,0},{5,1},{6,2},{7,3},{8,4},{9,5},{1... | collective-permute-start | bytes 589832 | tf_op jit(solution)/shard_map/ppermute | solution.py:303
  23.0 0.0 collective-permute-start.5
  23.0 1.0 collective-permute-start.6
  24.0 0.1 broadcast_multiply_fusion.1
  24.1 0.0 collective-permute-done
  24.1 1.6 %collective-permute-start.3 = (bf16[768,128]{1,0:T(8,128)(2,1)S(1)}, bf16[768,128]{1,0:T(8,128)(2,1)S(1)}, u32[]{:S(2)}, u32[]{:S(2)}) collective-permute-start(bf16[768,128]{1,0:T(8,128)(2,1)S(1)} %constant_dynamic-update-slice_fusion.rest_0_), channel_id=1, source_target_pairs={{0,2},{1,3},{2,0},{3,1},{4,6},{5,7},{6,4},{7,5},{8,10},{9,11},{10,... | collective-permute-start | bytes 589832 | tf_op jit(solution)/shard_map/ppermute | solution.py:303
  25.7 2.6 %collective-permute-done.4.rest_2_ = bf16[768,128]{1,0:T(8,128)(2,1)S(1)} collective-permute-done((bf16[768,128]{1,0:T(8,128)(2,1)S(1)}, bf16[768,128]{1,0:T(8,128)(2,1)S(1)}, u32[]{:S(2)}, u32[]{:S(2)}) %collective-permute-start.4) | collective-permute-done | bytes 196640 | tf_op jit(solution)/shard_map/ppermute | solution.py:303
  28.3 1.5 %collective-permute-start.7 = (bf16[768,128]{1,0:T(8,128)(2,1)S(1)}, bf16[768,128]{1,0:T(8,128)(2,1)S(1)}, u32[]{:S(2)}, u32[]{:S(2)}) collective-permute-start(bf16[768,128]{1,0:T(8,128)(2,1)S(1)} %collective-permute-done.4.rest_2_), channel_id=1, source_target_pairs={{0,2},{1,3},{2,0},{3,1},{4,6},{5,7},{6,4},{7,5},{8,10},{9,11},{10,... | collective-permute-start | bytes 589832 | tf_op jit(solution)/shard_map/ppermute | solution.py:303
  29.8 3.7 %collective-permute-done.5.rest_3_ = bf16[768,128]{1,0:T(8,128)(2,1)S(1)} collective-permute-done((bf16[768,128]{1,0:T(8,128)(2,1)S(1)}, bf16[768,128]{1,0:T(8,128)(2,1)S(1)}, u32[]{:S(2)}, u32[]{:S(2)}) %collective-permute-start.5) | collective-permute-done | bytes 196640 | tf_op jit(solution)/shard_map/ppermute | solution.py:303
  33.5 1.5 %collective-permute-start.8 = (bf16[768,128]{1,0:T(8,128)(2,1)S(1)}, bf16[768,128]{1,0:T(8,128)(2,1)S(1)}, u32[]{:S(2)}, u32[]{:S(2)}) collective-permute-start(bf16[768,128]{1,0:T(8,128)(2,1)S(1)} %collective-permute-done.5.rest_3_), channel_id=1, source_target_pairs={{0,2},{1,3},{2,0},{3,1},{4,6},{5,7},{6,4},{7,5},{8,10},{9,11},{10,... | collective-permute-start | bytes 589832 | tf_op jit(solution)/shard_map/ppermute | solution.py:303
  35.0 5.2 %collective-permute-done.6.rest_4_ = bf16[768,128]{1,0:T(8,128)(2,1)S(1)} collective-permute-done((bf16[768,128]{1,0:T(8,128)(2,1)S(1)}, bf16[768,128]{1,0:T(8,128)(2,1)S(1)}, u32[]{:S(2)}, u32[]{:S(2)}) %collective-permute-start.6) | collective-permute-done | bytes 196640 | tf_op jit(solution)/shard_map/ppermute | solution.py:303
  40.2 1.5 %collective-permute-start.9 = (bf16[768,128]{1,0:T(8,128)(2,1)S(1)}, bf16[768,128]{1,0:T(8,128)(2,1)S(1)}, u32[]{:S(2)}, u32[]{:S(2)}) collective-permute-start(bf16[768,128]{1,0:T(8,128)(2,1)S(1)} %collective-permute-done.6.rest_4_), channel_id=1, source_target_pairs={{0,2},{1,3},{2,0},{3,1},{4,6},{5,7},{6,4},{7,5},{8,10},{9,11},{10,... | collective-permute-start | bytes 589832 | tf_op jit(solution)/shard_map/ppermute | solution.py:303
  41.7 1.9 %sine_multiply_fusion = (f32[64,9,128]{2,1,0:T(8,128)S(1)}, f32[64,9,128]{2,1,0:T(8,128)S(1)}) fusion(f32[128]{0:T(128)S(1)} %compare_select_fusion, f32[64,9]{1,0:T(8,128)S(1)} %broadcast_multiply_fusion, f32[9,128]{1,0:T(8,128)S(1)} %broadcast_multiply_fusion.1), kind=kLoop, calls=%fused_computation.1 | loop fusion | flops 221184 | bytes 597248 | tf_op jit(solution)/shard_map/mul | solution.py:366
  43.7 0.1 maximum_convert_fusion.group
  43.7 0.0 collective-permute-done.3.rest_1_
  43.7 0.0 collective-permute-done.7.rest_5_
  43.7 0.0 collective-permute-done.8.rest_6_
  43.8 2.8 %collective-permute-done.9.rest_7_ = bf16[768,128]{1,0:T(8,128)(2,1)S(1)} collective-permute-done((bf16[768,128]{1,0:T(8,128)(2,1)S(1)}, bf16[768,128]{1,0:T(8,128)(2,1)S(1)}, u32[]{:S(2)}, u32[]{:S(2)}) %collective-permute-start.9) | collective-permute-done | bytes 196640 | tf_op jit(solution)/shard_map/ppermute | solution.py:303
  46.6 0.0 collective-permute-done.1.other
  46.6 1.2 %copy-done.9 = bf16[64,8192]{1,0:T(8,128)(2,1)S(1)} copy-done((bf16[64,8192]{1,0:T(8,128)(2,1)S(1)}, bf16[64,8192]{1,0:T(8,128)(2,1)}, u32[]{:S(2)}) %copy-start.9) | copy-done | bytes 1048600
  47.8 0.9 copy-done.11
  48.7 11.0 %score.1.mine = f32[576,128]{1,0:T(8,128)S(1)} custom-call(s32[4096]{0:T(1024)S(1)} %bitcast.22, s32[1,128]{1,0:T(1,128)S(1)} %maximum_convert_fusion.group, f32[64,9,128]{2,1,0:T(8,128)S(1)} %get-tuple-element.38.cosine, f32[64,9,128]{2,1,0:T(8,128)S(1)} %get-tuple-element.37.sine, bf16[64,8192]{1,0:T(8,128)(2,1)S(1)} %copy-done.9, ...), custom_call_target="tpu_custom_call" | custom-call | flops 4000000000 | bytes 10000000 | tf_op jit(solution)/shard_map/score/pallas_call | solution.py:369
  59.7 0.1 collective-permute-start.10
  59.8 1.6 %collective-permute-done.10.theirs = f32[576,128]{1,0:T(8,128)S(1)} collective-permute-done((f32[576,128]{1,0:T(8,128)S(1)}, f32[576,128]{1,0:T(8,128)S(1)}, u32[]{:S(2)}, u32[]{:S(2)}) %collective-permute-start.10) | collective-permute-done | bytes 294944 | tf_op jit(solution)/shard_map/ppermute | solution.py:303
  61.4 15.1 %back.1 = (f32[1,128]{1,0:T(1,128)S(1)}, bf16[2048,128]{1,0:T(8,128)(2,1)S(1)}, bf16[2048,128]{1,0:T(8,128)(2,1)S(1)}, bf16[512,128]{1,0:T(8,128)(2,1)S(1)}, bf1...) custom-call(s32[4096]{0:T(1024)S(1)} %bitcast.23, f32[576,128]{1,0:T(8,128)S(1)} %score.1.mine, ...), custom_call_target="tpu_custom_call" | custom-call | flops 4000000000 | bytes 10000000 | tf_op jit(solution)/shard_map/back/pallas_call | solution.py:388
  76.5 1.5 %collective-permute-start.11 = (bf16[2048,128]{1,0:T(8,128)(2,1)S(1)}, bf16[2048,128]{1,0:T(8,128)(2,1)S(1)}, u32[]{:S(2)}, u32[]{:S(2)}) collective-permute-start(bf16[2048,128]{1,0:T(8,128)(2,1)S(1)} %get-tuple-element.24), channel_id=1, source_target_pairs={{0,2},{1,3},{2,0},{3,1},{4,6},{5,7},{6,4},{7,5},{8,10},{9,11},{10,... | collective-permute-start | bytes 1572872 | tf_op jit(solution)/shard_map/ppermute | solution.py:303
  78.0 0.0 collective-permute-start.15
  78.0 3.8 %collective-permute-start.16 = (bf16[512,128]{1,0:T(8,128)(2,1)}, bf16[512,128]{1,0:T(8,128)(2,1)S(1)}, u32[]{:S(2)}, u32[]{:S(2)}) collective-permute-start(bf16[512,128]{1,0:T(8,128)(2,1)} %get-tuple-element.27), channel_id=1, source_target_pairs={{0,12},{1,13},{2,14},{3,15},{4,0},{5,1},{6,2},{7,3},{8,4},{9,5},{1... | collective-permute-start | bytes 393224 | tf_op jit(solution)/shard_map/ppermute | solution.py:303
  81.8 0.0 collective-permute-start.17
  81.8 0.1 copy.11
  81.9 4.5 %collective-permute-done.15 = bf16[512,128]{1,0:T(8,128)(2,1)S(1)} collective-permute-done((bf16[512,128]{1,0:T(8,128)(2,1)}, bf16[512,128]{1,0:T(8,128)(2,1)S(1)}, u32[]{:S(2)}, u32[]{:S(2)}) %collective-permute-start.15) | collective-permute-done | bytes 131104 | tf_op jit(solution)/shard_map/ppermute | solution.py:303
  86.4 0.0 collective-permute-done.16
  86.4 6.3 %collective-permute-done.17 = bf16[512,128]{1,0:T(8,128)(2,1)S(1)} collective-permute-done((bf16[512,128]{1,0:T(8,128)(2,1)S(1)}, bf16[512,128]{1,0:T(8,128)(2,1)S(1)}, u32[]{:S(2)}, u32[]{:S(2)}) %collective-permute-start.17) | collective-permute-done | bytes 131104 | tf_op jit(solution)/shard_map/ppermute | solution.py:303
  92.8 0.1 convert_add_fusion.1
  92.9 0.6 collective-permute-start.18
  93.4 0.0 collective-permute-done.11
  93.4 0.8 copy-done.12
  94.2 1.2 %fusion.6 = (bf16[2048,128]{1,0:T(8,128)(2,1)S(1)}, f32[2048,128]{1,0:T(8,128)S(1)}) fusion(bf16[2048,128]{1,0:T(8,128)(2,1)} %copy-done.12, bf16[2048,128]{1,0:T(8,128)(2,1)S(1)} %get-tuple-element.23), kind=kLoop, calls=%fused_computation.27 | loop fusion | flops 1048576 | bytes 2621440 | tf_op jit(solution)/shard_map/convert_element_type | solution.py:407
  95.4 0.0 copy-start.4
  95.5 0.1 collective-permute-start.12
  95.5 3.8 %collective-permute-start.13 = (bf16[512,128]{1,0:T(8,128)(2,1)S(1)}, bf16[512,128]{1,0:T(8,128)(2,1)S(1)}, u32[]{:S(2)}, u32[]{:S(2)}) collective-permute-start(bf16[512,128]{1,0:T(8,128)(2,1)S(1)} %get-tuple-element.34), channel_id=1, source_target_pairs={{0,12},{1,13},{2,14},{3,15},{4,0},{5,1},{6,2},{7,3},{8,4},{9,5},{1... | collective-permute-start | bytes 393224 | tf_op jit(solution)/shard_map/ppermute | solution.py:303
  99.4 0.0 collective-permute-start.14
  99.4 4.5 %collective-permute-done.12 = bf16[512,128]{1,0:T(8,128)(2,1)S(1)} collective-permute-done((bf16[512,128]{1,0:T(8,128)(2,1)S(1)}, bf16[512,128]{1,0:T(8,128)(2,1)S(1)}, u32[]{:S(2)}, u32[]{:S(2)}) %collective-permute-start.12) | collective-permute-done | bytes 131104 | tf_op jit(solution)/shard_map/ppermute | solution.py:303
  103.9 0.0 collective-permute-done.13
  103.9 4.6 %collective-permute-done.14 = bf16[512,128]{1,0:T(8,128)(2,1)S(1)} collective-permute-done((bf16[512,128]{1,0:T(8,128)(2,1)S(1)}, bf16[512,128]{1,0:T(8,128)(2,1)S(1)}, u32[]{:S(2)}, u32[]{:S(2)}) %collective-permute-start.14) | collective-permute-done | bytes 131104 | tf_op jit(solution)/shard_map/ppermute | solution.py:303
  108.5 0.1 fusion.2
  108.6 0.1 collective-permute-start.19
  108.6 0.5 slice_bitcast_fusion
  109.2 0.9 collective-permute-done.19.other
  110.1 5.1 %adjoint.1 = f32[1024,256]{1,0:T(8,128)} custom-call(s32[4]{0:T(128)S(1)} %pad_add_fusion.meta, f32[8,384]{1,0:T(8,128)S(1)} %bitcast.18, f32[384,8]{1,0:T(8,128)S(1)} %get-tuple-element.16.slots, bf16[1024,256]{1,0:T(8,128)(2,1)S(1)} %copy-done.1, bf16[8,128,128]{2,1,0:T(8,128)(2,1)S(1)} %copy-done.4, f32[384,128]{1,0:T(8,128)S(1)} %get-tuple-element.36.keep, ...), custom_call_target="tpu_custom_call" | custom-call | flops 1000000000 | bytes 2000000 | tf_op jit(solution)/shard_map/adjoint/pallas_call | solution.py:424
  (33 shorter events, 0.2 us)
Async XLA Ops:
  0.6 10.1 %copy-start.5 = (s32[4096,1]{0,1:T(1,128)S(1)}, s32[4096,1]{0,1:T(1,128)}, u32[]{:S(2)}) copy-start(s32[4096,1]{0,1:T(1,128)} %param.13) | copy-start | bytes 49156
  0.6 10.0 %copy-start.6 = (s32[4096]{0:T(1024)S(1)}, s32[4096]{0:T(1024)}, u32[]{:S(2)}) copy-start(s32[4096]{0:T(1024)} %param.14) | copy-start | bytes 49156
  0.7 10.0 %copy-start.7 = (s32[4096]{0:T(1024)S(1)}, s32[4096]{0:T(1024)}, u32[]{:S(2)}) copy-start(s32[4096]{0:T(1024)} %param.15) | copy-start | bytes 49156
  1.5 1.6 %copy-start = (bf16[64,16384]{1,0:T(8,128)(2,1)S(1)}, bf16[64,16384]{1,0:T(8,128)(2,1)}, u32[]{:S(2)}) copy-start(bf16[64,16384]{1,0:T(8,128)(2,1)} %images.1) | copy-start | bytes 6291460
  3.1 0.9 copy-start.2
  4.1 6.6 %copy-start.1 = (bf16[1024,256]{1,0:T(8,128)(2,1)S(1)}, bf16[1024,256]{1,0:T(8,128)(2,1)}, u32[]{:S(2)}) copy-start(bf16[1024,256]{1,0:T(8,128)(2,1)} %volume.3) | copy-start | bytes 1572868
  4.1 6.6 %copy-start.3 = (bf16[8,128,128]{2,1,0:T(8,128)(2,1)S(1)}, bf16[8,128,128]{2,1,0:T(8,128)(2,1)}, u32[]{:S(2)}) copy-start(bf16[8,128,128]{2,1,0:T(8,128)(2,1)} %interp.3) | copy-start | bytes 786436
  8.6 1.0 copy-start.8
  9.5 0.7 copy-start.10
  10.2 6.7 %copy-start.14 = (s32[64]{0:T(128)S(1)}, s32[64]{0:T(128)}, u32[]{:S(2)}) copy-start(s32[64]{0:T(128)} %param.10) | copy-start | bytes 772
  10.2 7.2 %copy-start.13 = (s32[9,2]{0,1:T(2,128)S(1)}, s32[9,2]{0,1:T(2,128)}, u32[]{:S(2)}) copy-start(s32[9,2]{0,1:T(2,128)} %param.11) | copy-start | bytes 220
  10.2 36.3 %collective-permute-start.1 = (bf16[64,8192]{1,0:T(8,128)(2,1)S(1)}, bf16[64,8192]{1,0:T(8,128)(2,1)S(1)}, u32[]{:S(2)}, u32[]{:S(2)}) collective-permute-start(bf16[64,8192]{1,0:T(8,128)(2,1)S(1)} %get-tuple-element.19), channel_id=1, source_target_pairs={{0,1},{1,0},{2,3},{3,2},{4,5},{5,4},{6,7},{7,6},{8,9},{9,8},{10,11... | collective-permute-start | bytes 3145736 | tf_op jit(solution)/shard_map/ppermute | solution.py:303
  16.8 1.4 %collective-permute-start.2 = (bf16[384,128]{1,0:T(8,128)(2,1)S(1)}, bf16[384,128]{1,0:T(8,128)(2,1)S(1)}, u32[]{:S(2)}, u32[]{:S(2)}) collective-permute-start(bf16[384,128]{1,0:T(8,128)(2,1)S(1)} %get-tuple-element.22), channel_id=1, source_target_pairs={{0,1},{1,0},{2,3},{3,2},{4,5},{5,4},{6,7},{7,6},{8,9},{9,8},{10,11... | collective-permute-start | bytes 294920 | tf_op jit(solution)/shard_map/ppermute | solution.py:303
  16.9 7.2 %collective-permute-start = (f32[1,64]{1,0:T(1,128)S(1)}, f32[1,64]{1,0:T(1,128)S(1)}, u32[]{:S(2)}, u32[]{:S(2)}) collective-permute-start(f32[1,64]{1,0:T(1,128)S(1)} %convert_bitcast_fusion.2), channel_id=1, source_target_pairs={{0,1},{1,0},{2,3},{3,2},{4,5},{5,4},{6,7},{7,6},{8,9},{9,8},{10,11... | collective-permute-start | bytes 776 | tf_op jit(solution)/shard_map/ppermute | solution.py:303
  18.2 10.1 %collective-permute-start.4 = (bf16[768,128]{1,0:T(8,128)(2,1)S(1)}, bf16[768,128]{1,0:T(8,128)(2,1)S(1)}, u32[]{:S(2)}, u32[]{:S(2)}) collective-permute-start(bf16[768,128]{1,0:T(8,128)(2,1)S(1)} %constant_dynamic-update-slice_fusion.rest_0_), channel_id=1, source_target_pairs={{0,12},{1,13},{2,14},{3,15},{4,0},{5,1},{6,2},{7,3},{8,4},{9,5},{1... | collective-permute-start | bytes 589832 | tf_op jit(solution)/shard_map/ppermute | solution.py:303
  23.0 10.5 %collective-permute-start.5 = (bf16[768,128]{1,0:T(8,128)(2,1)S(1)}, bf16[768,128]{1,0:T(8,128)(2,1)S(1)}, u32[]{:S(2)}, u32[]{:S(2)}) collective-permute-start(bf16[768,128]{1,0:T(8,128)(2,1)S(1)} %constant_dynamic-update-slice_fusion.rest_0_), channel_id=1, source_target_pairs={{0,4},{1,5},{2,6},{3,7},{4,8},{5,9},{6,10},{7,11},{8,12},{9,13},{1... | collective-permute-start | bytes 589832 | tf_op jit(solution)/shard_map/ppermute | solution.py:303
  23.0 17.2 %collective-permute-start.6 = (bf16[768,128]{1,0:T(8,128)(2,1)S(1)}, bf16[768,128]{1,0:T(8,128)(2,1)S(1)}, u32[]{:S(2)}, u32[]{:S(2)}) collective-permute-start(bf16[768,128]{1,0:T(8,128)(2,1)S(1)} %constant_dynamic-update-slice_fusion.rest_0_), channel_id=1, source_target_pairs={{0,8},{1,9},{2,10},{3,11},{4,12},{5,13},{6,14},{7,15},{8,0},{9,1},... | collective-permute-start | bytes 589832 | tf_op jit(solution)/shard_map/ppermute | solution.py:303
  24.1 19.6 %collective-permute-start.3 = (bf16[768,128]{1,0:T(8,128)(2,1)S(1)}, bf16[768,128]{1,0:T(8,128)(2,1)S(1)}, u32[]{:S(2)}, u32[]{:S(2)}) collective-permute-start(bf16[768,128]{1,0:T(8,128)(2,1)S(1)} %constant_dynamic-update-slice_fusion.rest_0_), channel_id=1, source_target_pairs={{0,2},{1,3},{2,0},{3,1},{4,6},{5,7},{6,4},{7,5},{8,10},{9,11},{10,... | collective-permute-start | bytes 589832 | tf_op jit(solution)/shard_map/ppermute | solution.py:303
  28.3 15.4 %collective-permute-start.7 = (bf16[768,128]{1,0:T(8,128)(2,1)S(1)}, bf16[768,128]{1,0:T(8,128)(2,1)S(1)}, u32[]{:S(2)}, u32[]{:S(2)}) collective-permute-start(bf16[768,128]{1,0:T(8,128)(2,1)S(1)} %collective-permute-done.4.rest_2_), channel_id=1, source_target_pairs={{0,2},{1,3},{2,0},{3,1},{4,6},{5,7},{6,4},{7,5},{8,10},{9,11},{10,... | collective-permute-start | bytes 589832 | tf_op jit(solution)/shard_map/ppermute | solution.py:303
  33.5 10.3 %collective-permute-start.8 = (bf16[768,128]{1,0:T(8,128)(2,1)S(1)}, bf16[768,128]{1,0:T(8,128)(2,1)S(1)}, u32[]{:S(2)}, u32[]{:S(2)}) collective-permute-start(bf16[768,128]{1,0:T(8,128)(2,1)S(1)} %collective-permute-done.5.rest_3_), channel_id=1, source_target_pairs={{0,2},{1,3},{2,0},{3,1},{4,6},{5,7},{6,4},{7,5},{8,10},{9,11},{10,... | collective-permute-start | bytes 589832 | tf_op jit(solution)/shard_map/ppermute | solution.py:303
  40.2 6.3 %collective-permute-start.9 = (bf16[768,128]{1,0:T(8,128)(2,1)S(1)}, bf16[768,128]{1,0:T(8,128)(2,1)S(1)}, u32[]{:S(2)}, u32[]{:S(2)}) collective-permute-start(bf16[768,128]{1,0:T(8,128)(2,1)S(1)} %collective-permute-done.6.rest_4_), channel_id=1, source_target_pairs={{0,2},{1,3},{2,0},{3,1},{4,6},{5,7},{6,4},{7,5},{8,10},{9,11},{10,... | collective-permute-start | bytes 589832 | tf_op jit(solution)/shard_map/ppermute | solution.py:303
  46.6 1.2 %copy-start.9 = (bf16[64,8192]{1,0:T(8,128)(2,1)S(1)}, bf16[64,8192]{1,0:T(8,128)(2,1)}, u32[]{:S(2)}) copy-start(bf16[64,8192]{1,0:T(8,128)(2,1)} %copy-done.8) | copy-start | bytes 3145732
  47.8 0.9 copy-start.11
  59.7 1.6 %collective-permute-start.10 = (f32[576,128]{1,0:T(8,128)S(1)}, f32[576,128]{1,0:T(8,128)S(1)}, u32[]{:S(2)}, u32[]{:S(2)}) collective-permute-start(f32[576,128]{1,0:T(8,128)S(1)} %score.1.mine), channel_id=1, source_target_pairs={{0,1},{1,0},{2,3},{3,2},{4,5},{5,4},{6,7},{7,6},{8,9},{9,8},{10,11... | collective-permute-start | bytes 884744 | tf_op jit(solution)/shard_map/ppermute | solution.py:303
  76.5 16.9 %collective-permute-start.11 = (bf16[2048,128]{1,0:T(8,128)(2,1)S(1)}, bf16[2048,128]{1,0:T(8,128)(2,1)S(1)}, u32[]{:S(2)}, u32[]{:S(2)}) collective-permute-start(bf16[2048,128]{1,0:T(8,128)(2,1)S(1)} %get-tuple-element.24), channel_id=1, source_target_pairs={{0,2},{1,3},{2,0},{3,1},{4,6},{5,7},{6,4},{7,5},{8,10},{9,11},{10,... | collective-permute-start | bytes 1572872 | tf_op jit(solution)/shard_map/ppermute | solution.py:303
  78.0 8.4 %collective-permute-start.15 = (bf16[512,128]{1,0:T(8,128)(2,1)}, bf16[512,128]{1,0:T(8,128)(2,1)S(1)}, u32[]{:S(2)}, u32[]{:S(2)}) collective-permute-start(bf16[512,128]{1,0:T(8,128)(2,1)} %get-tuple-element.26), channel_id=1, source_target_pairs={{0,4},{1,5},{2,6},{3,7},{4,8},{5,9},{6,10},{7,11},{8,12},{9,13},{1... | collective-permute-start | bytes 393224 | tf_op jit(solution)/shard_map/ppermute | solution.py:303
  78.0 8.4 %collective-permute-start.16 = (bf16[512,128]{1,0:T(8,128)(2,1)}, bf16[512,128]{1,0:T(8,128)(2,1)S(1)}, u32[]{:S(2)}, u32[]{:S(2)}) collective-permute-start(bf16[512,128]{1,0:T(8,128)(2,1)} %get-tuple-element.27), channel_id=1, source_target_pairs={{0,12},{1,13},{2,14},{3,15},{4,0},{5,1},{6,2},{7,3},{8,4},{9,5},{1... | collective-permute-start | bytes 393224 | tf_op jit(solution)/shard_map/ppermute | solution.py:303
  81.8 10.9 %collective-permute-start.17 = (bf16[512,128]{1,0:T(8,128)(2,1)S(1)}, bf16[512,128]{1,0:T(8,128)(2,1)S(1)}, u32[]{:S(2)}, u32[]{:S(2)}) collective-permute-start(bf16[512,128]{1,0:T(8,128)(2,1)S(1)} %get-tuple-element.28), channel_id=1, source_target_pairs={{0,8},{1,9},{2,10},{3,11},{4,12},{5,13},{6,14},{7,15},{8,0},{9,1},... | collective-permute-start | bytes 393224 | tf_op jit(solution)/shard_map/ppermute | solution.py:303
  92.9 6.5 %collective-permute-start.18 = (bf16[256,128]{1,0:T(8,128)(2,1)S(1)}, bf16[256,128]{1,0:T(8,128)(2,1)S(1)}, u32[]{:S(2)}, u32[]{:S(2)}) collective-permute-start(bf16[256,128]{1,0:T(8,128)(2,1)S(1)} %slice.61), channel_id=1, source_target_pairs={{0,2},{1,3},{2,0},{3,1},{4,6},{5,7},{6,4},{7,5},{8,10},{9,11},{10,... | collective-permute-start | bytes 196616 | tf_op jit(solution)/shard_map/ppermute | solution.py:303
  93.4 0.8 copy-start.12
  95.4 14.6 %copy-start.4 = (bf16[8,128,128]{2,1,0:T(8,128)(2,1)S(1)}, bf16[8,128,128]{2,1,0:T(8,128)(2,1)}, u32[]{:S(2)}) copy-start(bf16[8,128,128]{2,1,0:T(8,128)(2,1)} %interp.3) | copy-start | bytes 786436
  95.5 8.4 %collective-permute-start.12 = (bf16[512,128]{1,0:T(8,128)(2,1)S(1)}, bf16[512,128]{1,0:T(8,128)(2,1)S(1)}, u32[]{:S(2)}, u32[]{:S(2)}) collective-permute-start(bf16[512,128]{1,0:T(8,128)(2,1)S(1)} %get-tuple-element.32), channel_id=1, source_target_pairs={{0,4},{1,5},{2,6},{3,7},{4,8},{5,9},{6,10},{7,11},{8,12},{9,13},{1... | collective-permute-start | bytes 393224 | tf_op jit(solution)/shard_map/ppermute | solution.py:303
  95.5 8.3 %collective-permute-start.13 = (bf16[512,128]{1,0:T(8,128)(2,1)S(1)}, bf16[512,128]{1,0:T(8,128)(2,1)S(1)}, u32[]{:S(2)}, u32[]{:S(2)}) collective-permute-start(bf16[512,128]{1,0:T(8,128)(2,1)S(1)} %get-tuple-element.34), channel_id=1, source_target_pairs={{0,12},{1,13},{2,14},{3,15},{4,0},{5,1},{6,2},{7,3},{8,4},{9,5},{1... | collective-permute-start | bytes 393224 | tf_op jit(solution)/shard_map/ppermute | solution.py:303
  99.4 9.1 %collective-permute-start.14 = (bf16[512,128]{1,0:T(8,128)(2,1)S(1)}, bf16[512,128]{1,0:T(8,128)(2,1)S(1)}, u32[]{:S(2)}, u32[]{:S(2)}) collective-permute-start(bf16[512,128]{1,0:T(8,128)(2,1)S(1)} %get-tuple-element.33), channel_id=1, source_target_pairs={{0,8},{1,9},{2,10},{3,11},{4,12},{5,13},{6,14},{7,15},{8,0},{9,1},... | collective-permute-start | bytes 393224 | tf_op jit(solution)/shard_map/ppermute | solution.py:303
  108.6 1.5 %collective-permute-start.19 = (f32[384,128]{1,0:T(8,128)S(1)}, f32[384,128]{1,0:T(8,128)S(1)}, u32[]{:S(2)}, u32[]{:S(2)}) collective-permute-start(f32[384,128]{1,0:T(8,128)S(1)} %get-tuple-element.35), channel_id=1, source_target_pairs={{0,1},{1,0},{2,3},{3,2},{4,5},{5,4},{6,7},{7,6},{8,9},{9,8},{10,11... | collective-permute-start | bytes 589832 | tf_op jit(solution)/shard_map/ppermute | solution.py:303

commit v2 on v1

--- a/solution.py
+++ b/solution.py
@@ -13,7 +13,7 @@
 R = 64
 HALF = BW // 2
 BLOCKS = R * KB
-GROUP = 8
+GROUP = 4
 
 F32 = jnp.float32
 BF16 = jnp.bfloat16
@@ -41,23 +41,22 @@
     )
 
 
-def slice_kernel(
-    devices, ny, nz, cap, meta, owner, local, table, volume, interp, target, slots, keep, send
-):
-    me = meta[0]
+def triangles(rows):
+    upper = jnp.where(iota((BW, BW), 0) <= iota((BW, BW), 1), 1.0, 0.0).astype(BF16)
+    lower = jnp.where(iota((rows, rows), 1) < iota((rows, rows), 0), 1.0, 0.0).astype(BF16)
+    return upper, jnp.ones((BW, BW), BF16), lower
+
+
+def target_kernel(devices, ny, nz, cap, meta, owner, target):
     z, y, core = meta[1], meta[2], meta[3]
     own = owner[...]
-    rows = own.shape[0]
-    upper = jnp.where(iota((BW, BW), 0) <= iota((BW, BW), 1), 1.0, 0.0).astype(BF16)
-    ones = jnp.ones((BW, BW), BF16)
-    lower = jnp.where(iota((rows, rows), 1) < iota((rows, rows), 0), 1.0, 0.0).astype(BF16)
+    upper, ones, lower = triangles(own.shape[0])
 
     def rank(d, pos):
         member = jnp.where(own == d, 1.0, 0.0)
         bits = member.astype(BF16)
-        inclusive = dot(bits, upper)
         before = dot(lower, dot(bits, ones).astype(BF16))
-        return pos + member * (inclusive - 1.0 + before)
+        return pos + member * (dot(bits, upper) - 1.0 + before)
 
     pos = jnp.zeros(own.shape, F32)
     if devices <= 16:
@@ -65,45 +64,71 @@
             pos = rank(d, pos)
     else:
         pos = lax.fori_loop(0, devices, rank, pos)
-    pos = pos.astype(jnp.int32)
-    shift_y = 1
-    shift_z = 1 + (ny.bit_length() - 1)
     rel_core = (own & 1) ^ core
-    rel_y = (lax.shift_right_logical(own, shift_y) - y) & (ny - 1)
-    rel_z = (lax.shift_right_logical(own, shift_z) - z) & (nz - 1)
-    target[...] = ((rel_z * ny + rel_y) * 2 + rel_core) * cap + pos
-
-    mine = jnp.where(own == me, pos, -1)
-    slot = iota((cap, BW), 0)
-    kind = iota((8, BW), 0)
-    loc, tab = local[...], table[...]
-    high = lax.shift_right_logical(loc, 8).astype(F32)
-    low = (loc & 255).astype(F32)
-    tab = tab.astype(F32)
-    found = jnp.zeros((cap, 8), F32)
-    for g in range(rows):
-        row = slice(g, g + 1)
-        hot = jnp.where(slot == mine[row], 1.0, 0.0).astype(BF16)
-        values = jnp.where(
-            kind == 0,
-            high[row],
-            jnp.where(kind == 1, low[row], jnp.where(kind == 2, tab[row], 1.0)),
-        ).astype(BF16)
-        found = found + dot(hot, values, NT)
-    valid = found[:, 3:4] > 0.5
-    place = jnp.where(valid, found[:, 0:1] * 256.0 + found[:, 1:2], -1.0)
-    which = found[:, 2:3]
+    rel_y = (lax.shift_right_logical(own, 1) - y) & (ny - 1)
+    rel_z = (lax.shift_right_logical(own, ny.bit_length()) - z) & (nz - 1)
+    target[...] = ((rel_z * ny + rel_y) * 2 + rel_core) * cap + pos.astype(jnp.int32)
+
+
+def slice_kernel(meta, *refs):
+    sources, (slots, keep, send), held, arrived = refs[:5], refs[5:8], refs[8:13], refs[13]
+    copies = [
+        pltpu.make_async_copy(source, place, arrived.at[i])
+        for i, (source, place) in enumerate(zip(sources, held))
+    ]
+    for copy in copies:
+        copy.start()
+    owner, local, table, volume, interp = held
+    me, core = meta[0], meta[3]
+    cap = keep.shape[0]
+    for copy in copies[:3]:
+        copy.wait()
+    own = owner[...]
+    rows = own.shape[0]
+    upper, ones, lower = triangles(rows)
+    member = own == me
+    bits = jnp.where(member, 1.0, 0.0).astype(BF16)
+    total = dot(bits, ones)
+    before = dot(lower, total.astype(BF16))
+    pos = (dot(bits, upper) - 1.0 + before).astype(jnp.int32)
+    number = iota((rows, cap), 1).astype(F32)
+    start, stop = before[:, 0:1], before[:, 0:1] + total[:, 0:1]
+    row_hot = jnp.where(number >= start, jnp.where(number < stop, 1.0, 0.0), 0.0)
+    loc = local[...]
+    fields = [
+        jnp.where(member, lax.shift_right_logical(pos, 7), 255),
+        pos & 127,
+        lax.shift_right_logical(loc, 8),
+        loc & 255,
+        table[...],
+    ]
+    fields = jnp.concatenate([f.astype(F32) for f in fields], axis=1).astype(BF16)
+    found = dot(row_hot.T.astype(BF16), fields)
+    slot = iota((cap, BW), 0).astype(F32)
+    valid = slot < stop[rows - 1 : rows]
+    hit = found[:, :BW] * 128.0 + found[:, BW : 2 * BW] == jnp.where(valid, slot, -1.0)
+    place = jnp.where(hit, found[:, 2 * BW : 3 * BW] * 256.0 + found[:, 3 * BW : 4 * BW], 0.0)
+    place = jnp.sum(place, axis=1, keepdims=True)
+    place = jnp.where(valid[:, 0:1], place, -1.0)
+    which = jnp.sum(jnp.where(hit, found[:, 4 * BW :], 0.0), axis=1, keepdims=True)
     column = iota((cap, 8), 1)
     slots[...] = jnp.where(column == 0, place, jnp.where(column == 1, which, 0.0))
 
+    for copy in copies[3:]:
+        copy.wait()
     depth = volume.shape[0]
     pick = jnp.where(iota((cap, depth), 1) == place.astype(jnp.int32), 1.0, 0.0).astype(BF16)
     voxels = dot(pick, volume[...])
     voxels = jnp.concatenate([voxels[:, :BW], voxels[:, BW:]], axis=0)
     which = jnp.concatenate([which, which], axis=0)
     out = jnp.zeros((2 * cap, BW), F32)
-    for t in range(interp.shape[0]):
-        out = out + dot(jnp.where(which == float(t), voxels, 0.0).astype(BF16), interp[t], NT)
+    for t in range(0, interp.shape[0], 2):
+        pair = [jnp.where(which == float(t + i), voxels, 0.0).astype(BF16) for i in range(2)]
+        out = out + dot(
+            jnp.concatenate(pair, axis=1),
+            jnp.concatenate([interp[t], interp[t + 1]], axis=1),
+            NT,
+        )
     left, right = split_halves(out[:cap], out[cap:])
     keep[...] = jnp.where(core == 0, left, right).astype(BF16)
     send[...] = jnp.where(core == 0, right, left).astype(BF16)
@@ -138,22 +163,39 @@
 
 
 def score_kernel(
-    order, rows, target, group, cosine, sine, keep, other, squares, *rest
+    places, target, group, cosine, sine, keep, other, squares, *rest
 ):
-    pieces = rest[: len(order)]
-    scores, gathered, block, left, power, norms = rest[len(order) :]
+    pieces = rest[: len(places)]
+    scores, gathered, norms, *stages = rest[len(places) :]
+    blocks, lefts, powers = stages[0:2], stages[2:4], stages[4:6]
     shifts = cosine.shape[1]
-    for number, piece in zip(order, pieces):
-        gathered[pl.ds(number * rows, rows), :] = piece[...].astype(F32)
+    steps = KB // GROUP
+    wide = GROUP * BW
+    for piece, moves in zip(pieces, places):
+        for source, size, start in moves:
+            gathered[start + 8 : start + 8 + size, :] = piece[source : source + size, :].astype(F32)
     scores[...] = jnp.zeros(scores.shape, F32)
     norms[...] = jnp.zeros(norms.shape, F32)
 
-    def body(group_index, carry):
+    sublane = iota((8, BW), 0)
+
+    def fetch(b, first):
+        value = None
+        for k in range(8):
+            row = target[(first + k) * KB + b]
+            loaded = gathered[pl.ds(row - k + 8, 8), :]
+            value = loaded if k == 0 else jnp.where(sublane == k, loaded, value)
+        return value
+
+    def gather(step, block):
         for part in range(GROUP):
-            b = group_index * GROUP + part
+            for first in range(0, R, 8):
+                block[part, first : first + 8, :] = fetch(step * GROUP + part, first)
+
+    def rotate(step, block, left, power):
+        for part in range(GROUP):
+            b = step * GROUP + part
             lanes = slice(part * BW, (part + 1) * BW)
-            for r in range(R):
-                block[part, r : r + 1, :] = gathered[pl.ds(target[r * KB + b], 1), :]
             value = block[part]
             swapped = swap_halves(value)
             for s in range(shifts):
@@ -163,13 +205,26 @@
             high = square.astype(BF16)
             power[0:R, lanes] = high
             power[R : 2 * R, lanes] = (square - high.astype(F32)).astype(BF16)
-        lanes = pl.ds(pl.multiple_of(group_index * GROUP * BW, BW), GROUP * BW)
+
+    def multiply(step, left, power):
+        lanes = pl.ds(pl.multiple_of(step * wide, wide), wide)
         right = jnp.concatenate([keep[:, lanes], other[:, lanes]], axis=0)
         scores[...] += dot(left[...], right, NT)
         norms[...] += dot(power[...], squares[:, lanes], NT)
+
+    def body(pair, carry):
+        for half in range(2):
+            step = 2 * pair + half
+            gather(jnp.minimum(step + 1, steps - 1), blocks[1 - half])
+            rotate(step, blocks[half], lefts[half], powers[half])
+            multiply(jnp.maximum(step - 1, 0), lefts[1 - half], powers[1 - half])
         return carry
 
-    lax.fori_loop(0, KB // GROUP, body, 0)
+    gather(0, blocks[0])
+    lefts[1][...] = jnp.zeros(lefts[1].shape, BF16)
+    powers[1][...] = jnp.zeros(powers[1].shape, BF16)
+    lax.fori_loop(0, steps // 2, body, 0)
+    multiply(steps - 1, lefts[1], powers[1])
     half = squares.shape[0] // 2
     total = norms[...]
     total = total[:R, :half] + total[:R, half:] + total[R:, :half] + total[R:, half:]
@@ -182,9 +237,9 @@
 
 def back_kernel(ny, nz, rows, first, target, mine, theirs, cosine, sine, keep, other, *rest):
     evidence = rest[0]
-    by_y = rest[1 : 1 + ny]
-    by_z = rest[1 + ny : 1 + ny + nz]
-    placed, block = rest[1 + ny + nz :]
+    parts = rest[1 : 1 + ny * nz]
+    by_z = rest[1 + ny * nz : 1 + ny * nz + nz]
+    (placed,) = rest[1 + ny * nz + nz :]
     shifts = cosine.shape[1]
     scale = 1.0 / math.sqrt(KB * BW)
     placed[...] = jnp.zeros(placed.shape, F32)
@@ -194,6 +249,7 @@
     total = jnp.sum(exponent, axis=0, keepdims=True)
     evidence[...] = top + jnp.log(total)
     weights = (exponent / total).astype(BF16)
+    sublane = iota((8, BW), 0)
 
     def body(pair, carry):
         lanes = pl.ds(pl.multiple_of(pair * 2 * BW, BW), 2 * BW)
@@ -207,18 +263,24 @@
                 term = sums[s * R : (s + 1) * R, part * BW : (part + 1) * BW]
                 straight = straight + term * cosine[b, s : s + 1, :]
                 crossed = crossed + term * sine[b, s : s + 1, :]
-            block[part] = straight + swap_halves(crossed)
+            value = straight + swap_halves(crossed)
             for r in range(R):
-                placed[pl.ds(target[r * KB + b], 1), :] = block[part, r : r + 1, :]
+                k = r % 8
+                row = target[r * KB + b]
+                pltpu.store(
+                    placed.at[pl.ds(row + (8 - k), 8), :],
+                    value[r - k : r - k + 8],
+                    mask=sublane == k,
+                )
         return carry
 
-    lax.fori_loop(0, KB // 2, body, 0)
+    lax.fori_loop(0, KB // 2, body, 0, unroll=4)
+    later = rows - first
     for kz in range(nz):
         for ky in range(ny):
-            start = (kz * ny + ky) * rows
-            by_y[ky][kz * first : (kz + 1) * first, :] = placed[start : start + first, :].astype(BF16)
-            rest_rows = rows - first
-            by_z[kz][ky * rest_rows : (ky + 1) * rest_rows, :] = placed[
+            start = (kz * ny + ky) * rows + 8
+            parts[kz * ny + ky][...] = placed[start : start + first, :].astype(BF16)
+            by_z[kz][ky * later : (ky + 1) * later, :] = placed[
                 start + first : start + rows, :
             ].astype(BF16)
 
@@ -236,36 +298,34 @@
     high = value.astype(BF16).astype(F32)
     rest = value - high
     out = jnp.zeros((2 * cap, BW), F32)
-    for t in range(interp.shape[0]):
-        chosen = which == float(t)
-        out = out + dot(jnp.where(chosen, high, 0.0).astype(BF16), interp[t])
-        out = out + dot(jnp.where(chosen, rest, 0.0).astype(BF16), interp[t])
+    for t in range(0, interp.shape[0], 2):
+        matrix = jnp.concatenate([interp[t], interp[t + 1]], axis=0)
+        for part in (high, rest):
+            pair = [jnp.where(which == float(t + i), part, 0.0).astype(BF16) for i in range(2)]
+            out = out + dot(jnp.concatenate(pair, axis=1), matrix)
     out = jnp.concatenate([out[:cap], out[cap:]], axis=1)
     depth = volume.shape[0]
     spread = jnp.where(
         iota((depth, cap), 0) == place[0:1, :].astype(jnp.int32), 1.0, 0.0
     ).astype(BF16)
     high = out.astype(BF16)
-    rest = out - high.astype(F32)
-    middle = rest.astype(BF16)
-    low = (rest - middle.astype(F32)).astype(BF16)
-    new_map[...] = volume[...].astype(F32) + (
-        dot(spread, high) + (dot(spread, middle) + dot(spread, low))
-    )
+    rest = (out - high.astype(F32)).astype(BF16)
+    new_map[...] = volume[...].astype(F32) + (dot(spread, high) + dot(spread, rest))
 
 
 SMEM = pl.BlockSpec(memory_space=pltpu.SMEM)
 VMEM = pl.BlockSpec(memory_space=pltpu.VMEM)
-
-
-def call(kernel, in_specs, out_shapes, scratch, flops, touched, name):
+ANY = pl.BlockSpec(memory_space=pl.ANY)
+
+
+def call(kernel, in_specs, out_shapes, scratch, flops, touched, name, limit=40):
     return pl.pallas_call(
         kernel,
         in_specs=in_specs,
         out_specs=[VMEM] * len(out_shapes),
         out_shape=out_shapes,
         scratch_shapes=scratch,
-        compiler_params=pltpu.CompilerParams(vmem_limit_bytes=40 * 1024 * 1024),
+        compiler_params=pltpu.CompilerParams(vmem_limit_bytes=limit * 1024 * 1024),
         cost_estimate=pl.CostEstimate(flops=flops, bytes_accessed=touched, transcendentals=0),
         name=name,
     )
@@ -303,32 +363,58 @@
         return lax.ppermute(array, "img", pairs)
 
     wide = (BLOCKS // BW, BW)
-    target, slots, slice_keep, slice_send = call(
-        functools.partial(slice_kernel, devices, ny, nz, cap),
-        [SMEM] + [VMEM] * 5,
-        [
-            struct(wide, jnp.int32),
-            struct((cap, 8), F32),
-            struct((cap, BW), BF16),
-            struct((cap, BW), BF16),
+    owner = owner.reshape(wide)
+    slots, slice_keep, slice_send = call(
+        slice_kernel,
+        [SMEM] + [ANY] * 5,
+        [struct((cap, 8), F32), struct((cap, BW), BF16), struct((cap, BW), BF16)],
+        [pltpu.VMEM(wide, jnp.int32)] * 3
+        + [
+            pltpu.VMEM(volume.shape, BF16),
+            pltpu.VMEM(interp.shape, BF16),
+            pltpu.SemaphoreType.DMA((5,)),
         ],
+        10**9,
+        10**6,
+        "own_slices",
+        60,
+    )(meta, owner, local.reshape(wide), table_id.reshape(wide), volume, interp)
+    own_piece = jnp.concatenate([slice_keep, to(slice_send, core_pairs)], axis=0)
+    images, owner, groups, shifts, _ = lax.optimization_barrier(
+        (images, owner, groups, shifts, own_piece)
+    )
+    (target,) = call(
+        functools.partial(target_kernel, devices, ny, nz, cap),
+        [SMEM, VMEM],
+        [struct(wide, jnp.int32)],
         [],
         10**9,
         10**6,
-        "own_slices",
-    )(meta, owner.reshape(wide), local.reshape(wide), table_id.reshape(wide), volume, interp)
+        "target",
+    )(meta, owner)
     target = target.reshape(BLOCKS)
-    own_piece = jnp.concatenate([slice_keep, to(slice_send, core_pairs)], axis=0)
-
-    pieces = {(0, 0): own_piece}
+
+    later = max(16, rows // 6 // 16 * 16)
+    first = rows - later
     near = sorted(range(1, nz), key=lambda k: min(k, nz - k))
+    pieces = [(own_piece, [(0, rows, 0)])]
+    others = [own_piece[first:]]
+    by_z = {kz: to(own_piece[:first], along_z(-kz)) for kz in near}
     for ky in range(1, ny):
-        pieces[0, ky] = to(own_piece, along_y(-ky))
+        piece = to(own_piece, along_y(-ky))
+        pieces.append((piece, [(0, rows, ky * rows)]))
+        others.append(piece[first:])
+    others = jnp.concatenate(others, axis=0)
     for kz in near:
-        pieces[kz, 0] = to(own_piece, along_z(-kz))
+        start = kz * ny * rows
+        pieces.append((by_z[kz], [(0, first, start)]))
+        for ky in range(1, ny):
+            piece = to(by_z[kz], along_y(-ky))
+            pieces.append((piece, [(0, first, start + ky * rows)]))
     for kz in near:
-        for ky in range(1, ny):
-            pieces[kz, ky] = to(pieces[kz, 0], along_y(-ky))
+        start = kz * ny * rows + first
+        piece = to(others, along_z(-kz))
+        pieces.append((piece, [(ky * later, later, start + ky * rows) for ky in range(ny)]))
 
     weight_keep, weight_send, squares = call(
         weigh_kernel,
@@ -365,50 +451,50 @@
     cosine = jnp.cos(angles)
     sine = jnp.sin(angles) * jnp.where(lane < HALF, -1.0, 1.0)
 
-    order = tuple(kz * ny + ky for kz, ky in pieces)
     (partial,) = call(
-        functools.partial(score_kernel, order, rows),
-        [SMEM] + [VMEM] * (6 + len(order)),
+        functools.partial(score_kernel, [moves for _, moves in pieces]),
+        [SMEM] + [VMEM] * (6 + len(pieces)),
         [struct((shift_count * R, 2 * count), F32)],
         [
-            pltpu.VMEM((chips * rows, BW), F32),
-            pltpu.VMEM((GROUP, R, BW), F32),
-            pltpu.VMEM((shift_count * R, GROUP * BW), BF16),
-            pltpu.VMEM((2 * R, GROUP * BW), BF16),
+            pltpu.VMEM((chips * rows + 16, BW), F32),
             pltpu.VMEM((2 * R, 2 * ctf.shape[0]), F32),
-        ],
+        ]
+        + [pltpu.VMEM((GROUP, R, BW), F32)] * 2
+        + [pltpu.VMEM((shift_count * R, GROUP * BW), BF16)] * 2
+        + [pltpu.VMEM((2 * R, GROUP * BW), BF16)] * 2,
         4 * 10**9,
         10**7,
         "score",
-    )(target, group_row, cosine, sine, weight_keep, weight_other, squares, *pieces.values())
+    )(target, group_row, cosine, sine, weight_keep, weight_other, squares, *[piece for piece, _ in pieces])
 
     theirs = to(partial, core_pairs)
-    first = rows * 2 // 3
-    later = rows - first
     outs = call(
         functools.partial(back_kernel, ny, nz, rows, first),
         [SMEM] + [VMEM] * 6,
         [struct((1, 2 * count), F32)]
-        + [struct((nz * first, BW), BF16)] * ny
+        + [struct((first, BW), BF16)] * chips
         + [struct((ny * later, BW), BF16)] * nz,
-        [pltpu.VMEM((chips * rows, BW), F32), pltpu.VMEM((2, R, BW), F32)],
+        [pltpu.VMEM((chips * rows + 16, BW), F32)],
         4 * 10**9,
         10**7,
         "back",
     )(target, partial, theirs, cosine, sine, weight_keep, weight_other)
     evidence = outs[0][0, :count]
-    by_y, by_z = outs[1 : 1 + ny], outs[1 + ny :]
-
-    from_y = [to(by_y[ky], along_y(ky)) for ky in range(1, ny)]
-    from_z = [to(by_z[kz], along_z(kz)) for kz in near]
-    summed_y = by_y[0].astype(F32)
-    for part in from_y:
-        summed_y = summed_y + part.astype(F32)
-    packed_y = summed_y.astype(BF16)
-    final_first = summed_y[:first]
-    for kz in near:
-        part = to(packed_y[kz * first : (kz + 1) * first], along_z(kz))
-        final_first = final_first + part.astype(F32)
+    parts, by_z = outs[1 : 1 + chips], outs[1 + chips :]
+
+    far = near[::-1]
+    summed = {}
+    from_y = {}
+    for kz in far + [0]:
+        from_y[kz] = [to(parts[kz * ny + ky], along_y(ky)) for ky in range(1, ny)]
+    from_z = [to(by_z[kz], along_z(kz)) for kz in far]
+    for kz in far + [0]:
+        summed[kz] = parts[kz * ny].astype(F32)
+        for part in from_y[kz]:
+            summed[kz] = summed[kz] + part.astype(F32)
+    final_first = summed[0]
+    for kz in far:
+        final_first = final_first + to(summed[kz].astype(BF16), along_z(kz)).astype(F32)
     summed_z = by_z[0].astype(F32)
     for part in from_z:
         summed_z = summed_z + part.astype(F32)

time: 116 us -> 91.3 us (0.79)
  waiting for transfers between devices: 37.4 us -> 22.8 us
  Pallas kernels: 41.8 us -> 32 us
  starting transfers between devices: 22.9 us -> 29.7 us
  local copies, waits for them, and re-layouts: 8.59 us -> 2.31 us
    ppermute x20 -> x26, waiting for transfers between devices: 37.4 us -> 22.8 us  [to(): return lax.ppermute(array, 'img', pairs)]
    ppermute x20 -> x26, starting transfers between devices: 22.9 us -> 29.7 us  [to(): return lax.ppermute(array, 'img', pairs)]
    pallas_call x1, Pallas kernels: 15.1 us -> 8.66 us  [per_device(): call(functools.partial(back_kernel, ny, nz, rows, first), [SMEM] + [VMEM]...]
    unnamed x31 -> x19, local copies, waits for them, and re-layouts: 7.21 us -> 0.94 us
    pallas_call x2 -> x3, Pallas kernels: 17.1 us -> 14.6 us  [the longest x1 8.22 us: per_device(): call(functools.partial(score_kernel, [moves for _, moves in pieces]), [SM...]
  transfers between devices with their start and end apart: 20 -> 26, of which waited for: 11 -> 14; matrix products, arithmetic and copies ran while one was open for 4% -> 5% of each run, Pallas kernels for 5% -> 7%
where the time goes in v2:
time: 91.3 us; the launch traced here: 90.9 us
  Pallas kernels  32 us (35%)
  starting transfers between devices  29.7 us (33%)
  waiting for transfers between devices  22.8 us (25%)
  other arithmetic  3.12 us (3%)
  local copies, waits for them, and re-layouts  2.31 us (3%)
    ppermute x26, starting transfers between devices, to(): return lax.ppermute(array, 'img', pairs)  29.7 us
    ppermute x26, waiting for transfers between devices, to(): return lax.ppermute(array, 'img', pairs)  22.8 us
    pallas_call x1, Pallas kernels, per_device(): call(functools.partial(back_kernel, ny, nz, rows, first), [SMEM] + [VMEM]...  8.66 us
    pallas_call x1, Pallas kernels, per_device(): call(functools.partial(score_kernel, [moves for _, moves in pieces]), [SM...  8.22 us
    pallas_call x1, Pallas kernels, per_device(): call(weigh_kernel, [SMEM] + [VMEM] * 3, [struct((count, KB * BW), BF16),...  4.49 us
    pallas_call x1, Pallas kernels, per_device(): call(slice_kernel, [SMEM] + [ANY] * 5, [struct((cap, 8), F32), struct((ca...  4.32 us
    pallas_call x1, Pallas kernels, per_device(): call(adjoint_kernel, [SMEM] + [VMEM] * 6, [struct(volume.shape, F32)], []...  4.3 us
    pallas_call x1, Pallas kernels, per_device(): call(functools.partial(target_kernel, devices, ny, nz, cap), [SMEM, VMEM]...  2.02 us
  transfers between devices with their start and end apart: 26, of which 14 were waited for; matrix products, arithmetic and copies ran while one was open for 5% of the time, Pallas kernels for 7%

profile of v2, /device:TPU:0, one launch (start us, length us, event | category | flops | bytes accessed | tf_op | source)
XLA Modules:
  0.0 90.9 jit_solution(6472797577738840328)
XLA Ops:
  0.7 0.6 pad_add_fusion.meta
  1.3 4.3 %own_slices.1 = (f32[384,8]{1,0:T(8,128)}, bf16[384,128]{1,0:T(8,128)(2,1)}, bf16[384,128]{1,0:T(8,128)(2,1)}) custom-call(s32[4]{0:T(128)} %pad_add_fusion.meta, s32[32,128]{1,0:T(8,128)} %bitcast.19, s32[32,128]{1,0:T(8,128)} %bitcast.24, s32[32,128]{1,0:T(8,128)} %bitcast.25, bf16[1024,256]{1,0:T(8,128)(2,1)} %volume.1, bf16[8,128,128]{2,1,0:T(8,128)(2,1)} %interp.1), custom_call_target="tpu_custom_call" | custom-call | flops 1000000000 | bytes 1000000 | tf_op jit(solution)/shard_map/own_slices/pallas_call | solution.py:367
  5.7 0.5 collective-permute-start
  6.2 0.9 constant_dynamic-update-slice_fusion.1
  7.1 0.0 copy-start.7
  7.1 0.2 collective-permute-done
  7.3 2.9 %collective-permute-start.3 = (bf16[768,128]{1,0:T(8,128)(2,1)S(1)}, bf16[768,128]{1,0:T(8,128)(2,1)S(1)}, u32[]{:S(2)}, u32[]{:S(2)}) collective-permute-start(bf16[768,128]{1,0:T(8,128)(2,1)S(1)} %constant_dynamic-update-slice_fusion.rest_0_), channel_id=1, source_target_pairs={{0,2},{1,3},{2,0},{3,1},{4,6},{5,7},{6,4},{7,5},{8,10},{9,11},{10,... | collective-permute-start | bytes 589832 | tf_op jit(solution)/shard_map/ppermute | solution.py:363
  10.3 0.7 slice.42
  10.9 3.6 %collective-permute-start.4 = (bf16[640,128]{1,0:T(8,128)(2,1)}, bf16[640,128]{1,0:T(8,128)(2,1)S(1)}, u32[]{:S(2)}, u32[]{:S(2)}) collective-permute-start(bf16[640,128]{1,0:T(8,128)(2,1)} %slice.42), channel_id=1, source_target_pairs={{0,12},{1,13},{2,14},{3,15},{4,0},{5,1},{6,2},{7,3},{8,4},{9,5},{1... | collective-permute-start | bytes 491528 | tf_op jit(solution)/shard_map/ppermute | solution.py:363
  14.5 1.0 %collective-permute-start.8 = (bf16[640,128]{1,0:T(8,128)(2,1)}, bf16[640,128]{1,0:T(8,128)(2,1)S(1)}, u32[]{:S(2)}, u32[]{:S(2)}) collective-permute-start(bf16[640,128]{1,0:T(8,128)(2,1)} %slice.42), channel_id=1, source_target_pairs={{0,8},{1,9},{2,10},{3,11},{4,12},{5,13},{6,14},{7,15},{8,0},{9,1},... | collective-permute-start | bytes 491528 | tf_op jit(solution)/shard_map/ppermute | solution.py:363
  15.6 0.1 copy.12.group
  15.7 0.0 copy-start.6
  15.7 4.5 %weigh.1 = (bf16[64,8192]{1,0:T(8,128)(2,1)S(1)}, bf16[64,8192]{1,0:T(8,128)(2,1)S(1)}, bf16[16,8192]{1,0:T(8,128)(2,1)S(1)}) custom-call(s32[4]{0:T(128)S(1)} %copy-done.1, bf16[64,16384]{1,0:T(8,128)(2,1)S(1)} %copy-done.2, s32[64,1]{1,0:T(8,128)S(1)} %copy.12.group, f32[8,8192]{1,0:T(8,128)S(1)} %copy-done.4), custom_call_target="tpu_custom_call" | custom-call | flops 1000000000 | bytes 4000000 | tf_op jit(solution)/shard_map/weigh/pallas_call | solution.py:419
  20.2 0.1 collective-permute-start.2
  20.3 0.1 broadcast_multiply_fusion.1
  20.4 0.1 broadcast_multiply_fusion
  20.4 0.5 collective-permute-start.1
  21.0 1.9 %collective-permute-done.1 = f32[1,64]{1,0:T(1,128)S(1)} collective-permute-done((f32[1,64]{1,0:T(1,128)S(1)}, f32[1,64]{1,0:T(1,128)S(1)}, u32[]{:S(2)}, u32[]{:S(2)}) %collective-permute-start.1) | collective-permute-done | bytes 288 | tf_op jit(solution)/shard_map/ppermute | solution.py:363
  22.9 2.8 %collective-permute-start.10 = (bf16[256,128]{1,0:T(8,128)(2,1)S(1)}, bf16[256,128]{1,0:T(8,128)(2,1)S(1)}, u32[]{:S(2)}, u32[]{:S(2)}) collective-permute-start(bf16[256,128]{1,0:T(8,128)(2,1)S(1)} %pad_maximum_fusion.1), channel_id=1, source_target_pairs={{0,12},{1,13},{2,14},{3,15},{4,0},{5,1},{6,2},{7,3},{8,4},{9,5},{1... | collective-permute-start | bytes 196616 | tf_op jit(solution)/shard_map/ppermute | solution.py:363
  25.7 1.9 %sine_multiply_fusion = (f32[64,9,128]{2,1,0:T(8,128)S(1)}, f32[64,9,128]{2,1,0:T(8,128)S(1)}) fusion(f32[128]{0:T(128)S(1)} %compare_select_fusion, f32[64,9]{1,0:T(8,128)S(1)} %broadcast_multiply_fusion, f32[9,128]{1,0:T(8,128)S(1)} %broadcast_multiply_fusion.1), kind=kLoop, calls=%fused_computation | loop fusion | flops 221184 | bytes 597248 | tf_op jit(solution)/shard_map/mul | solution.py:452
  27.6 0.0 collective-permute-done.4.rest_2_
  27.7 0.6 collective-permute-start.5
  28.2 0.0 collective-permute-done.6.rest_4_
  28.2 1.5 %collective-permute-start.7 = (bf16[640,128]{1,0:T(8,128)(2,1)S(1)}, bf16[640,128]{1,0:T(8,128)(2,1)S(1)}, u32[]{:S(2)}, u32[]{:S(2)}) collective-permute-start(bf16[640,128]{1,0:T(8,128)(2,1)S(1)} %collective-permute-done.6.rest_4_), channel_id=1, source_target_pairs={{0,2},{1,3},{2,0},{3,1},{4,6},{5,7},{6,4},{7,5},{8,10},{9,11},{10,... | collective-permute-start | bytes 491528 | tf_op jit(solution)/shard_map/ppermute | solution.py:363
  29.8 0.5 collective-permute-start.9
  30.3 0.6 collective-permute-start.11
  30.8 2.0 %target.1 = s32[32,128]{1,0:T(8,128)S(1)} custom-call(s32[4]{0:T(128)S(1)} %copy-done.1, s32[32,128]{1,0:T(8,128)S(1)} %bitcast.20), custom_call_target="tpu_custom_call" | custom-call | flops 1000000000 | bytes 1000000 | tf_op jit(solution)/shard_map/target/pallas_call | solution.py:386
  32.9 3.5 %collective-permute-done.11.rest_9_ = bf16[256,128]{1,0:T(8,128)(2,1)S(1)} collective-permute-done((bf16[256,128]{1,0:T(8,128)(2,1)S(1)}, bf16[256,128]{1,0:T(8,128)(2,1)S(1)}, u32[]{:S(2)}, u32[]{:S(2)}) %collective-permute-start.11) | collective-permute-done | bytes 65568 | tf_op jit(solution)/shard_map/ppermute | solution.py:363
  36.3 0.2 collective-permute-start.12
  36.6 0.1 maximum_convert_fusion.group
  36.6 4.9 %collective-permute-done.12.rest_10_ = bf16[256,128]{1,0:T(8,128)(2,1)S(1)} collective-permute-done((bf16[256,128]{1,0:T(8,128)(2,1)S(1)}, bf16[256,128]{1,0:T(8,128)(2,1)S(1)}, u32[]{:S(2)}, u32[]{:S(2)}) %collective-permute-start.12) | collective-permute-done | bytes 65568 | tf_op jit(solution)/shard_map/ppermute | solution.py:363
  41.5 0.0 collective-permute-done.7.rest_5_
  41.5 0.0 collective-permute-done.9.rest_7_
  41.5 0.0 collective-permute-done.2.other
  41.5 8.2 %score.1.mine = f32[576,128]{1,0:T(8,128)S(1)} custom-call(s32[4096]{0:T(1024)S(1)} %bitcast.21, s32[1,128]{1,0:T(1,128)S(1)} %maximum_convert_fusion.group, f32[64,9,128]{2,1,0:T(8,128)S(1)} %get-tuple-element.51.cosine, f32[64,9,128]{2,1,0:T(8,128)S(1)} %get-tuple-element.50.sine, bf16[64,8192]{1,0:T(8,128)(2,1)S(1)} %get-tuple-element.32.keep, ...), custom_call_target="tpu_custom_call" | custom-call | flops 4000000000 | bytes 10000000 | tf_op jit(solution)/shard_map/score/pallas_call | solution.py:454
  49.7 0.0 copy-start
  49.8 0.1 collective-permute-start.13
  49.8 1.6 %collective-permute-done.13.theirs = f32[576,128]{1,0:T(8,128)S(1)} collective-permute-done((f32[576,128]{1,0:T(8,128)S(1)}, f32[576,128]{1,0:T(8,128)S(1)}, u32[]{:S(2)}, u32[]{:S(2)}) %collective-permute-start.13) | collective-permute-done | bytes 294944 | tf_op jit(solution)/shard_map/ppermute | solution.py:363
  51.4 8.7 %back.1 = (f32[1,128]{1,0:T(1,128)S(1)}, bf16[640,128]{1,0:T(8,128)(2,1)S(1)}, bf16[640,128]{1,0:T(8,128)(2,1)S(1)}, bf16[640,128]{1,0:T(8,128)(2,1)S(1)}, bf16[...) custom-call(s32[4096]{0:T(1024)S(1)} %bitcast.22, ...), custom_call_target="tpu_custom_call" | custom-call | flops 4000000000 | bytes 10000000 | tf_op jit(solution)/shard_map/back/pallas_call | solution.py:471
  60.1 1.3 %collective-permute-start.21 = (bf16[256,128]{1,0:T(8,128)(2,1)S(1)}, bf16[256,128]{1,0:T(8,128)(2,1)S(1)}, u32[]{:S(2)}, u32[]{:S(2)}) collective-permute-start(bf16[256,128]{1,0:T(8,128)(2,1)S(1)} %get-tuple-element.44), channel_id=1, source_target_pairs={{0,8},{1,9},{2,10},{3,11},{4,12},{5,13},{6,14},{7,15},{8,0},{9,1},... | collective-permute-start | bytes 196616 | tf_op jit(solution)/shard_map/ppermute | solution.py:363
  61.3 1.2 %collective-permute-start.22 = (bf16[256,128]{1,0:T(8,128)(2,1)S(1)}, bf16[256,128]{1,0:T(8,128)(2,1)S(1)}, u32[]{:S(2)}, u32[]{:S(2)}) collective-permute-start(bf16[256,128]{1,0:T(8,128)(2,1)S(1)} %get-tuple-element.45), channel_id=1, source_target_pairs={{0,12},{1,13},{2,14},{3,15},{4,0},{5,1},{6,2},{7,3},{8,4},{9,5},{1... | collective-permute-start | bytes 196616 | tf_op jit(solution)/shard_map/ppermute | solution.py:363
  62.5 0.8 collective-permute-start.23
  63.4 0.1 copy.11
  63.4 0.7 collective-permute-start.15
  64.2 1.3 %collective-permute-start.17 = (bf16[640,128]{1,0:T(8,128)(2,1)S(1)}, bf16[640,128]{1,0:T(8,128)(2,1)S(1)}, u32[]{:S(2)}, u32[]{:S(2)}) collective-permute-start(bf16[640,128]{1,0:T(8,128)(2,1)S(1)} %get-tuple-element.40), channel_id=1, source_target_pairs={{0,2},{1,3},{2,0},{3,1},{4,6},{5,7},{6,4},{7,5},{8,10},{9,11},{10,... | collective-permute-start | bytes 491528 | tf_op jit(solution)/shard_map/ppermute | solution.py:363
  65.5 0.6 collective-permute-done.21
  66.2 1.4 %collective-permute-start.19 = (bf16[640,128]{1,0:T(8,128)(2,1)S(1)}, bf16[640,128]{1,0:T(8,128)(2,1)S(1)}, u32[]{:S(2)}, u32[]{:S(2)}) collective-permute-start(bf16[640,128]{1,0:T(8,128)(2,1)S(1)} %get-tuple-element.42), channel_id=1, source_target_pairs={{0,2},{1,3},{2,0},{3,1},{4,6},{5,7},{6,4},{7,5},{8,10},{9,11},{10,... | collective-permute-start | bytes 491528 | tf_op jit(solution)/shard_map/ppermute | solution.py:363
  67.6 0.6 collective-permute-start.14
  68.2 0.5 collective-permute-done.23
  68.7 1.2 %collective-permute-start.24 = (bf16[128,128]{1,0:T(8,128)(2,1)S(1)}, bf16[128,128]{1,0:T(8,128)(2,1)S(1)}, u32[]{:S(2)}, u32[]{:S(2)}) collective-permute-start(bf16[128,128]{1,0:T(8,128)(2,1)S(1)} %slice.53), channel_id=1, source_target_pairs={{0,2},{1,3},{2,0},{3,1},{4,6},{5,7},{6,4},{7,5},{8,10},{9,11},{10,... | collective-permute-start | bytes 98312 | tf_op jit(solution)/shard_map/ppermute | solution.py:363
  69.9 0.7 collective-permute-done.15
  70.7 1.8 %collective-permute-start.16 = (bf16[640,128]{1,0:T(8,128)(2,1)S(1)}, bf16[640,128]{1,0:T(8,128)(2,1)S(1)}, u32[]{:S(2)}, u32[]{:S(2)}) collective-permute-start(bf16[640,128]{1,0:T(8,128)(2,1)S(1)} %add_convert_fusion.2), channel_id=1, source_target_pairs={{0,8},{1,9},{2,10},{3,11},{4,12},{5,13},{6,14},{7,15},{8,0},{9,1},... | collective-permute-start | bytes 491528 | tf_op jit(solution)/shard_map/ppermute | solution.py:363
  72.5 1.7 %collective-permute-done.17 = bf16[640,128]{1,0:T(8,128)(2,1)S(1)} collective-permute-done((bf16[640,128]{1,0:T(8,128)(2,1)S(1)}, bf16[640,128]{1,0:T(8,128)(2,1)S(1)}, u32[]{:S(2)}, u32[]{:S(2)}) %collective-permute-start.17) | collective-permute-done | bytes 163872 | tf_op jit(solution)/shard_map/ppermute | solution.py:363
  74.2 3.0 %collective-permute-start.18 = (bf16[640,128]{1,0:T(8,128)(2,1)S(1)}, bf16[640,128]{1,0:T(8,128)(2,1)S(1)}, u32[]{:S(2)}, u32[]{:S(2)}) collective-permute-start(bf16[640,128]{1,0:T(8,128)(2,1)S(1)} %add_convert_fusion.1), channel_id=1, source_target_pairs={{0,12},{1,13},{2,14},{3,15},{4,0},{5,1},{6,2},{7,3},{8,4},{9,5},{1... | collective-permute-start | bytes 491528 | tf_op jit(solution)/shard_map/ppermute | solution.py:363
  77.2 0.4 collective-permute-done.19
  77.7 1.2 %collective-permute-start.20 = (bf16[640,128]{1,0:T(8,128)(2,1)S(1)}, bf16[640,128]{1,0:T(8,128)(2,1)S(1)}, u32[]{:S(2)}, u32[]{:S(2)}) collective-permute-start(bf16[640,128]{1,0:T(8,128)(2,1)S(1)} %add_convert_fusion), channel_id=1, source_target_pairs={{0,4},{1,5},{2,6},{3,7},{4,8},{5,9},{6,10},{7,11},{8,12},{9,13},{1... | collective-permute-start | bytes 491528 | tf_op jit(solution)/shard_map/ppermute | solution.py:363
  78.9 1.2 %collective-permute-done.24 = bf16[128,128]{1,0:T(8,128)(2,1)S(1)} collective-permute-done((bf16[128,128]{1,0:T(8,128)(2,1)S(1)}, bf16[128,128]{1,0:T(8,128)(2,1)S(1)}, u32[]{:S(2)}, u32[]{:S(2)}) %collective-permute-start.24) | collective-permute-done | bytes 32800 | tf_op jit(solution)/shard_map/ppermute | solution.py:363
  80.1 2.8 %collective-permute-done.16 = bf16[640,128]{1,0:T(8,128)(2,1)S(1)} collective-permute-done((bf16[640,128]{1,0:T(8,128)(2,1)S(1)}, bf16[640,128]{1,0:T(8,128)(2,1)S(1)}, u32[]{:S(2)}, u32[]{:S(2)}) %collective-permute-start.16) | collective-permute-done | bytes 163872 | tf_op jit(solution)/shard_map/ppermute | solution.py:363
  83.0 2.0 %collective-permute-done.20 = bf16[640,128]{1,0:T(8,128)(2,1)S(1)} collective-permute-done((bf16[640,128]{1,0:T(8,128)(2,1)S(1)}, bf16[640,128]{1,0:T(8,128)(2,1)S(1)}, u32[]{:S(2)}, u32[]{:S(2)}) %collective-permute-start.20) | collective-permute-done | bytes 163872 | tf_op jit(solution)/shard_map/ppermute | solution.py:363
  84.9 0.1 convert_add_fusion
  85.1 0.1 collective-permute-start.25
  85.1 0.5 slice_bitcast_fusion
  85.7 0.9 %collective-permute-done.25.other = f32[384,128]{1,0:T(8,128)S(1)} collective-permute-done((f32[384,128]{1,0:T(8,128)S(1)}, f32[384,128]{1,0:T(8,128)S(1)}, u32[]{:S(2)}, u32[]{:S(2)}) %collective-permute-start.25) | collective-permute-done | bytes 196640 | tf_op jit(solution)/shard_map/ppermute | solution.py:363
  86.6 4.3 %adjoint.1 = f32[1024,256]{1,0:T(8,128)} custom-call(s32[4]{0:T(128)S(1)} %copy-done.1, f32[8,384]{1,0:T(8,128)S(1)} %bitcast.18, f32[384,8]{1,0:T(8,128)S(1)} %copy-done, bf16[1024,256]{1,0:T(8,128)(2,1)S(1)} %copy-done.3, bf16[8,128,128]{2,1,0:T(8,128)(2,1)S(1)} %copy-done.5, f32[384,128]{1,0:T(8,128)S(1)} %get-tuple-element.49.keep, ...), custom_call_target="tpu_custom_call" | custom-call | flops 1000000000 | bytes 2000000 | tf_op jit(solution)/shard_map/adjoint/pallas_call | solution.py:510
  (39 shorter events, 0.3 us)
Async XLA Ops:
  1.3 14.2 %copy-start.8 = (s32[64]{0:T(128)S(1)}, s32[64]{0:T(128)}, u32[]{:S(2)}) copy-start(s32[64]{0:T(128)} %param.10) | copy-start | bytes 772
  1.3 14.3 %copy-start.1 = (s32[4]{0:T(128)S(1)}, s32[4]{0:T(128)}, u32[]{:S(2)}) copy-start(s32[4]{0:T(128)} %pad_add_fusion.meta) | copy-start | bytes 52
  1.3 14.3 %copy-start.2 = (bf16[64,16384]{1,0:T(8,128)(2,1)S(1)}, bf16[64,16384]{1,0:T(8,128)(2,1)}, u32[]{:S(2)}) copy-start(bf16[64,16384]{1,0:T(8,128)(2,1)} %images) | copy-start | bytes 6291460
  1.3 14.3 %copy-start.4 = (f32[8,8192]{1,0:T(8,128)S(1)}, f32[8,8192]{1,0:T(8,128)}, u32[]{:S(2)}) copy-start(f32[8,8192]{1,0:T(8,128)} %ctf.1) | copy-start | bytes 786436
  5.7 1.7 %collective-permute-start = (bf16[384,128]{1,0:T(8,128)(2,1)}, bf16[384,128]{1,0:T(8,128)(2,1)S(1)}, u32[]{:S(2)}, u32[]{:S(2)}) collective-permute-start(bf16[384,128]{1,0:T(8,128)(2,1)} %get-tuple-element.27), channel_id=1, source_target_pairs={{0,1},{1,0},{2,3},{3,2},{4,5},{5,4},{6,7},{7,6},{8,9},{9,8},{10,11... | collective-permute-start | bytes 294920 | tf_op jit(solution)/shard_map/ppermute | solution.py:363
  7.1 13.2 %copy-start.7 = (s32[9,2]{0,1:T(2,128)S(1)}, s32[9,2]{0,1:T(2,128)}, u32[]{:S(2)}) copy-start(s32[9,2]{0,1:T(2,128)} %param.11) | copy-start | bytes 220
  7.3 13.1 %collective-permute-start.3 = (bf16[768,128]{1,0:T(8,128)(2,1)S(1)}, bf16[768,128]{1,0:T(8,128)(2,1)S(1)}, u32[]{:S(2)}, u32[]{:S(2)}) collective-permute-start(bf16[768,128]{1,0:T(8,128)(2,1)S(1)} %constant_dynamic-update-slice_fusion.rest_0_), channel_id=1, source_target_pairs={{0,2},{1,3},{2,0},{3,1},{4,6},{5,7},{6,4},{7,5},{8,10},{9,11},{10,... | collective-permute-start | bytes 589832 | tf_op jit(solution)/shard_map/ppermute | solution.py:363
  10.9 16.7 %collective-permute-start.4 = (bf16[640,128]{1,0:T(8,128)(2,1)}, bf16[640,128]{1,0:T(8,128)(2,1)S(1)}, u32[]{:S(2)}, u32[]{:S(2)}) collective-permute-start(bf16[640,128]{1,0:T(8,128)(2,1)} %slice.42), channel_id=1, source_target_pairs={{0,12},{1,13},{2,14},{3,15},{4,0},{5,1},{6,2},{7,3},{8,4},{9,5},{1... | collective-permute-start | bytes 491528 | tf_op jit(solution)/shard_map/ppermute | solution.py:363
  14.5 13.7 %collective-permute-start.6 = (bf16[640,128]{1,0:T(8,128)(2,1)}, bf16[640,128]{1,0:T(8,128)(2,1)S(1)}, u32[]{:S(2)}, u32[]{:S(2)}) collective-permute-start(bf16[640,128]{1,0:T(8,128)(2,1)} %slice.42), channel_id=1, source_target_pairs={{0,4},{1,5},{2,6},{3,7},{4,8},{5,9},{6,10},{7,11},{8,12},{9,13},{1... | collective-permute-start | bytes 491528 | tf_op jit(solution)/shard_map/ppermute | solution.py:363
  14.5 15.2 %collective-permute-start.8 = (bf16[640,128]{1,0:T(8,128)(2,1)}, bf16[640,128]{1,0:T(8,128)(2,1)S(1)}, u32[]{:S(2)}, u32[]{:S(2)}) collective-permute-start(bf16[640,128]{1,0:T(8,128)(2,1)} %slice.42), channel_id=1, source_target_pairs={{0,8},{1,9},{2,10},{3,11},{4,12},{5,13},{6,14},{7,15},{8,0},{9,1},... | collective-permute-start | bytes 491528 | tf_op jit(solution)/shard_map/ppermute | solution.py:363
  15.7 15.2 %copy-start.6 = (s32[4096,1]{0,1:T(1,128)S(1)}, s32[4096,1]{0,1:T(1,128)}, u32[]{:S(2)}) copy-start(s32[4096,1]{0,1:T(1,128)} %param.13) | copy-start | bytes 49156
  20.2 21.3 %collective-permute-start.2 = (bf16[64,8192]{1,0:T(8,128)(2,1)S(1)}, bf16[64,8192]{1,0:T(8,128)(2,1)S(1)}, u32[]{:S(2)}, u32[]{:S(2)}) collective-permute-start(bf16[64,8192]{1,0:T(8,128)(2,1)S(1)} %get-tuple-element.33), channel_id=1, source_target_pairs={{0,1},{1,0},{2,3},{3,2},{4,5},{5,4},{6,7},{7,6},{8,9},{9,8},{10,11... | collective-permute-start | bytes 3145736 | tf_op jit(solution)/shard_map/ppermute | solution.py:363
  20.4 2.5 %collective-permute-start.1 = (f32[1,64]{1,0:T(1,128)S(1)}, f32[1,64]{1,0:T(1,128)S(1)}, u32[]{:S(2)}, u32[]{:S(2)}) collective-permute-start(f32[1,64]{1,0:T(1,128)S(1)} %convert_bitcast_fusion.2), channel_id=1, source_target_pairs={{0,1},{1,0},{2,3},{3,2},{4,5},{5,4},{6,7},{7,6},{8,9},{9,8},{10,11... | collective-permute-start | bytes 776 | tf_op jit(solution)/shard_map/ppermute | solution.py:363
  22.9 7.4 %collective-permute-start.10 = (bf16[256,128]{1,0:T(8,128)(2,1)S(1)}, bf16[256,128]{1,0:T(8,128)(2,1)S(1)}, u32[]{:S(2)}, u32[]{:S(2)}) collective-permute-start(bf16[256,128]{1,0:T(8,128)(2,1)S(1)} %pad_maximum_fusion.1), channel_id=1, source_target_pairs={{0,12},{1,13},{2,14},{3,15},{4,0},{5,1},{6,2},{7,3},{8,4},{9,5},{1... | collective-permute-start | bytes 196616 | tf_op jit(solution)/shard_map/ppermute | solution.py:363
  27.7 13.8 %collective-permute-start.5 = (bf16[640,128]{1,0:T(8,128)(2,1)S(1)}, bf16[640,128]{1,0:T(8,128)(2,1)S(1)}, u32[]{:S(2)}, u32[]{:S(2)}) collective-permute-start(bf16[640,128]{1,0:T(8,128)(2,1)S(1)} %collective-permute-done.4.rest_2_), channel_id=1, source_target_pairs={{0,2},{1,3},{2,0},{3,1},{4,6},{5,7},{6,4},{7,5},{8,10},{9,11},{10,... | collective-permute-start | bytes 491528 | tf_op jit(solution)/shard_map/ppermute | solution.py:363
  28.2 13.3 %collective-permute-start.7 = (bf16[640,128]{1,0:T(8,128)(2,1)S(1)}, bf16[640,128]{1,0:T(8,128)(2,1)S(1)}, u32[]{:S(2)}, u32[]{:S(2)}) collective-permute-start(bf16[640,128]{1,0:T(8,128)(2,1)S(1)} %collective-permute-done.6.rest_4_), channel_id=1, source_target_pairs={{0,2},{1,3},{2,0},{3,1},{4,6},{5,7},{6,4},{7,5},{8,10},{9,11},{10,... | collective-permute-start | bytes 491528 | tf_op jit(solution)/shard_map/ppermute | solution.py:363
  29.8 11.8 %collective-permute-start.9 = (bf16[640,128]{1,0:T(8,128)(2,1)S(1)}, bf16[640,128]{1,0:T(8,128)(2,1)S(1)}, u32[]{:S(2)}, u32[]{:S(2)}) collective-permute-start(bf16[640,128]{1,0:T(8,128)(2,1)S(1)} %collective-permute-done.8.rest_6_), channel_id=1, source_target_pairs={{0,2},{1,3},{2,0},{3,1},{4,6},{5,7},{6,4},{7,5},{8,10},{9,11},{10,... | collective-permute-start | bytes 491528 | tf_op jit(solution)/shard_map/ppermute | solution.py:363
  30.3 6.1 %collective-permute-start.11 = (bf16[256,128]{1,0:T(8,128)(2,1)S(1)}, bf16[256,128]{1,0:T(8,128)(2,1)S(1)}, u32[]{:S(2)}, u32[]{:S(2)}) collective-permute-start(bf16[256,128]{1,0:T(8,128)(2,1)S(1)} %pad_maximum_fusion.1), channel_id=1, source_target_pairs={{0,4},{1,5},{2,6},{3,7},{4,8},{5,9},{6,10},{7,11},{8,12},{9,13},{1... | collective-permute-start | bytes 196616 | tf_op jit(solution)/shard_map/ppermute | solution.py:363
  36.3 5.2 %collective-permute-start.12 = (bf16[256,128]{1,0:T(8,128)(2,1)S(1)}, bf16[256,128]{1,0:T(8,128)(2,1)S(1)}, u32[]{:S(2)}, u32[]{:S(2)}) collective-permute-start(bf16[256,128]{1,0:T(8,128)(2,1)S(1)} %pad_maximum_fusion.1), channel_id=1, source_target_pairs={{0,8},{1,9},{2,10},{3,11},{4,12},{5,13},{6,14},{7,15},{8,0},{9,1},... | collective-permute-start | bytes 196616 | tf_op jit(solution)/shard_map/ppermute | solution.py:363
  49.7 13.6 %copy-start = (f32[384,8]{1,0:T(8,128)S(1)}, f32[384,8]{1,0:T(8,128)}, u32[]{:S(2)}) copy-start(f32[384,8]{1,0:T(8,128)} %get-tuple-element.25.slots) | copy-start | bytes 36868
  49.8 1.6 %collective-permute-start.13 = (f32[576,128]{1,0:T(8,128)S(1)}, f32[576,128]{1,0:T(8,128)S(1)}, u32[]{:S(2)}, u32[]{:S(2)}) collective-permute-start(f32[576,128]{1,0:T(8,128)S(1)} %score.1.mine), channel_id=1, source_target_pairs={{0,1},{1,0},{2,3},{3,2},{4,5},{5,4},{6,7},{7,6},{8,9},{9,8},{10,11... | collective-permute-start | bytes 884744 | tf_op jit(solution)/shard_map/ppermute | solution.py:363
  60.1 6.1 %collective-permute-start.21 = (bf16[256,128]{1,0:T(8,128)(2,1)S(1)}, bf16[256,128]{1,0:T(8,128)(2,1)S(1)}, u32[]{:S(2)}, u32[]{:S(2)}) collective-permute-start(bf16[256,128]{1,0:T(8,128)(2,1)S(1)} %get-tuple-element.44), channel_id=1, source_target_pairs={{0,8},{1,9},{2,10},{3,11},{4,12},{5,13},{6,14},{7,15},{8,0},{9,1},... | collective-permute-start | bytes 196616 | tf_op jit(solution)/shard_map/ppermute | solution.py:363
  61.3 6.2 %collective-permute-start.22 = (bf16[256,128]{1,0:T(8,128)(2,1)S(1)}, bf16[256,128]{1,0:T(8,128)(2,1)S(1)}, u32[]{:S(2)}, u32[]{:S(2)}) collective-permute-start(bf16[256,128]{1,0:T(8,128)(2,1)S(1)} %get-tuple-element.45), channel_id=1, source_target_pairs={{0,12},{1,13},{2,14},{3,15},{4,0},{5,1},{6,2},{7,3},{8,4},{9,5},{1... | collective-permute-start | bytes 196616 | tf_op jit(solution)/shard_map/ppermute | solution.py:363
  62.5 6.1 %collective-permute-start.23 = (bf16[256,128]{1,0:T(8,128)(2,1)S(1)}, bf16[256,128]{1,0:T(8,128)(2,1)S(1)}, u32[]{:S(2)}, u32[]{:S(2)}) collective-permute-start(bf16[256,128]{1,0:T(8,128)(2,1)S(1)} %get-tuple-element.46), channel_id=1, source_target_pairs={{0,4},{1,5},{2,6},{3,7},{4,8},{5,9},{6,10},{7,11},{8,12},{9,13},{1... | collective-permute-start | bytes 196616 | tf_op jit(solution)/shard_map/ppermute | solution.py:363
  63.4 7.2 %collective-permute-start.15 = (bf16[640,128]{1,0:T(8,128)(2,1)S(1)}, bf16[640,128]{1,0:T(8,128)(2,1)S(1)}, u32[]{:S(2)}, u32[]{:S(2)}) collective-permute-start(bf16[640,128]{1,0:T(8,128)(2,1)S(1)} %get-tuple-element.38), channel_id=1, source_target_pairs={{0,2},{1,3},{2,0},{3,1},{4,6},{5,7},{6,4},{7,5},{8,10},{9,11},{10,... | collective-permute-start | bytes 491528 | tf_op jit(solution)/shard_map/ppermute | solution.py:363
  64.2 10.0 %collective-permute-start.17 = (bf16[640,128]{1,0:T(8,128)(2,1)S(1)}, bf16[640,128]{1,0:T(8,128)(2,1)S(1)}, u32[]{:S(2)}, u32[]{:S(2)}) collective-permute-start(bf16[640,128]{1,0:T(8,128)(2,1)S(1)} %get-tuple-element.40), channel_id=1, source_target_pairs={{0,2},{1,3},{2,0},{3,1},{4,6},{5,7},{6,4},{7,5},{8,10},{9,11},{10,... | collective-permute-start | bytes 491528 | tf_op jit(solution)/shard_map/ppermute | solution.py:363
  66.2 11.5 %collective-permute-start.19 = (bf16[640,128]{1,0:T(8,128)(2,1)S(1)}, bf16[640,128]{1,0:T(8,128)(2,1)S(1)}, u32[]{:S(2)}, u32[]{:S(2)}) collective-permute-start(bf16[640,128]{1,0:T(8,128)(2,1)S(1)} %get-tuple-element.42), channel_id=1, source_target_pairs={{0,2},{1,3},{2,0},{3,1},{4,6},{5,7},{6,4},{7,5},{8,10},{9,11},{10,... | collective-permute-start | bytes 491528 | tf_op jit(solution)/shard_map/ppermute | solution.py:363
  67.6 12.6 %collective-permute-start.14 = (bf16[640,128]{1,0:T(8,128)(2,1)S(1)}, bf16[640,128]{1,0:T(8,128)(2,1)S(1)}, u32[]{:S(2)}, u32[]{:S(2)}) collective-permute-start(bf16[640,128]{1,0:T(8,128)(2,1)S(1)} %get-tuple-element.36), channel_id=1, source_target_pairs={{0,2},{1,3},{2,0},{3,1},{4,6},{5,7},{6,4},{7,5},{8,10},{9,11},{10,... | collective-permute-start | bytes 491528 | tf_op jit(solution)/shard_map/ppermute | solution.py:363
  68.6 17.9 %copy-start.3 = (bf16[1024,256]{1,0:T(8,128)(2,1)S(1)}, bf16[1024,256]{1,0:T(8,128)(2,1)}, u32[]{:S(2)}) copy-start(bf16[1024,256]{1,0:T(8,128)(2,1)} %volume.1) | copy-start | bytes 1572868
  68.6 17.9 %copy-start.5 = (bf16[8,128,128]{2,1,0:T(8,128)(2,1)S(1)}, bf16[8,128,128]{2,1,0:T(8,128)(2,1)}, u32[]{:S(2)}) copy-start(bf16[8,128,128]{2,1,0:T(8,128)(2,1)} %interp.1) | copy-start | bytes 786436
  68.7 11.4 %collective-permute-start.24 = (bf16[128,128]{1,0:T(8,128)(2,1)S(1)}, bf16[128,128]{1,0:T(8,128)(2,1)S(1)}, u32[]{:S(2)}, u32[]{:S(2)}) collective-permute-start(bf16[128,128]{1,0:T(8,128)(2,1)S(1)} %slice.53), channel_id=1, source_target_pairs={{0,2},{1,3},{2,0},{3,1},{4,6},{5,7},{6,4},{7,5},{8,10},{9,11},{10,... | collective-permute-start | bytes 98312 | tf_op jit(solution)/shard_map/ppermute | solution.py:363
  70.7 12.3 %collective-permute-start.16 = (bf16[640,128]{1,0:T(8,128)(2,1)S(1)}, bf16[640,128]{1,0:T(8,128)(2,1)S(1)}, u32[]{:S(2)}, u32[]{:S(2)}) collective-permute-start(bf16[640,128]{1,0:T(8,128)(2,1)S(1)} %add_convert_fusion.2), channel_id=1, source_target_pairs={{0,8},{1,9},{2,10},{3,11},{4,12},{5,13},{6,14},{7,15},{8,0},{9,1},... | collective-permute-start | bytes 491528 | tf_op jit(solution)/shard_map/ppermute | solution.py:363
  74.2 8.8 %collective-permute-start.18 = (bf16[640,128]{1,0:T(8,128)(2,1)S(1)}, bf16[640,128]{1,0:T(8,128)(2,1)S(1)}, u32[]{:S(2)}, u32[]{:S(2)}) collective-permute-start(bf16[640,128]{1,0:T(8,128)(2,1)S(1)} %add_convert_fusion.1), channel_id=1, source_target_pairs={{0,12},{1,13},{2,14},{3,15},{4,0},{5,1},{6,2},{7,3},{8,4},{9,5},{1... | collective-permute-start | bytes 491528 | tf_op jit(solution)/shard_map/ppermute | solution.py:363
  77.7 7.2 %collective-permute-start.20 = (bf16[640,128]{1,0:T(8,128)(2,1)S(1)}, bf16[640,128]{1,0:T(8,128)(2,1)S(1)}, u32[]{:S(2)}, u32[]{:S(2)}) collective-permute-start(bf16[640,128]{1,0:T(8,128)(2,1)S(1)} %add_convert_fusion), channel_id=1, source_target_pairs={{0,4},{1,5},{2,6},{3,7},{4,8},{5,9},{6,10},{7,11},{8,12},{9,13},{1... | collective-permute-start | bytes 491528 | tf_op jit(solution)/shard_map/ppermute | solution.py:363
  85.1 1.5 %collective-permute-start.25 = (f32[384,128]{1,0:T(8,128)S(1)}, f32[384,128]{1,0:T(8,128)S(1)}, u32[]{:S(2)}, u32[]{:S(2)}) collective-permute-start(f32[384,128]{1,0:T(8,128)S(1)} %get-tuple-element.48), channel_id=1, source_target_pairs={{0,1},{1,0},{2,3},{3,2},{4,5},{5,4},{6,7},{7,6},{8,9},{9,8},{10,11... | collective-permute-start | bytes 589832 | tf_op jit(solution)/shard_map/ppermute | solution.py:363

commit v3 on v2

--- a/solution.py
+++ b/solution.py
@@ -121,14 +121,10 @@
     voxels = dot(pick, volume[...])
     voxels = jnp.concatenate([voxels[:, :BW], voxels[:, BW:]], axis=0)
     which = jnp.concatenate([which, which], axis=0)
-    out = jnp.zeros((2 * cap, BW), F32)
-    for t in range(0, interp.shape[0], 2):
-        pair = [jnp.where(which == float(t + i), voxels, 0.0).astype(BF16) for i in range(2)]
-        out = out + dot(
-            jnp.concatenate(pair, axis=1),
-            jnp.concatenate([interp[t], interp[t + 1]], axis=1),
-            NT,
-        )
+    tables = range(interp.shape[0])
+    chosen = [jnp.where(which == float(t), voxels, 0.0).astype(BF16) for t in tables]
+    matrix = jnp.concatenate([interp[t] for t in tables], axis=1)
+    out = dot(jnp.concatenate(chosen, axis=1), matrix, NT)
     left, right = split_halves(out[:cap], out[cap:])
     keep[...] = jnp.where(core == 0, left, right).astype(BF16)
     send[...] = jnp.where(core == 0, right, left).astype(BF16)
@@ -159,7 +155,7 @@
         squares[:, lanes] = jnp.concatenate([high.astype(F32), rest], axis=0).astype(BF16)
         return carry
 
-    lax.fori_loop(0, KB, body, 0, unroll=2)
+    lax.fori_loop(0, KB, body, 0, unroll=8)
 
 
 def score_kernel(
@@ -295,14 +291,13 @@
     value = jnp.concatenate([real, imag], axis=0)
     which = slots[:, 1:2]
     which = jnp.concatenate([which, which], axis=0)
+    tables = range(interp.shape[0])
+    matrix = jnp.concatenate([interp[t] for t in tables], axis=0)
     high = value.astype(BF16).astype(F32)
-    rest = value - high
     out = jnp.zeros((2 * cap, BW), F32)
-    for t in range(0, interp.shape[0], 2):
-        matrix = jnp.concatenate([interp[t], interp[t + 1]], axis=0)
-        for part in (high, rest):
-            pair = [jnp.where(which == float(t + i), part, 0.0).astype(BF16) for i in range(2)]
-            out = out + dot(jnp.concatenate(pair, axis=1), matrix)
+    for part in (high, value - high):
+        chosen = [jnp.where(which == float(t), part, 0.0).astype(BF16) for t in tables]
+        out = out + dot(jnp.concatenate(chosen, axis=1), matrix)
     out = jnp.concatenate([out[:cap], out[cap:]], axis=1)
     depth = volume.shape[0]
     spread = jnp.where(
@@ -310,7 +305,9 @@
     ).astype(BF16)
     high = out.astype(BF16)
     rest = (out - high.astype(F32)).astype(BF16)
-    new_map[...] = volume[...].astype(F32) + (dot(spread, high) + dot(spread, rest))
+    new_map[...] = volume[...].astype(F32) + dot(
+        jnp.concatenate([spread, spread], axis=1), jnp.concatenate([high, rest], axis=0)
+    )
 
 
 SMEM = pl.BlockSpec(memory_space=pltpu.SMEM)
@@ -380,9 +377,23 @@
         60,
     )(meta, owner, local.reshape(wide), table_id.reshape(wide), volume, interp)
     own_piece = jnp.concatenate([slice_keep, to(slice_send, core_pairs)], axis=0)
-    images, owner, groups, shifts, _ = lax.optimization_barrier(
-        (images, owner, groups, shifts, own_piece)
-    )
+    images, groups, _ = lax.optimization_barrier((images, groups, own_piece))
+
+    later = max(16, rows // 6 // 16 * 16)
+    first = rows - later
+    near = sorted(range(1, nz), key=lambda k: min(k, nz - k))
+    pieces = [(own_piece, [(0, rows, 0)])]
+    by_z = {kz: to(own_piece, along_z(-kz)) for kz in near}
+    for ky in range(1, ny):
+        pieces.append((to(own_piece, along_y(-ky)), [(0, rows, ky * rows)]))
+    for kz in near:
+        start = kz * ny * rows
+        pieces.append((by_z[kz], [(0, rows, start)]))
+        for ky in range(1, ny):
+            piece = to(by_z[kz], along_y(-ky))
+            pieces.append((piece, [(0, rows, start + ky * rows)]))
+
+    owner, shifts, _ = lax.optimization_barrier((owner, shifts, by_z[near[0]]))
     (target,) = call(
         functools.partial(target_kernel, devices, ny, nz, cap),
         [SMEM, VMEM],
@@ -393,28 +404,6 @@
         "target",
     )(meta, owner)
     target = target.reshape(BLOCKS)
-
-    later = max(16, rows // 6 // 16 * 16)
-    first = rows - later
-    near = sorted(range(1, nz), key=lambda k: min(k, nz - k))
-    pieces = [(own_piece, [(0, rows, 0)])]
-    others = [own_piece[first:]]
-    by_z = {kz: to(own_piece[:first], along_z(-kz)) for kz in near}
-    for ky in range(1, ny):
-        piece = to(own_piece, along_y(-ky))
-        pieces.append((piece, [(0, rows, ky * rows)]))
-        others.append(piece[first:])
-    others = jnp.concatenate(others, axis=0)
-    for kz in near:
-        start = kz * ny * rows
-        pieces.append((by_z[kz], [(0, first, start)]))
-        for ky in range(1, ny):
-            piece = to(by_z[kz], along_y(-ky))
-            pieces.append((piece, [(0, first, start + ky * rows)]))
-    for kz in near:
-        start = kz * ny * rows + first
-        piece = to(others, along_z(-kz))
-        pieces.append((piece, [(ky * later, later, start + ky * rows) for ky in range(ny)]))
 
     weight_keep, weight_send, squares = call(
         weigh_kernel,

time: 91.3 us -> 86 us (0.942)
  starting transfers between devices: 29.7 us -> 26.8 us
  Pallas kernels: 32 us -> 29.9 us
    ppermute x26 -> x23, starting transfers between devices: 29.7 us -> 26.8 us  [to(): return lax.ppermute(array, 'img', pairs)]
    pallas_call x1, Pallas kernels: 4.49 us -> 2.78 us  [per_device(): call(weigh_kernel, [SMEM] + [VMEM] * 3, [struct((count, KB * BW), BF16),...]
    ppermute x26 -> x23, waiting for transfers between devices: 22.8 us -> 23.3 us  [to(): return lax.ppermute(array, 'img', pairs)]
  transfers between devices with their start and end apart: 26 -> 23, of which waited for: 14 -> 13; matrix products, arithmetic and copies ran while one was open for 5% -> 5% of each run, Pallas kernels for 7% -> 6%
where the time goes in v3:
time: 86 us; the launch traced here: 85.7 us
  Pallas kernels  29.9 us (35%)
  starting transfers between devices  26.8 us (31%)
  waiting for transfers between devices  23.3 us (27%)
  other arithmetic  3.13 us (4%)
  local copies, waits for them, and re-layouts  1.65 us (2%)
  between operations  0.93 us (1%)
    ppermute x23, starting transfers between devices, to(): return lax.ppermute(array, 'img', pairs)  26.8 us
    ppermute x23, waiting for transfers between devices, to(): return lax.ppermute(array, 'img', pairs)  23.3 us
    pallas_call x1, Pallas kernels, per_device(): call(functools.partial(back_kernel, ny, nz, rows, first), [SMEM] + [VMEM]...  8.66 us
    pallas_call x1, Pallas kernels, per_device(): call(functools.partial(score_kernel, [moves for _, moves in pieces]), [SM...  8.23 us
    pallas_call x1, Pallas kernels, per_device(): call(slice_kernel, [SMEM] + [ANY] * 5, [struct((cap, 8), F32), struct((ca...  4.31 us
    pallas_call x1, Pallas kernels, per_device(): call(adjoint_kernel, [SMEM] + [VMEM] * 6, [struct(volume.shape, F32)], []...  3.88 us
    pallas_call x1, Pallas kernels, per_device(): call(weigh_kernel, [SMEM] + [VMEM] * 3, [struct((count, KB * BW), BF16),...  2.78 us
    pallas_call x1, Pallas kernels, per_device(): call(functools.partial(target_kernel, devices, ny, nz, cap), [SMEM, VMEM]...  2.02 us
  transfers between devices with their start and end apart: 23, of which 13 were waited for; matrix products, arithmetic and copies ran while one was open for 5% of the time, Pallas kernels for 6%

profile of v3, /device:TPU:0, one launch (start us, length us, event | category | flops | bytes accessed | tf_op | source)
XLA Modules:
  0.0 85.7 jit_solution(6097163235846701915)
XLA Ops:
  0.7 0.7 pad_add_fusion.meta
  1.4 4.3 %own_slices.1 = (f32[384,8]{1,0:T(8,128)}, bf16[384,128]{1,0:T(8,128)(2,1)}, bf16[384,128]{1,0:T(8,128)(2,1)}) custom-call(s32[4]{0:T(128)} %pad_add_fusion.meta, s32[32,128]{1,0:T(8,128)} %bitcast.19, s32[32,128]{1,0:T(8,128)} %bitcast.24, s32[32,128]{1,0:T(8,128)} %bitcast.25, bf16[1024,256]{1,0:T(8,128)(2,1)} %volume.1, bf16[8,128,128]{2,1,0:T(8,128)(2,1)} %interp.1), custom_call_target="tpu_custom_call" | custom-call | flops 1000000000 | bytes 1000000 | tf_op jit(solution)/shard_map/own_slices/pallas_call | solution.py:364
  5.7 0.0 copy-start.6
  5.7 0.5 collective-permute-start
  6.2 0.9 %constant_dynamic-update-slice_fusion.1 = bf16[768,128]{1,0:T(8,128)(2,1)S(1)} fusion(bf16[384,128]{1,0:T(8,128)(2,1)} %get-tuple-element.26), kind=kLoop, calls=%fused_computation.13 | loop fusion | bytes 196608
  7.1 0.2 collective-permute-done
  7.4 5.0 %collective-permute-start.1 = (bf16[768,128]{1,0:T(8,128)(2,1)S(1)}, bf16[768,128]{1,0:T(8,128)(2,1)S(1)}, u32[]{:S(2)}, u32[]{:S(2)}) collective-permute-start(bf16[768,128]{1,0:T(8,128)(2,1)S(1)} %constant_dynamic-update-slice_fusion.rest_0_), channel_id=1, source_target_pairs={{0,12},{1,13},{2,14},{3,15},{4,0},{5,1},{6,2},{7,3},{8,4},{9,5},{1... | collective-permute-start | bytes 589832 | tf_op jit(solution)/shard_map/ppermute | solution.py:360
  12.4 0.0 collective-permute-start.6
  12.4 1.0 %collective-permute-start.8 = (bf16[768,128]{1,0:T(8,128)(2,1)S(1)}, bf16[768,128]{1,0:T(8,128)(2,1)S(1)}, u32[]{:S(2)}, u32[]{:S(2)}) collective-permute-start(bf16[768,128]{1,0:T(8,128)(2,1)S(1)} %constant_dynamic-update-slice_fusion.rest_0_), channel_id=1, source_target_pairs={{0,8},{1,9},{2,10},{3,11},{4,12},{5,13},{6,14},{7,15},{8,0},{9,1},... | collective-permute-start | bytes 589832 | tf_op jit(solution)/shard_map/ppermute | solution.py:360
  13.4 1.5 %collective-permute-start.4 = (bf16[768,128]{1,0:T(8,128)(2,1)S(1)}, bf16[768,128]{1,0:T(8,128)(2,1)S(1)}, u32[]{:S(2)}, u32[]{:S(2)}) collective-permute-start(bf16[768,128]{1,0:T(8,128)(2,1)S(1)} %constant_dynamic-update-slice_fusion.rest_0_), channel_id=1, source_target_pairs={{0,2},{1,3},{2,0},{3,1},{4,6},{5,7},{6,4},{7,5},{8,10},{9,11},{10,... | collective-permute-start | bytes 589832 | tf_op jit(solution)/shard_map/ppermute | solution.py:360
  14.9 0.1 copy.12.group
  15.0 0.0 collective-permute-start.2
  15.1 2.8 %weigh.1 = (bf16[64,8192]{1,0:T(8,128)(2,1)S(1)}, bf16[64,8192]{1,0:T(8,128)(2,1)S(1)}, bf16[16,8192]{1,0:T(8,128)(2,1)S(1)}) custom-call(s32[4]{0:T(128)S(1)} %copy-done.1, bf16[64,16384]{1,0:T(8,128)(2,1)S(1)} %copy-done.2, s32[64,1]{1,0:T(8,128)S(1)} %copy.12.group, f32[8,8192]{1,0:T(8,128)S(1)} %copy-done.4), custom_call_target="tpu_custom_call" | custom-call | flops 1000000000 | bytes 4000000 | tf_op jit(solution)/shard_map/weigh/pallas_call | solution.py:408
  17.9 0.0 copy-start.7
  17.9 0.0 collective-permute-done.2
  17.9 0.5 collective-permute-start.3
  18.4 0.1 maximum_convert_fusion.group
  18.5 0.0 collective-permute-done.1.rest_2_
  18.5 0.7 collective-permute-start.5
  19.2 3.7 %collective-permute-done.6.rest_4_ = bf16[768,128]{1,0:T(8,128)(2,1)S(1)} collective-permute-done((bf16[768,128]{1,0:T(8,128)(2,1)S(1)}, bf16[768,128]{1,0:T(8,128)(2,1)S(1)}, u32[]{:S(2)}, u32[]{:S(2)}) %collective-permute-start.6) | collective-permute-done | bytes 196640 | tf_op jit(solution)/shard_map/ppermute | solution.py:360
  22.9 1.5 %collective-permute-start.7 = (bf16[768,128]{1,0:T(8,128)(2,1)S(1)}, bf16[768,128]{1,0:T(8,128)(2,1)S(1)}, u32[]{:S(2)}, u32[]{:S(2)}) collective-permute-start(bf16[768,128]{1,0:T(8,128)(2,1)S(1)} %collective-permute-done.6.rest_4_), channel_id=1, source_target_pairs={{0,2},{1,3},{2,0},{3,1},{4,6},{5,7},{6,4},{7,5},{8,10},{9,11},{10,... | collective-permute-start | bytes 589832 | tf_op jit(solution)/shard_map/ppermute | solution.py:360
  24.4 5.0 %collective-permute-done.8.rest_6_ = bf16[768,128]{1,0:T(8,128)(2,1)S(1)} collective-permute-done((bf16[768,128]{1,0:T(8,128)(2,1)S(1)}, bf16[768,128]{1,0:T(8,128)(2,1)S(1)}, u32[]{:S(2)}, u32[]{:S(2)}) %collective-permute-start.8) | collective-permute-done | bytes 196640 | tf_op jit(solution)/shard_map/ppermute | solution.py:360
  29.4 1.5 %collective-permute-start.9 = (bf16[768,128]{1,0:T(8,128)(2,1)S(1)}, bf16[768,128]{1,0:T(8,128)(2,1)S(1)}, u32[]{:S(2)}, u32[]{:S(2)}) collective-permute-start(bf16[768,128]{1,0:T(8,128)(2,1)S(1)} %collective-permute-done.8.rest_6_), channel_id=1, source_target_pairs={{0,2},{1,3},{2,0},{3,1},{4,6},{5,7},{6,4},{7,5},{8,10},{9,11},{10,... | collective-permute-start | bytes 589832 | tf_op jit(solution)/shard_map/ppermute | solution.py:360
  30.9 2.0 %target.1 = s32[32,128]{1,0:T(8,128)S(1)} custom-call(s32[4]{0:T(128)S(1)} %copy-done.1, s32[32,128]{1,0:T(8,128)S(1)} %bitcast.20), custom_call_target="tpu_custom_call" | custom-call | flops 1000000000 | bytes 1000000 | tf_op jit(solution)/shard_map/target/pallas_call | solution.py:397
  32.9 0.0 copy-done.7
  33.0 0.1 broadcast_multiply_fusion.1
  33.0 0.1 broadcast_multiply_fusion
  33.1 1.9 %sine_multiply_fusion = (f32[64,9,128]{2,1,0:T(8,128)S(1)}, f32[64,9,128]{2,1,0:T(8,128)S(1)}) fusion(f32[128]{0:T(128)S(1)} %compare_select_fusion, f32[64,9]{1,0:T(8,128)S(1)} %broadcast_multiply_fusion, f32[9,128]{1,0:T(8,128)S(1)} %broadcast_multiply_fusion.1), kind=kLoop, calls=%fused_computation | loop fusion | flops 221184 | bytes 597248 | tf_op jit(solution)/shard_map/mul | solution.py:441
  35.0 0.0 collective-permute-done.4.rest_1_
  35.1 0.0 collective-permute-done.5.rest_3_
  35.1 0.0 collective-permute-done.7.rest_5_
  35.1 0.5 collective-permute-done.9.rest_7_
  35.5 0.0 collective-permute-done.3.other
  35.5 8.2 %score.1.mine = f32[576,128]{1,0:T(8,128)S(1)} custom-call(s32[4096]{0:T(1024)S(1)} %bitcast.21, s32[1,128]{1,0:T(1,128)S(1)} %maximum_convert_fusion.group, f32[64,9,128]{2,1,0:T(8,128)S(1)} %get-tuple-element.51.cosine, f32[64,9,128]{2,1,0:T(8,128)S(1)} %get-tuple-element.50.sine, bf16[64,8192]{1,0:T(8,128)(2,1)S(1)} %get-tuple-element.32.keep, ...), custom_call_target="tpu_custom_call" | custom-call | flops 4000000000 | bytes 10000000 | tf_op jit(solution)/shard_map/score/pallas_call | solution.py:443
  43.8 0.0 copy-start
  43.8 0.1 collective-permute-start.10
  43.9 1.6 %collective-permute-done.10.theirs = f32[576,128]{1,0:T(8,128)S(1)} collective-permute-done((f32[576,128]{1,0:T(8,128)S(1)}, f32[576,128]{1,0:T(8,128)S(1)}, u32[]{:S(2)}, u32[]{:S(2)}) %collective-permute-start.10) | collective-permute-done | bytes 294944 | tf_op jit(solution)/shard_map/ppermute | solution.py:360
  45.4 8.7 %back.1 = (f32[1,128]{1,0:T(1,128)S(1)}, bf16[640,128]{1,0:T(8,128)(2,1)S(1)}, bf16[640,128]{1,0:T(8,128)(2,1)S(1)}, bf16[640,128]{1,0:T(8,128)(2,1)S(1)}, bf16[...) custom-call(s32[4096]{0:T(1024)S(1)} %bitcast.22, ...), custom_call_target="tpu_custom_call" | custom-call | flops 4000000000 | bytes 10000000 | tf_op jit(solution)/shard_map/back/pallas_call | solution.py:460
  54.1 0.2 collective-permute-start.18
  54.3 3.8 %collective-permute-start.19 = (bf16[256,128]{1,0:T(8,128)(2,1)S(1)}, bf16[256,128]{1,0:T(8,128)(2,1)S(1)}, u32[]{:S(2)}, u32[]{:S(2)}) collective-permute-start(bf16[256,128]{1,0:T(8,128)(2,1)S(1)} %get-tuple-element.45), channel_id=1, source_target_pairs={{0,12},{1,13},{2,14},{3,15},{4,0},{5,1},{6,2},{7,3},{8,4},{9,5},{1... | collective-permute-start | bytes 196616 | tf_op jit(solution)/shard_map/ppermute | solution.py:360
  58.2 0.1 copy.11
  58.2 0.6 collective-permute-start.12
  58.8 1.5 %collective-permute-start.14 = (bf16[640,128]{1,0:T(8,128)(2,1)S(1)}, bf16[640,128]{1,0:T(8,128)(2,1)S(1)}, u32[]{:S(2)}, u32[]{:S(2)}) collective-permute-start(bf16[640,128]{1,0:T(8,128)(2,1)S(1)} %get-tuple-element.40), channel_id=1, source_target_pairs={{0,2},{1,3},{2,0},{3,1},{4,6},{5,7},{6,4},{7,5},{8,10},{9,11},{10,... | collective-permute-start | bytes 491528 | tf_op jit(solution)/shard_map/ppermute | solution.py:360
  60.3 0.8 collective-permute-done.18
  61.1 1.1 %collective-permute-start.16 = (bf16[640,128]{1,0:T(8,128)(2,1)S(1)}, bf16[640,128]{1,0:T(8,128)(2,1)S(1)}, u32[]{:S(2)}, u32[]{:S(2)}) collective-permute-start(bf16[640,128]{1,0:T(8,128)(2,1)S(1)} %get-tuple-element.42), channel_id=1, source_target_pairs={{0,2},{1,3},{2,0},{3,1},{4,6},{5,7},{6,4},{7,5},{8,10},{9,11},{10,... | collective-permute-start | bytes 491528 | tf_op jit(solution)/shard_map/ppermute | solution.py:360
  62.3 0.0 collective-permute-done.19
  62.3 0.9 %collective-permute-start.11 = (bf16[640,128]{1,0:T(8,128)(2,1)S(1)}, bf16[640,128]{1,0:T(8,128)(2,1)S(1)}, u32[]{:S(2)}, u32[]{:S(2)}) collective-permute-start(bf16[640,128]{1,0:T(8,128)(2,1)S(1)} %get-tuple-element.36), channel_id=1, source_target_pairs={{0,2},{1,3},{2,0},{3,1},{4,6},{5,7},{6,4},{7,5},{8,10},{9,11},{10,... | collective-permute-start | bytes 491528 | tf_op jit(solution)/shard_map/ppermute | solution.py:360
  63.2 1.1 %collective-permute-done.20 = bf16[256,128]{1,0:T(8,128)(2,1)S(1)} collective-permute-done((bf16[256,128]{1,0:T(8,128)(2,1)S(1)}, bf16[256,128]{1,0:T(8,128)(2,1)S(1)}, u32[]{:S(2)}, u32[]{:S(2)}) %collective-permute-start.20) | collective-permute-done | bytes 65568 | tf_op jit(solution)/shard_map/ppermute | solution.py:360
  64.3 0.7 collective-permute-start.21
  65.0 0.5 collective-permute-done.12
  65.5 1.0 %collective-permute-start.13 = (bf16[640,128]{1,0:T(8,128)(2,1)S(1)}, bf16[640,128]{1,0:T(8,128)(2,1)S(1)}, u32[]{:S(2)}, u32[]{:S(2)}) collective-permute-start(bf16[640,128]{1,0:T(8,128)(2,1)S(1)} %add_convert_fusion.2), channel_id=1, source_target_pairs={{0,8},{1,9},{2,10},{3,11},{4,12},{5,13},{6,14},{7,15},{8,0},{9,1},... | collective-permute-start | bytes 491528 | tf_op jit(solution)/shard_map/ppermute | solution.py:360
  66.5 2.4 %collective-permute-done.14 = bf16[640,128]{1,0:T(8,128)(2,1)S(1)} collective-permute-done((bf16[640,128]{1,0:T(8,128)(2,1)S(1)}, bf16[640,128]{1,0:T(8,128)(2,1)S(1)}, u32[]{:S(2)}, u32[]{:S(2)}) %collective-permute-start.14) | collective-permute-done | bytes 163872 | tf_op jit(solution)/shard_map/ppermute | solution.py:360
  69.0 3.9 %collective-permute-start.15 = (bf16[640,128]{1,0:T(8,128)(2,1)S(1)}, bf16[640,128]{1,0:T(8,128)(2,1)S(1)}, u32[]{:S(2)}, u32[]{:S(2)}) collective-permute-start(bf16[640,128]{1,0:T(8,128)(2,1)S(1)} %add_convert_fusion.1), channel_id=1, source_target_pairs={{0,12},{1,13},{2,14},{3,15},{4,0},{5,1},{6,2},{7,3},{8,4},{9,5},{1... | collective-permute-start | bytes 491528 | tf_op jit(solution)/shard_map/ppermute | solution.py:360
  72.9 0.0 collective-permute-done.16
  72.9 0.6 collective-permute-start.17
  73.5 1.7 %collective-permute-done.21 = bf16[128,128]{1,0:T(8,128)(2,1)S(1)} collective-permute-done((bf16[128,128]{1,0:T(8,128)(2,1)S(1)}, bf16[128,128]{1,0:T(8,128)(2,1)S(1)}, u32[]{:S(2)}, u32[]{:S(2)}) %collective-permute-start.21) | collective-permute-done | bytes 32800 | tf_op jit(solution)/shard_map/ppermute | solution.py:360
  75.2 1.7 %collective-permute-done.13 = bf16[640,128]{1,0:T(8,128)(2,1)S(1)} collective-permute-done((bf16[640,128]{1,0:T(8,128)(2,1)S(1)}, bf16[640,128]{1,0:T(8,128)(2,1)S(1)}, u32[]{:S(2)}, u32[]{:S(2)}) %collective-permute-start.13) | collective-permute-done | bytes 163872 | tf_op jit(solution)/shard_map/ppermute | solution.py:360
  76.9 0.0 collective-permute-done.15
  76.9 3.3 %collective-permute-done.17 = bf16[640,128]{1,0:T(8,128)(2,1)S(1)} collective-permute-done((bf16[640,128]{1,0:T(8,128)(2,1)S(1)}, bf16[640,128]{1,0:T(8,128)(2,1)S(1)}, u32[]{:S(2)}, u32[]{:S(2)}) %collective-permute-start.17) | collective-permute-done | bytes 163872 | tf_op jit(solution)/shard_map/ppermute | solution.py:360
  80.2 0.1 convert_add_fusion
  80.3 0.1 collective-permute-start.22
  80.4 0.5 slice_bitcast_fusion
  80.9 0.9 %collective-permute-done.22.other = f32[384,128]{1,0:T(8,128)S(1)} collective-permute-done((f32[384,128]{1,0:T(8,128)S(1)}, f32[384,128]{1,0:T(8,128)S(1)}, u32[]{:S(2)}, u32[]{:S(2)}) %collective-permute-start.22) | collective-permute-done | bytes 196640 | tf_op jit(solution)/shard_map/ppermute | solution.py:360
  81.8 3.9 %adjoint.1 = f32[1024,256]{1,0:T(8,128)} custom-call(s32[4]{0:T(128)S(1)} %copy-done.1, f32[8,384]{1,0:T(8,128)S(1)} %bitcast.18, f32[384,8]{1,0:T(8,128)S(1)} %copy-done, bf16[1024,256]{1,0:T(8,128)(2,1)S(1)} %copy-done.3, bf16[8,128,128]{2,1,0:T(8,128)(2,1)S(1)} %copy-done.5, f32[384,128]{1,0:T(8,128)S(1)} %get-tuple-element.49.keep, ...), custom_call_target="tpu_custom_call" | custom-call | flops 1000000000 | bytes 2000000 | tf_op jit(solution)/shard_map/adjoint/pallas_call | solution.py:499
  (29 shorter events, 0.3 us)
Async XLA Ops:
  0.6 14.3 %copy-start.8 = (s32[64]{0:T(128)S(1)}, s32[64]{0:T(128)}, u32[]{:S(2)}) copy-start(s32[64]{0:T(128)} %param.10) | copy-start | bytes 772
  0.7 14.4 %copy-start.2 = (bf16[64,16384]{1,0:T(8,128)(2,1)S(1)}, bf16[64,16384]{1,0:T(8,128)(2,1)}, u32[]{:S(2)}) copy-start(bf16[64,16384]{1,0:T(8,128)(2,1)} %images) | copy-start | bytes 6291460
  0.7 14.4 %copy-start.4 = (f32[8,8192]{1,0:T(8,128)S(1)}, f32[8,8192]{1,0:T(8,128)}, u32[]{:S(2)}) copy-start(f32[8,8192]{1,0:T(8,128)} %ctf.1) | copy-start | bytes 786436
  1.4 13.7 %copy-start.1 = (s32[4]{0:T(128)S(1)}, s32[4]{0:T(128)}, u32[]{:S(2)}) copy-start(s32[4]{0:T(128)} %pad_add_fusion.meta) | copy-start | bytes 52
  5.7 25.2 %copy-start.6 = (s32[4096,1]{0,1:T(1,128)S(1)}, s32[4096,1]{0,1:T(1,128)}, u32[]{:S(2)}) copy-start(s32[4096,1]{0,1:T(1,128)} %param.13) | copy-start | bytes 49156
  5.7 1.7 %collective-permute-start = (bf16[384,128]{1,0:T(8,128)(2,1)}, bf16[384,128]{1,0:T(8,128)(2,1)S(1)}, u32[]{:S(2)}, u32[]{:S(2)}) collective-permute-start(bf16[384,128]{1,0:T(8,128)(2,1)} %get-tuple-element.27), channel_id=1, source_target_pairs={{0,1},{1,0},{2,3},{3,2},{4,5},{5,4},{6,7},{7,6},{8,9},{9,8},{10,11... | collective-permute-start | bytes 294920 | tf_op jit(solution)/shard_map/ppermute | solution.py:360
  7.4 11.1 %collective-permute-start.1 = (bf16[768,128]{1,0:T(8,128)(2,1)S(1)}, bf16[768,128]{1,0:T(8,128)(2,1)S(1)}, u32[]{:S(2)}, u32[]{:S(2)}) collective-permute-start(bf16[768,128]{1,0:T(8,128)(2,1)S(1)} %constant_dynamic-update-slice_fusion.rest_0_), channel_id=1, source_target_pairs={{0,12},{1,13},{2,14},{3,15},{4,0},{5,1},{6,2},{7,3},{8,4},{9,5},{1... | collective-permute-start | bytes 589832 | tf_op jit(solution)/shard_map/ppermute | solution.py:360
  12.4 10.5 %collective-permute-start.6 = (bf16[768,128]{1,0:T(8,128)(2,1)S(1)}, bf16[768,128]{1,0:T(8,128)(2,1)S(1)}, u32[]{:S(2)}, u32[]{:S(2)}) collective-permute-start(bf16[768,128]{1,0:T(8,128)(2,1)S(1)} %constant_dynamic-update-slice_fusion.rest_0_), channel_id=1, source_target_pairs={{0,4},{1,5},{2,6},{3,7},{4,8},{5,9},{6,10},{7,11},{8,12},{9,13},{1... | collective-permute-start | bytes 589832 | tf_op jit(solution)/shard_map/ppermute | solution.py:360
  12.4 17.0 %collective-permute-start.8 = (bf16[768,128]{1,0:T(8,128)(2,1)S(1)}, bf16[768,128]{1,0:T(8,128)(2,1)S(1)}, u32[]{:S(2)}, u32[]{:S(2)}) collective-permute-start(bf16[768,128]{1,0:T(8,128)(2,1)S(1)} %constant_dynamic-update-slice_fusion.rest_0_), channel_id=1, source_target_pairs={{0,8},{1,9},{2,10},{3,11},{4,12},{5,13},{6,14},{7,15},{8,0},{9,1},... | collective-permute-start | bytes 589832 | tf_op jit(solution)/shard_map/ppermute | solution.py:360
  13.4 21.6 %collective-permute-start.4 = (bf16[768,128]{1,0:T(8,128)(2,1)S(1)}, bf16[768,128]{1,0:T(8,128)(2,1)S(1)}, u32[]{:S(2)}, u32[]{:S(2)}) collective-permute-start(bf16[768,128]{1,0:T(8,128)(2,1)S(1)} %constant_dynamic-update-slice_fusion.rest_0_), channel_id=1, source_target_pairs={{0,2},{1,3},{2,0},{3,1},{4,6},{5,7},{6,4},{7,5},{8,10},{9,11},{10,... | collective-permute-start | bytes 589832 | tf_op jit(solution)/shard_map/ppermute | solution.py:360
  15.0 2.9 %collective-permute-start.2 = (f32[1,64]{1,0:T(1,128)S(1)}, f32[1,64]{1,0:T(1,128)S(1)}, u32[]{:S(2)}, u32[]{:S(2)}) collective-permute-start(f32[1,64]{1,0:T(1,128)S(1)} %convert_bitcast_fusion.2), channel_id=1, source_target_pairs={{0,1},{1,0},{2,3},{3,2},{4,5},{5,4},{6,7},{7,6},{8,9},{9,8},{10,11... | collective-permute-start | bytes 776 | tf_op jit(solution)/shard_map/ppermute | solution.py:360
  17.9 15.1 %copy-start.7 = (s32[9,2]{0,1:T(2,128)S(1)}, s32[9,2]{0,1:T(2,128)}, u32[]{:S(2)}) copy-start(s32[9,2]{0,1:T(2,128)} %param.11) | copy-start | bytes 220
  17.9 17.6 %collective-permute-start.3 = (bf16[64,8192]{1,0:T(8,128)(2,1)S(1)}, bf16[64,8192]{1,0:T(8,128)(2,1)S(1)}, u32[]{:S(2)}, u32[]{:S(2)}) collective-permute-start(bf16[64,8192]{1,0:T(8,128)(2,1)S(1)} %get-tuple-element.33), channel_id=1, source_target_pairs={{0,1},{1,0},{2,3},{3,2},{4,5},{5,4},{6,7},{7,6},{8,9},{9,8},{10,11... | collective-permute-start | bytes 3145736 | tf_op jit(solution)/shard_map/ppermute | solution.py:360
  18.5 16.5 %collective-permute-start.5 = (bf16[768,128]{1,0:T(8,128)(2,1)S(1)}, bf16[768,128]{1,0:T(8,128)(2,1)S(1)}, u32[]{:S(2)}, u32[]{:S(2)}) collective-permute-start(bf16[768,128]{1,0:T(8,128)(2,1)S(1)} %collective-permute-done.1.rest_2_), channel_id=1, source_target_pairs={{0,2},{1,3},{2,0},{3,1},{4,6},{5,7},{6,4},{7,5},{8,10},{9,11},{10,... | collective-permute-start | bytes 589832 | tf_op jit(solution)/shard_map/ppermute | solution.py:360
  22.9 12.2 %collective-permute-start.7 = (bf16[768,128]{1,0:T(8,128)(2,1)S(1)}, bf16[768,128]{1,0:T(8,128)(2,1)S(1)}, u32[]{:S(2)}, u32[]{:S(2)}) collective-permute-start(bf16[768,128]{1,0:T(8,128)(2,1)S(1)} %collective-permute-done.6.rest_4_), channel_id=1, source_target_pairs={{0,2},{1,3},{2,0},{3,1},{4,6},{5,7},{6,4},{7,5},{8,10},{9,11},{10,... | collective-permute-start | bytes 589832 | tf_op jit(solution)/shard_map/ppermute | solution.py:360
  29.4 6.1 %collective-permute-start.9 = (bf16[768,128]{1,0:T(8,128)(2,1)S(1)}, bf16[768,128]{1,0:T(8,128)(2,1)S(1)}, u32[]{:S(2)}, u32[]{:S(2)}) collective-permute-start(bf16[768,128]{1,0:T(8,128)(2,1)S(1)} %collective-permute-done.8.rest_6_), channel_id=1, source_target_pairs={{0,2},{1,3},{2,0},{3,1},{4,6},{5,7},{6,4},{7,5},{8,10},{9,11},{10,... | collective-permute-start | bytes 589832 | tf_op jit(solution)/shard_map/ppermute | solution.py:360
  43.8 14.4 %copy-start = (f32[384,8]{1,0:T(8,128)S(1)}, f32[384,8]{1,0:T(8,128)}, u32[]{:S(2)}) copy-start(f32[384,8]{1,0:T(8,128)} %get-tuple-element.25.slots) | copy-start | bytes 36868
  43.8 1.6 %collective-permute-start.10 = (f32[576,128]{1,0:T(8,128)S(1)}, f32[576,128]{1,0:T(8,128)S(1)}, u32[]{:S(2)}, u32[]{:S(2)}) collective-permute-start(f32[576,128]{1,0:T(8,128)S(1)} %score.1.mine), channel_id=1, source_target_pairs={{0,1},{1,0},{2,3},{3,2},{4,5},{5,4},{6,7},{7,6},{8,9},{9,8},{10,11... | collective-permute-start | bytes 884744 | tf_op jit(solution)/shard_map/ppermute | solution.py:360
  54.1 7.0 %collective-permute-start.18 = (bf16[256,128]{1,0:T(8,128)(2,1)S(1)}, bf16[256,128]{1,0:T(8,128)(2,1)S(1)}, u32[]{:S(2)}, u32[]{:S(2)}) collective-permute-start(bf16[256,128]{1,0:T(8,128)(2,1)S(1)} %get-tuple-element.44), channel_id=1, source_target_pairs={{0,8},{1,9},{2,10},{3,11},{4,12},{5,13},{6,14},{7,15},{8,0},{9,1},... | collective-permute-start | bytes 196616 | tf_op jit(solution)/shard_map/ppermute | solution.py:360
  54.3 7.9 %collective-permute-start.19 = (bf16[256,128]{1,0:T(8,128)(2,1)S(1)}, bf16[256,128]{1,0:T(8,128)(2,1)S(1)}, u32[]{:S(2)}, u32[]{:S(2)}) collective-permute-start(bf16[256,128]{1,0:T(8,128)(2,1)S(1)} %get-tuple-element.45), channel_id=1, source_target_pairs={{0,12},{1,13},{2,14},{3,15},{4,0},{5,1},{6,2},{7,3},{8,4},{9,5},{1... | collective-permute-start | bytes 196616 | tf_op jit(solution)/shard_map/ppermute | solution.py:360
  58.2 6.1 %collective-permute-start.20 = (bf16[256,128]{1,0:T(8,128)(2,1)S(1)}, bf16[256,128]{1,0:T(8,128)(2,1)S(1)}, u32[]{:S(2)}, u32[]{:S(2)}) collective-permute-start(bf16[256,128]{1,0:T(8,128)(2,1)S(1)} %get-tuple-element.46), channel_id=1, source_target_pairs={{0,4},{1,5},{2,6},{3,7},{4,8},{5,9},{6,10},{7,11},{8,12},{9,13},{1... | collective-permute-start | bytes 196616 | tf_op jit(solution)/shard_map/ppermute | solution.py:360
  58.2 7.2 %collective-permute-start.12 = (bf16[640,128]{1,0:T(8,128)(2,1)S(1)}, bf16[640,128]{1,0:T(8,128)(2,1)S(1)}, u32[]{:S(2)}, u32[]{:S(2)}) collective-permute-start(bf16[640,128]{1,0:T(8,128)(2,1)S(1)} %get-tuple-element.38), channel_id=1, source_target_pairs={{0,2},{1,3},{2,0},{3,1},{4,6},{5,7},{6,4},{7,5},{8,10},{9,11},{10,... | collective-permute-start | bytes 491528 | tf_op jit(solution)/shard_map/ppermute | solution.py:360
  58.8 10.1 %collective-permute-start.14 = (bf16[640,128]{1,0:T(8,128)(2,1)S(1)}, bf16[640,128]{1,0:T(8,128)(2,1)S(1)}, u32[]{:S(2)}, u32[]{:S(2)}) collective-permute-start(bf16[640,128]{1,0:T(8,128)(2,1)S(1)} %get-tuple-element.40), channel_id=1, source_target_pairs={{0,2},{1,3},{2,0},{3,1},{4,6},{5,7},{6,4},{7,5},{8,10},{9,11},{10,... | collective-permute-start | bytes 491528 | tf_op jit(solution)/shard_map/ppermute | solution.py:360
  61.1 11.7 %collective-permute-start.16 = (bf16[640,128]{1,0:T(8,128)(2,1)S(1)}, bf16[640,128]{1,0:T(8,128)(2,1)S(1)}, u32[]{:S(2)}, u32[]{:S(2)}) collective-permute-start(bf16[640,128]{1,0:T(8,128)(2,1)S(1)} %get-tuple-element.42), channel_id=1, source_target_pairs={{0,2},{1,3},{2,0},{3,1},{4,6},{5,7},{6,4},{7,5},{8,10},{9,11},{10,... | collective-permute-start | bytes 491528 | tf_op jit(solution)/shard_map/ppermute | solution.py:360
  62.3 12.9 %collective-permute-start.11 = (bf16[640,128]{1,0:T(8,128)(2,1)S(1)}, bf16[640,128]{1,0:T(8,128)(2,1)S(1)}, u32[]{:S(2)}, u32[]{:S(2)}) collective-permute-start(bf16[640,128]{1,0:T(8,128)(2,1)S(1)} %get-tuple-element.36), channel_id=1, source_target_pairs={{0,2},{1,3},{2,0},{3,1},{4,6},{5,7},{6,4},{7,5},{8,10},{9,11},{10,... | collective-permute-start | bytes 491528 | tf_op jit(solution)/shard_map/ppermute | solution.py:360
  64.2 17.6 %copy-start.3 = (bf16[1024,256]{1,0:T(8,128)(2,1)S(1)}, bf16[1024,256]{1,0:T(8,128)(2,1)}, u32[]{:S(2)}) copy-start(bf16[1024,256]{1,0:T(8,128)(2,1)} %volume.1) | copy-start | bytes 1572868
  64.2 17.6 %copy-start.5 = (bf16[8,128,128]{2,1,0:T(8,128)(2,1)S(1)}, bf16[8,128,128]{2,1,0:T(8,128)(2,1)}, u32[]{:S(2)}) copy-start(bf16[8,128,128]{2,1,0:T(8,128)(2,1)} %interp.1) | copy-start | bytes 786436
  64.3 10.9 %collective-permute-start.21 = (bf16[128,128]{1,0:T(8,128)(2,1)S(1)}, bf16[128,128]{1,0:T(8,128)(2,1)S(1)}, u32[]{:S(2)}, u32[]{:S(2)}) collective-permute-start(bf16[128,128]{1,0:T(8,128)(2,1)S(1)} %slice.36), channel_id=1, source_target_pairs={{0,2},{1,3},{2,0},{3,1},{4,6},{5,7},{6,4},{7,5},{8,10},{9,11},{10,... | collective-permute-start | bytes 98312 | tf_op jit(solution)/shard_map/ppermute | solution.py:360
  65.5 11.4 %collective-permute-start.13 = (bf16[640,128]{1,0:T(8,128)(2,1)S(1)}, bf16[640,128]{1,0:T(8,128)(2,1)S(1)}, u32[]{:S(2)}, u32[]{:S(2)}) collective-permute-start(bf16[640,128]{1,0:T(8,128)(2,1)S(1)} %add_convert_fusion.2), channel_id=1, source_target_pairs={{0,8},{1,9},{2,10},{3,11},{4,12},{5,13},{6,14},{7,15},{8,0},{9,1},... | collective-permute-start | bytes 491528 | tf_op jit(solution)/shard_map/ppermute | solution.py:360
  69.0 7.9 %collective-permute-start.15 = (bf16[640,128]{1,0:T(8,128)(2,1)S(1)}, bf16[640,128]{1,0:T(8,128)(2,1)S(1)}, u32[]{:S(2)}, u32[]{:S(2)}) collective-permute-start(bf16[640,128]{1,0:T(8,128)(2,1)S(1)} %add_convert_fusion.1), channel_id=1, source_target_pairs={{0,12},{1,13},{2,14},{3,15},{4,0},{5,1},{6,2},{7,3},{8,4},{9,5},{1... | collective-permute-start | bytes 491528 | tf_op jit(solution)/shard_map/ppermute | solution.py:360
  72.9 7.3 %collective-permute-start.17 = (bf16[640,128]{1,0:T(8,128)(2,1)S(1)}, bf16[640,128]{1,0:T(8,128)(2,1)S(1)}, u32[]{:S(2)}, u32[]{:S(2)}) collective-permute-start(bf16[640,128]{1,0:T(8,128)(2,1)S(1)} %add_convert_fusion), channel_id=1, source_target_pairs={{0,4},{1,5},{2,6},{3,7},{4,8},{5,9},{6,10},{7,11},{8,12},{9,13},{1... | collective-permute-start | bytes 491528 | tf_op jit(solution)/shard_map/ppermute | solution.py:360
  80.3 1.5 %collective-permute-start.22 = (f32[384,128]{1,0:T(8,128)S(1)}, f32[384,128]{1,0:T(8,128)S(1)}, u32[]{:S(2)}, u32[]{:S(2)}) collective-permute-start(f32[384,128]{1,0:T(8,128)S(1)} %get-tuple-element.48), channel_id=1, source_target_pairs={{0,1},{1,0},{2,3},{3,2},{4,5},{5,4},{6,7},{7,6},{8,9},{9,8},{10,11... | collective-permute-start | bytes 589832 | tf_op jit(solution)/shard_map/ppermute | solution.py:360

commit v4 on v3

--- a/solution.py
+++ b/solution.py
@@ -47,8 +47,13 @@
     return upper, jnp.ones((BW, BW), BF16), lower
 
 
-def target_kernel(devices, ny, nz, cap, meta, owner, target):
-    z, y, core = meta[1], meta[2], meta[3]
+def position(ny):
+    me = lax.axis_index("img")
+    return me, lax.shift_right_logical(me, ny.bit_length()), lax.shift_right_logical(me, 1) & (ny - 1), me & 1
+
+
+def target_kernel(devices, ny, nz, cap, owner, target):
+    _, z, y, core = position(ny)
     own = owner[...]
     upper, ones, lower = triangles(own.shape[0])
 
@@ -67,10 +72,13 @@
     rel_core = (own & 1) ^ core
     rel_y = (lax.shift_right_logical(own, 1) - y) & (ny - 1)
     rel_z = (lax.shift_right_logical(own, ny.bit_length()) - z) & (nz - 1)
-    target[...] = ((rel_z * ny + rel_y) * 2 + rel_core) * cap + pos.astype(jnp.int32)
-
-
-def slice_kernel(meta, *refs):
+    place = ((rel_z * ny + rel_y) * 2 + rel_core) * cap + pos.astype(jnp.int32)
+    ref = 2 * iota(own.shape, 0) + jnp.where(iota(own.shape, 1) < KB, 0, 1)
+    place = place + 8 - (ref & 7)
+    target[...] = place + pltpu.roll(place, KB, 1) * 65536
+
+
+def slice_kernel(*refs):
     sources, (slots, keep, send), held, arrived = refs[:5], refs[5:8], refs[8:13], refs[13]
     copies = [
         pltpu.make_async_copy(source, place, arrived.at[i])
@@ -79,7 +87,8 @@
     for copy in copies:
         copy.start()
     owner, local, table, volume, interp = held
-    me, core = meta[0], meta[3]
+    me = lax.axis_index("img")
+    core = me & 1
     cap = keep.shape[0]
     for copy in copies[:3]:
         copy.wait()
@@ -130,8 +139,8 @@
     send[...] = jnp.where(core == 0, right, left).astype(BF16)
 
 
-def weigh_kernel(meta, images, group, ctf, keep, send, squares):
-    core = meta[3]
+def weigh_kernel(images, group, ctf, keep, send, squares):
+    core = lax.axis_index("img") & 1
     count = images.shape[0]
     groups = ctf.shape[0]
     number = jnp.broadcast_to(group[...], (count, BW))
@@ -158,6 +167,11 @@
     lax.fori_loop(0, KB, body, 0, unroll=8)
 
 
+def rows_of(target, r, b):
+    both = target[(r // 2) * BW + b]
+    return both & 65535, lax.shift_right_logical(both, 16)
+
+
 def score_kernel(
     places, target, group, cosine, sine, keep, other, squares, *rest
 ):
@@ -177,10 +191,10 @@
 
     def fetch(b, first):
         value = None
-        for k in range(8):
-            row = target[(first + k) * KB + b]
-            loaded = gathered[pl.ds(row - k + 8, 8), :]
-            value = loaded if k == 0 else jnp.where(sublane == k, loaded, value)
+        for r in range(first, first + 8, 2):
+            for i, row in enumerate(rows_of(target, r, b)):
+                loaded = gathered[pl.ds(row, 8), :]
+                value = loaded if value is None else jnp.where(sublane == r + i - first, loaded, value)
         return value
 
     def gather(step, block):
@@ -231,11 +245,9 @@
         scores[s * R : (s + 1) * R, :] -= 0.5 * norm
 
 
-def back_kernel(ny, nz, rows, first, target, mine, theirs, cosine, sine, keep, other, *rest):
+def back_kernel(ny, rows, order, target, mine, theirs, cosine, sine, keep, other, *rest):
     evidence = rest[0]
-    parts = rest[1 : 1 + ny * nz]
-    by_z = rest[1 + ny * nz : 1 + ny * nz + nz]
-    (placed,) = rest[1 + ny * nz + nz :]
+    placed = rest[-1]
     shifts = cosine.shape[1]
     scale = 1.0 / math.sqrt(KB * BW)
     placed[...] = jnp.zeros(placed.shape, F32)
@@ -260,29 +272,25 @@
                 straight = straight + term * cosine[b, s : s + 1, :]
                 crossed = crossed + term * sine[b, s : s + 1, :]
             value = straight + swap_halves(crossed)
-            for r in range(R):
-                k = r % 8
-                row = target[r * KB + b]
-                pltpu.store(
-                    placed.at[pl.ds(row + (8 - k), 8), :],
-                    value[r - k : r - k + 8],
-                    mask=sublane == k,
-                )
+            for r in range(0, R, 2):
+                for i, row in enumerate(rows_of(target, r, b)):
+                    k = (r + i) % 8
+                    pltpu.store(
+                        placed.at[pl.ds(row, 8), :],
+                        value[r + i - k : r + i - k + 8],
+                        mask=sublane == k,
+                    )
         return carry
 
     lax.fori_loop(0, KB // 2, body, 0, unroll=4)
-    later = rows - first
-    for kz in range(nz):
+    for i, kz in enumerate(order):
         for ky in range(ny):
             start = (kz * ny + ky) * rows + 8
-            parts[kz * ny + ky][...] = placed[start : start + first, :].astype(BF16)
-            by_z[kz][ky * later : (ky + 1) * later, :] = placed[
-                start + first : start + rows, :
-            ].astype(BF16)
-
-
-def adjoint_kernel(meta, place, slots, volume, interp, keep, other, new_map):
-    core = meta[3]
+            rest[1 + i * ny + ky][...] = placed[start : start + rows, :].astype(BF16)
+
+
+def adjoint_kernel(place, slots, volume, interp, keep, other, new_map):
+    core = lax.axis_index("img") & 1
     cap = keep.shape[0]
     mine, theirs = keep[...], other[...]
     left = jnp.where(core == 0, mine, theirs)
@@ -335,9 +343,6 @@
     nz = chips // ny
     me = lax.axis_index("img")
     core = me % 2
-    y = (me // 2) % ny
-    z = me // (2 * ny)
-    meta = jnp.stack([me, z, y, core]).astype(jnp.int32)
     cap = max(2, 3 * BLOCKS // (2 * devices))
     rows = 2 * cap
     count = images.shape[0]
@@ -363,7 +368,7 @@
     owner = owner.reshape(wide)
     slots, slice_keep, slice_send = call(
         slice_kernel,
-        [SMEM] + [ANY] * 5,
+        [ANY] * 5,
         [struct((cap, 8), F32), struct((cap, BW), BF16), struct((cap, BW), BF16)],
         [pltpu.VMEM(wide, jnp.int32)] * 3
         + [
@@ -375,12 +380,10 @@
         10**6,
         "own_slices",
         60,
-    )(meta, owner, local.reshape(wide), table_id.reshape(wide), volume, interp)
+    )(owner, local.reshape(wide), table_id.reshape(wide), volume, interp)
     own_piece = jnp.concatenate([slice_keep, to(slice_send, core_pairs)], axis=0)
     images, groups, _ = lax.optimization_barrier((images, groups, own_piece))
 
-    later = max(16, rows // 6 // 16 * 16)
-    first = rows - later
     near = sorted(range(1, nz), key=lambda k: min(k, nz - k))
     pieces = [(own_piece, [(0, rows, 0)])]
     by_z = {kz: to(own_piece, along_z(-kz)) for kz in near}
@@ -396,18 +399,18 @@
     owner, shifts, _ = lax.optimization_barrier((owner, shifts, by_z[near[0]]))
     (target,) = call(
         functools.partial(target_kernel, devices, ny, nz, cap),
-        [SMEM, VMEM],
+        [VMEM],
         [struct(wide, jnp.int32)],
         [],
         10**9,
         10**6,
         "target",
-    )(meta, owner)
+    )(owner)
     target = target.reshape(BLOCKS)
 
     weight_keep, weight_send, squares = call(
         weigh_kernel,
-        [SMEM] + [VMEM] * 3,
+        [VMEM] * 3,
         [
             struct((count, KB * BW), BF16),
             struct((count, KB * BW), BF16),
@@ -417,7 +420,7 @@
         10**9,
         4 * 10**6,
         "weigh",
-    )(meta, images, groups.reshape(count, 1), ctf)
+    )(images, groups.reshape(count, 1), ctf)
     weight_other = to(weight_send, core_pairs)
     group_row = groups.astype(F32).reshape(1, count)
     group_row = jnp.concatenate([group_row, to(group_row, core_pairs)], axis=1).astype(jnp.int32)
@@ -457,54 +460,40 @@
     )(target, group_row, cosine, sine, weight_keep, weight_other, squares, *[piece for piece, _ in pieces])
 
     theirs = to(partial, core_pairs)
+    order = near[::-1] + [0]
     outs = call(
-        functools.partial(back_kernel, ny, nz, rows, first),
+        functools.partial(back_kernel, ny, rows, order),
         [SMEM] + [VMEM] * 6,
         [struct((1, 2 * count), F32)]
-        + [struct((first, BW), BF16)] * chips
-        + [struct((ny * later, BW), BF16)] * nz,
+        + [struct((rows, BW), BF16)] * chips,
         [pltpu.VMEM((chips * rows + 16, BW), F32)],
         4 * 10**9,
         10**7,
         "back",
     )(target, partial, theirs, cosine, sine, weight_keep, weight_other)
     evidence = outs[0][0, :count]
-    parts, by_z = outs[1 : 1 + chips], outs[1 + chips :]
-
-    far = near[::-1]
+    parts = {kz: outs[1 + ny * i : 1 + ny * (i + 1)] for i, kz in enumerate(order)}
+    moved = {kz: [to(parts[kz][ky], along_y(ky)) for ky in range(1, ny)] for kz in order}
     summed = {}
-    from_y = {}
-    for kz in far + [0]:
-        from_y[kz] = [to(parts[kz * ny + ky], along_y(ky)) for ky in range(1, ny)]
-    from_z = [to(by_z[kz], along_z(kz)) for kz in far]
-    for kz in far + [0]:
-        summed[kz] = parts[kz * ny].astype(F32)
-        for part in from_y[kz]:
+    for kz in order:
+        summed[kz] = parts[kz][0].astype(F32)
+        for part in moved[kz]:
             summed[kz] = summed[kz] + part.astype(F32)
-    final_first = summed[0]
-    for kz in far:
-        final_first = final_first + to(summed[kz].astype(BF16), along_z(kz)).astype(F32)
-    summed_z = by_z[0].astype(F32)
-    for part in from_z:
-        summed_z = summed_z + part.astype(F32)
-    packed_z = summed_z.astype(BF16)
-    final_later = summed_z[:later]
-    for ky in range(1, ny):
-        part = to(packed_z[ky * later : (ky + 1) * later], along_y(ky))
-        final_later = final_later + part.astype(F32)
-    final = jnp.concatenate([final_first, final_later], axis=0)
+    final = summed[0]
+    for kz in near[::-1]:
+        final = final + to(summed[kz].astype(BF16), along_z(kz)).astype(F32)
     sum_keep = final[:cap]
     sum_other = to(final[cap:], core_pairs)
 
     (new_map,) = call(
         adjoint_kernel,
-        [SMEM] + [VMEM] * 6,
+        [VMEM] * 6,
         [struct(volume.shape, F32)],
         [],
         10**9,
         2 * 10**6,
         "adjoint",
-    )(meta, place, slots, volume, interp, sum_keep, sum_other)
+    )(place, slots, volume, interp, sum_keep, sum_other)
     return (new_map, evidence)
 
 

time: 86 us -> 82.3 us (0.957)
  waiting for transfers between devices: 23.3 us -> 29.6 us
  starting transfers between devices: 26.8 us -> 20.8 us
  Pallas kernels: 29.9 us -> 26.9 us
    ppermute x23 -> x19, waiting for transfers between devices: 23.3 us -> 29.6 us  [to(): return lax.ppermute(array, 'img', pairs)]
    ppermute x23 -> x19, starting transfers between devices: 26.8 us -> 20.8 us  [to(): return lax.ppermute(array, 'img', pairs)]
    pallas_call x5, Pallas kernels: 21.6 us -> 18.6 us  [the longest x1 7.89 us: per_device(): call(functools.partial(back_kernel, ny, rows, order), [SMEM] + [VMEM] * 6...]
  transfers between devices with their start and end apart: 23 -> 19, of which waited for: 13 -> 11; matrix products, arithmetic and copies ran while one was open for 5% -> 5% of each run, Pallas kernels for 6% -> 4%
where the time goes in v4:
time: 82.3 us; the launch traced here: 82.2 us
  waiting for transfers between devices  29.6 us (36%)
  Pallas kernels  26.9 us (33%)
  starting transfers between devices  20.8 us (25%)
  other arithmetic  2.44 us (3%)
  local copies, waits for them, and re-layouts  1.67 us (2%)
  between operations  0.87 us (1%)
    ppermute x19, waiting for transfers between devices, to(): return lax.ppermute(array, 'img', pairs)  29.6 us
    ppermute x19, starting transfers between devices, to(): return lax.ppermute(array, 'img', pairs)  20.8 us
    pallas_call x1, Pallas kernels, per_device(): call(functools.partial(score_kernel, [moves for _, moves in pieces]), [SM...  8.28 us
    pallas_call x1, Pallas kernels, per_device(): call(functools.partial(back_kernel, ny, rows, order), [SMEM] + [VMEM] * 6...  7.89 us
    pallas_call x1, Pallas kernels, per_device(): call(slice_kernel, [ANY] * 5, [struct((cap, 8), F32), struct((cap, BW), B...  3.67 us
    pallas_call x1, Pallas kernels, per_device(): call(adjoint_kernel, [VMEM] * 6, [struct(volume.shape, F32)], [], 10 ** 9...  3.33 us
    pallas_call x1, Pallas kernels, per_device(): call(weigh_kernel, [VMEM] * 3, [struct((count, KB * BW), BF16), struct((c...  2.12 us
    mul x1, other arithmetic, per_device(): sine = jnp.sin(angles) * jnp.where(lane < HALF, -1.0, 1.0)  1.92 us
  transfers between devices with their start and end apart: 19, of which 11 were waited for; matrix products, arithmetic and copies ran while one was open for 5% of the time, Pallas kernels for 4%

profile of v4, /device:TPU:0, one launch (start us, length us, event | category | flops | bytes accessed | tf_op | source)
XLA Modules:
  0.0 82.2 jit_solution(15084702555474788172)
XLA Ops:
  0.6 0.0 copy-start.7
  0.6 0.0 copy-start.1
  0.7 0.0 copy-start.3
  0.7 3.7 %own_slices.1 = (f32[384,8]{1,0:T(8,128)}, bf16[384,128]{1,0:T(8,128)(2,1)}, bf16[384,128]{1,0:T(8,128)(2,1)}) custom-call(s32[32,128]{1,0:T(8,128)} %bitcast.15, s32[32,128]{1,0:T(8,128)} %bitcast.20, s32[32,128]{1,0:T(8,128)} %bitcast.21, bf16[1024,256]{1,0:T(8,128)(2,1)} %volume.1, bf16[8,128,128]{2,1,0:T(8,128)(2,1)} %interp.1), custom_call_target="tpu_custom_call" | custom-call | flops 1000000000 | bytes 1000000 | tf_op jit(solution)/shard_map/own_slices/pallas_call | solution.py:369
  4.3 0.0 copy-start.5
  4.3 0.5 collective-permute-start
  4.9 0.9 %constant_dynamic-update-slice_fusion.1 = bf16[768,128]{1,0:T(8,128)(2,1)S(1)} fusion(bf16[384,128]{1,0:T(8,128)(2,1)} %get-tuple-element.22), kind=kLoop, calls=%fused_computation.9 | loop fusion | bytes 196608
  5.8 0.2 collective-permute-done
  6.0 5.0 %collective-permute-start.1 = (bf16[768,128]{1,0:T(8,128)(2,1)S(1)}, bf16[768,128]{1,0:T(8,128)(2,1)S(1)}, u32[]{:S(2)}, u32[]{:S(2)}) collective-permute-start(bf16[768,128]{1,0:T(8,128)(2,1)S(1)} %constant_dynamic-update-slice_fusion.rest_0_), channel_id=1, source_target_pairs={{0,12},{1,13},{2,14},{3,15},{4,0},{5,1},{6,2},{7,3},{8,4},{9,5},{1... | collective-permute-start | bytes 589832 | tf_op jit(solution)/shard_map/ppermute | solution.py:365
  11.1 0.0 collective-permute-start.6
  11.1 1.0 %collective-permute-start.8 = (bf16[768,128]{1,0:T(8,128)(2,1)S(1)}, bf16[768,128]{1,0:T(8,128)(2,1)S(1)}, u32[]{:S(2)}, u32[]{:S(2)}) collective-permute-start(bf16[768,128]{1,0:T(8,128)(2,1)S(1)} %constant_dynamic-update-slice_fusion.rest_0_), channel_id=1, source_target_pairs={{0,8},{1,9},{2,10},{3,11},{4,12},{5,13},{6,14},{7,15},{8,0},{9,1},... | collective-permute-start | bytes 589832 | tf_op jit(solution)/shard_map/ppermute | solution.py:365
  12.1 1.5 %collective-permute-start.4 = (bf16[768,128]{1,0:T(8,128)(2,1)S(1)}, bf16[768,128]{1,0:T(8,128)(2,1)S(1)}, u32[]{:S(2)}, u32[]{:S(2)}) collective-permute-start(bf16[768,128]{1,0:T(8,128)(2,1)S(1)} %constant_dynamic-update-slice_fusion.rest_0_), channel_id=1, source_target_pairs={{0,2},{1,3},{2,0},{3,1},{4,6},{5,7},{6,4},{7,5},{8,10},{9,11},{10,... | collective-permute-start | bytes 589832 | tf_op jit(solution)/shard_map/ppermute | solution.py:365
  13.6 0.1 copy.12.group
  13.7 0.0 collective-permute-start.2
  13.7 2.1 %weigh.1 = (bf16[64,8192]{1,0:T(8,128)(2,1)S(1)}, bf16[64,8192]{1,0:T(8,128)(2,1)S(1)}, bf16[16,8192]{1,0:T(8,128)(2,1)S(1)}) custom-call(bf16[64,16384]{1,0:T(8,128)(2,1)S(1)} %copy-done.1, s32[64,1]{1,0:T(8,128)S(1)} %copy.12.group, f32[8,8192]{1,0:T(8,128)S(1)} %copy-done.3), custom_call_target="tpu_custom_call" | custom-call | flops 1000000000 | bytes 4000000 | tf_op jit(solution)/shard_map/weigh/pallas_call | solution.py:411
  15.9 0.0 copy-start.6
  15.9 0.0 collective-permute-done.2
  15.9 0.5 collective-permute-start.3
  16.4 0.1 maximum_convert_fusion.group
  16.5 0.0 collective-permute-done.1.rest_2_
  16.5 1.4 %collective-permute-start.5 = (bf16[768,128]{1,0:T(8,128)(2,1)S(1)}, bf16[768,128]{1,0:T(8,128)(2,1)S(1)}, u32[]{:S(2)}, u32[]{:S(2)}) collective-permute-start(bf16[768,128]{1,0:T(8,128)(2,1)S(1)} %collective-permute-done.1.rest_2_), channel_id=1, source_target_pairs={{0,2},{1,3},{2,0},{3,1},{4,6},{5,7},{6,4},{7,5},{8,10},{9,11},{10,... | collective-permute-start | bytes 589832 | tf_op jit(solution)/shard_map/ppermute | solution.py:365
  17.9 3.7 %collective-permute-done.6.rest_4_ = bf16[768,128]{1,0:T(8,128)(2,1)S(1)} collective-permute-done((bf16[768,128]{1,0:T(8,128)(2,1)S(1)}, bf16[768,128]{1,0:T(8,128)(2,1)S(1)}, u32[]{:S(2)}, u32[]{:S(2)}) %collective-permute-start.6) | collective-permute-done | bytes 196640 | tf_op jit(solution)/shard_map/ppermute | solution.py:365
  21.5 1.5 %collective-permute-start.7 = (bf16[768,128]{1,0:T(8,128)(2,1)S(1)}, bf16[768,128]{1,0:T(8,128)(2,1)S(1)}, u32[]{:S(2)}, u32[]{:S(2)}) collective-permute-start(bf16[768,128]{1,0:T(8,128)(2,1)S(1)} %collective-permute-done.6.rest_4_), channel_id=1, source_target_pairs={{0,2},{1,3},{2,0},{3,1},{4,6},{5,7},{6,4},{7,5},{8,10},{9,11},{10,... | collective-permute-start | bytes 589832 | tf_op jit(solution)/shard_map/ppermute | solution.py:365
  23.0 5.0 %collective-permute-done.8.rest_6_ = bf16[768,128]{1,0:T(8,128)(2,1)S(1)} collective-permute-done((bf16[768,128]{1,0:T(8,128)(2,1)S(1)}, bf16[768,128]{1,0:T(8,128)(2,1)S(1)}, u32[]{:S(2)}, u32[]{:S(2)}) %collective-permute-start.8) | collective-permute-done | bytes 196640 | tf_op jit(solution)/shard_map/ppermute | solution.py:365
  28.1 1.5 %collective-permute-start.9 = (bf16[768,128]{1,0:T(8,128)(2,1)S(1)}, bf16[768,128]{1,0:T(8,128)(2,1)S(1)}, u32[]{:S(2)}, u32[]{:S(2)}) collective-permute-start(bf16[768,128]{1,0:T(8,128)(2,1)S(1)} %collective-permute-done.8.rest_6_), channel_id=1, source_target_pairs={{0,2},{1,3},{2,0},{3,1},{4,6},{5,7},{6,4},{7,5},{8,10},{9,11},{10,... | collective-permute-start | bytes 589832 | tf_op jit(solution)/shard_map/ppermute | solution.py:365
  29.6 1.6 %target.1 = s32[32,128]{1,0:T(8,128)S(1)} custom-call(s32[32,128]{1,0:T(8,128)S(1)} %bitcast.16), custom_call_target="tpu_custom_call" | custom-call | flops 1000000000 | bytes 1000000 | tf_op jit(solution)/shard_map/target/pallas_call | solution.py:400
  31.2 0.1 broadcast_multiply_fusion.1
  31.2 0.1 broadcast_multiply_fusion
  31.3 1.9 %sine_multiply_fusion = (f32[64,9,128]{2,1,0:T(8,128)S(1)}, f32[64,9,128]{2,1,0:T(8,128)S(1)}) fusion(f32[128]{0:T(128)S(1)} %compare_select_fusion, f32[64,9]{1,0:T(8,128)S(1)} %broadcast_multiply_fusion, f32[9,128]{1,0:T(8,128)S(1)} %broadcast_multiply_fusion.1), kind=kLoop, calls=%fused_computation | loop fusion | flops 221184 | bytes 597248 | tf_op jit(solution)/shard_map/mul | solution.py:444
  33.2 0.0 collective-permute-done.4.rest_1_
  33.2 0.0 collective-permute-done.5.rest_3_
  33.3 0.0 collective-permute-done.7.rest_5_
  33.3 0.9 %collective-permute-done.9.rest_7_ = bf16[768,128]{1,0:T(8,128)(2,1)S(1)} collective-permute-done((bf16[768,128]{1,0:T(8,128)(2,1)S(1)}, bf16[768,128]{1,0:T(8,128)(2,1)S(1)}, u32[]{:S(2)}, u32[]{:S(2)}) %collective-permute-start.9) | collective-permute-done | bytes 196640 | tf_op jit(solution)/shard_map/ppermute | solution.py:365
  34.2 0.0 collective-permute-done.3.other
  34.2 8.3 %score.1.mine = f32[576,128]{1,0:T(8,128)S(1)} custom-call(s32[4096]{0:T(1024)S(1)} %bitcast.17, s32[1,128]{1,0:T(1,128)S(1)} %maximum_convert_fusion.group, f32[64,9,128]{2,1,0:T(8,128)S(1)} %get-tuple-element.43.cosine, f32[64,9,128]{2,1,0:T(8,128)S(1)} %get-tuple-element.42.sine, bf16[64,8192]{1,0:T(8,128)(2,1)S(1)} %get-tuple-element.28.keep, ...), custom_call_target="tpu_custom_call" | custom-call | flops 4000000000 | bytes 10000000 | tf_op jit(solution)/shard_map/score/pallas_call | solution.py:446
  42.5 0.0 copy-start
  42.5 0.1 collective-permute-start.10
  42.6 1.6 %collective-permute-done.10.theirs = f32[576,128]{1,0:T(8,128)S(1)} collective-permute-done((f32[576,128]{1,0:T(8,128)S(1)}, f32[576,128]{1,0:T(8,128)S(1)}, u32[]{:S(2)}, u32[]{:S(2)}) %collective-permute-start.10) | collective-permute-done | bytes 294944 | tf_op jit(solution)/shard_map/ppermute | solution.py:365
  44.1 7.9 %back.1 = (f32[1,128]{1,0:T(1,128)S(1)}, bf16[768,128]{1,0:T(8,128)(2,1)S(1)}, bf16[768,128]{1,0:T(8,128)(2,1)S(1)}, bf16[768,128]{1,0:T(8,128)(2,1)S(1)}, bf16[...) custom-call(s32[4096]{0:T(1024)S(1)} %bitcast.18, ...), custom_call_target="tpu_custom_call" | custom-call | flops 4000000000 | bytes 10000000 | tf_op jit(solution)/shard_map/back/pallas_call | solution.py:464
  52.0 0.0 copy-start.2
  52.0 0.0 copy-start.4
  52.1 1.6 %collective-permute-start.12 = (bf16[768,128]{1,0:T(8,128)(2,1)S(1)}, bf16[768,128]{1,0:T(8,128)(2,1)S(1)}, u32[]{:S(2)}, u32[]{:S(2)}) collective-permute-start(bf16[768,128]{1,0:T(8,128)(2,1)S(1)} %get-tuple-element.34), channel_id=1, source_target_pairs={{0,2},{1,3},{2,0},{3,1},{4,6},{5,7},{6,4},{7,5},{8,10},{9,11},{10,... | collective-permute-start | bytes 589832 | tf_op jit(solution)/shard_map/ppermute | solution.py:365
  53.7 0.5 collective-permute-start.14
  54.1 1.5 %collective-permute-start.16 = (bf16[768,128]{1,0:T(8,128)(2,1)S(1)}, bf16[768,128]{1,0:T(8,128)(2,1)S(1)}, u32[]{:S(2)}, u32[]{:S(2)}) collective-permute-start(bf16[768,128]{1,0:T(8,128)(2,1)S(1)} %get-tuple-element.38), channel_id=1, source_target_pairs={{0,2},{1,3},{2,0},{3,1},{4,6},{5,7},{6,4},{7,5},{8,10},{9,11},{10,... | collective-permute-start | bytes 589832 | tf_op jit(solution)/shard_map/ppermute | solution.py:365
  55.7 0.5 collective-permute-start.11
  56.2 3.7 %collective-permute-done.12 = bf16[768,128]{1,0:T(8,128)(2,1)S(1)} collective-permute-done((bf16[768,128]{1,0:T(8,128)(2,1)S(1)}, bf16[768,128]{1,0:T(8,128)(2,1)S(1)}, u32[]{:S(2)}, u32[]{:S(2)}) %collective-permute-start.12) | collective-permute-done | bytes 196640 | tf_op jit(solution)/shard_map/ppermute | solution.py:365
  59.9 0.1 add_convert_fusion.2
  59.9 0.1 collective-permute-start.13
  60.0 4.1 %collective-permute-done.14 = bf16[768,128]{1,0:T(8,128)(2,1)S(1)} collective-permute-done((bf16[768,128]{1,0:T(8,128)(2,1)S(1)}, bf16[768,128]{1,0:T(8,128)(2,1)S(1)}, u32[]{:S(2)}, u32[]{:S(2)}) %collective-permute-start.14) | collective-permute-done | bytes 196640 | tf_op jit(solution)/shard_map/ppermute | solution.py:365
  64.1 0.1 add_convert_fusion.1
  64.1 2.4 %collective-permute-start.15 = (bf16[768,128]{1,0:T(8,128)(2,1)S(1)}, bf16[768,128]{1,0:T(8,128)(2,1)S(1)}, u32[]{:S(2)}, u32[]{:S(2)}) collective-permute-start(bf16[768,128]{1,0:T(8,128)(2,1)S(1)} %add_convert_fusion.1), channel_id=1, source_target_pairs={{0,12},{1,13},{2,14},{3,15},{4,0},{5,1},{6,2},{7,3},{8,4},{9,5},{1... | collective-permute-start | bytes 589832 | tf_op jit(solution)/shard_map/ppermute | solution.py:365
  66.5 1.8 %collective-permute-done.16 = bf16[768,128]{1,0:T(8,128)(2,1)S(1)} collective-permute-done((bf16[768,128]{1,0:T(8,128)(2,1)S(1)}, bf16[768,128]{1,0:T(8,128)(2,1)S(1)}, u32[]{:S(2)}, u32[]{:S(2)}) %collective-permute-start.16) | collective-permute-done | bytes 196640 | tf_op jit(solution)/shard_map/ppermute | solution.py:365
  68.3 0.1 add_convert_fusion
  68.4 1.0 %collective-permute-start.17 = (bf16[768,128]{1,0:T(8,128)(2,1)S(1)}, bf16[768,128]{1,0:T(8,128)(2,1)S(1)}, u32[]{:S(2)}, u32[]{:S(2)}) collective-permute-start(bf16[768,128]{1,0:T(8,128)(2,1)S(1)} %add_convert_fusion), channel_id=1, source_target_pairs={{0,4},{1,5},{2,6},{3,7},{4,8},{5,9},{6,10},{7,11},{8,12},{9,13},{1... | collective-permute-start | bytes 589832 | tf_op jit(solution)/shard_map/ppermute | solution.py:365
  69.4 0.1 copy.11
  69.5 2.2 %collective-permute-done.11 = bf16[768,128]{1,0:T(8,128)(2,1)S(1)} collective-permute-done((bf16[768,128]{1,0:T(8,128)(2,1)S(1)}, bf16[768,128]{1,0:T(8,128)(2,1)S(1)}, u32[]{:S(2)}, u32[]{:S(2)}) %collective-permute-start.11) | collective-permute-done | bytes 196640 | tf_op jit(solution)/shard_map/ppermute | solution.py:365
  71.7 0.0 collective-permute-done.13
  71.7 5.4 %collective-permute-done.15 = bf16[768,128]{1,0:T(8,128)(2,1)S(1)} collective-permute-done((bf16[768,128]{1,0:T(8,128)(2,1)S(1)}, bf16[768,128]{1,0:T(8,128)(2,1)S(1)}, u32[]{:S(2)}, u32[]{:S(2)}) %collective-permute-start.15) | collective-permute-done | bytes 196640 | tf_op jit(solution)/shard_map/ppermute | solution.py:365
  77.1 0.0 collective-permute-done.17
  77.1 0.1 convert_add_fusion
  77.3 0.1 collective-permute-start.18
  77.4 0.5 slice_bitcast_fusion
  77.9 0.9 %collective-permute-done.18.other = f32[384,128]{1,0:T(8,128)S(1)} collective-permute-done((f32[384,128]{1,0:T(8,128)S(1)}, f32[384,128]{1,0:T(8,128)S(1)}, u32[]{:S(2)}, u32[]{:S(2)}) %collective-permute-start.18) | collective-permute-done | bytes 196640 | tf_op jit(solution)/shard_map/ppermute | solution.py:365
  78.8 3.3 %adjoint.1 = f32[1024,256]{1,0:T(8,128)} custom-call(f32[8,384]{1,0:T(8,128)S(1)} %bitcast.14, f32[384,8]{1,0:T(8,128)S(1)} %copy-done, bf16[1024,256]{1,0:T(8,128)(2,1)S(1)} %copy-done.2, bf16[8,128,128]{2,1,0:T(8,128)(2,1)S(1)} %copy-done.4, f32[384,128]{1,0:T(8,128)S(1)} %get-tuple-element.41.keep, f32[384,128]{1,0:T(8,128)S(1)} %collective-permute-done.18.other), custom_call_target="tpu_custom_call" | custom-call | flops 1000000000 | bytes 2000000 | tf_op jit(solution)/shard_map/adjoint/pallas_call | solution.py:488
  (15 shorter events, 0.1 us)
Async XLA Ops:
  0.6 13.0 %copy-start.7 = (s32[64]{0:T(128)S(1)}, s32[64]{0:T(128)}, u32[]{:S(2)}) copy-start(s32[64]{0:T(128)} %param.10) | copy-start | bytes 772
  0.6 13.1 %copy-start.1 = (bf16[64,16384]{1,0:T(8,128)(2,1)S(1)}, bf16[64,16384]{1,0:T(8,128)(2,1)}, u32[]{:S(2)}) copy-start(bf16[64,16384]{1,0:T(8,128)(2,1)} %images) | copy-start | bytes 6291460
  0.7 13.1 %copy-start.3 = (f32[8,8192]{1,0:T(8,128)S(1)}, f32[8,8192]{1,0:T(8,128)}, u32[]{:S(2)}) copy-start(f32[8,8192]{1,0:T(8,128)} %ctf.1) | copy-start | bytes 786436
  4.3 25.2 %copy-start.5 = (s32[4096,1]{0,1:T(1,128)S(1)}, s32[4096,1]{0,1:T(1,128)}, u32[]{:S(2)}) copy-start(s32[4096,1]{0,1:T(1,128)} %param.13) | copy-start | bytes 49156
  4.3 1.7 %collective-permute-start = (bf16[384,128]{1,0:T(8,128)(2,1)}, bf16[384,128]{1,0:T(8,128)(2,1)S(1)}, u32[]{:S(2)}, u32[]{:S(2)}) collective-permute-start(bf16[384,128]{1,0:T(8,128)(2,1)} %get-tuple-element.23), channel_id=1, source_target_pairs={{0,1},{1,0},{2,3},{3,2},{4,5},{5,4},{6,7},{7,6},{8,9},{9,8},{10,11... | collective-permute-start | bytes 294920 | tf_op jit(solution)/shard_map/ppermute | solution.py:365
  6.0 10.5 %collective-permute-start.1 = (bf16[768,128]{1,0:T(8,128)(2,1)S(1)}, bf16[768,128]{1,0:T(8,128)(2,1)S(1)}, u32[]{:S(2)}, u32[]{:S(2)}) collective-permute-start(bf16[768,128]{1,0:T(8,128)(2,1)S(1)} %constant_dynamic-update-slice_fusion.rest_0_), channel_id=1, source_target_pairs={{0,12},{1,13},{2,14},{3,15},{4,0},{5,1},{6,2},{7,3},{8,4},{9,5},{1... | collective-permute-start | bytes 589832 | tf_op jit(solution)/shard_map/ppermute | solution.py:365
  11.1 10.5 %collective-permute-start.6 = (bf16[768,128]{1,0:T(8,128)(2,1)S(1)}, bf16[768,128]{1,0:T(8,128)(2,1)S(1)}, u32[]{:S(2)}, u32[]{:S(2)}) collective-permute-start(bf16[768,128]{1,0:T(8,128)(2,1)S(1)} %constant_dynamic-update-slice_fusion.rest_0_), channel_id=1, source_target_pairs={{0,4},{1,5},{2,6},{3,7},{4,8},{5,9},{6,10},{7,11},{8,12},{9,13},{1... | collective-permute-start | bytes 589832 | tf_op jit(solution)/shard_map/ppermute | solution.py:365
  11.1 17.0 %collective-permute-start.8 = (bf16[768,128]{1,0:T(8,128)(2,1)S(1)}, bf16[768,128]{1,0:T(8,128)(2,1)S(1)}, u32[]{:S(2)}, u32[]{:S(2)}) collective-permute-start(bf16[768,128]{1,0:T(8,128)(2,1)S(1)} %constant_dynamic-update-slice_fusion.rest_0_), channel_id=1, source_target_pairs={{0,8},{1,9},{2,10},{3,11},{4,12},{5,13},{6,14},{7,15},{8,0},{9,1},... | collective-permute-start | bytes 589832 | tf_op jit(solution)/shard_map/ppermute | solution.py:365
  12.1 21.2 %collective-permute-start.4 = (bf16[768,128]{1,0:T(8,128)(2,1)S(1)}, bf16[768,128]{1,0:T(8,128)(2,1)S(1)}, u32[]{:S(2)}, u32[]{:S(2)}) collective-permute-start(bf16[768,128]{1,0:T(8,128)(2,1)S(1)} %constant_dynamic-update-slice_fusion.rest_0_), channel_id=1, source_target_pairs={{0,2},{1,3},{2,0},{3,1},{4,6},{5,7},{6,4},{7,5},{8,10},{9,11},{10,... | collective-permute-start | bytes 589832 | tf_op jit(solution)/shard_map/ppermute | solution.py:365
  13.7 2.2 %collective-permute-start.2 = (f32[1,64]{1,0:T(1,128)S(1)}, f32[1,64]{1,0:T(1,128)S(1)}, u32[]{:S(2)}, u32[]{:S(2)}) collective-permute-start(f32[1,64]{1,0:T(1,128)S(1)} %convert_bitcast_fusion.2), channel_id=1, source_target_pairs={{0,1},{1,0},{2,3},{3,2},{4,5},{5,4},{6,7},{7,6},{8,9},{9,8},{10,11... | collective-permute-start | bytes 776 | tf_op jit(solution)/shard_map/ppermute | solution.py:365
  15.9 15.3 %copy-start.6 = (s32[9,2]{0,1:T(2,128)S(1)}, s32[9,2]{0,1:T(2,128)}, u32[]{:S(2)}) copy-start(s32[9,2]{0,1:T(2,128)} %param.11) | copy-start | bytes 220
  15.9 18.3 %collective-permute-start.3 = (bf16[64,8192]{1,0:T(8,128)(2,1)S(1)}, bf16[64,8192]{1,0:T(8,128)(2,1)S(1)}, u32[]{:S(2)}, u32[]{:S(2)}) collective-permute-start(bf16[64,8192]{1,0:T(8,128)(2,1)S(1)} %get-tuple-element.29), channel_id=1, source_target_pairs={{0,1},{1,0},{2,3},{3,2},{4,5},{5,4},{6,7},{7,6},{8,9},{9,8},{10,11... | collective-permute-start | bytes 3145736 | tf_op jit(solution)/shard_map/ppermute | solution.py:365
  16.5 16.7 %collective-permute-start.5 = (bf16[768,128]{1,0:T(8,128)(2,1)S(1)}, bf16[768,128]{1,0:T(8,128)(2,1)S(1)}, u32[]{:S(2)}, u32[]{:S(2)}) collective-permute-start(bf16[768,128]{1,0:T(8,128)(2,1)S(1)} %collective-permute-done.1.rest_2_), channel_id=1, source_target_pairs={{0,2},{1,3},{2,0},{3,1},{4,6},{5,7},{6,4},{7,5},{8,10},{9,11},{10,... | collective-permute-start | bytes 589832 | tf_op jit(solution)/shard_map/ppermute | solution.py:365
  21.5 11.7 %collective-permute-start.7 = (bf16[768,128]{1,0:T(8,128)(2,1)S(1)}, bf16[768,128]{1,0:T(8,128)(2,1)S(1)}, u32[]{:S(2)}, u32[]{:S(2)}) collective-permute-start(bf16[768,128]{1,0:T(8,128)(2,1)S(1)} %collective-permute-done.6.rest_4_), channel_id=1, source_target_pairs={{0,2},{1,3},{2,0},{3,1},{4,6},{5,7},{6,4},{7,5},{8,10},{9,11},{10,... | collective-permute-start | bytes 589832 | tf_op jit(solution)/shard_map/ppermute | solution.py:365
  28.1 6.1 %collective-permute-start.9 = (bf16[768,128]{1,0:T(8,128)(2,1)S(1)}, bf16[768,128]{1,0:T(8,128)(2,1)S(1)}, u32[]{:S(2)}, u32[]{:S(2)}) collective-permute-start(bf16[768,128]{1,0:T(8,128)(2,1)S(1)} %collective-permute-done.8.rest_6_), channel_id=1, source_target_pairs={{0,2},{1,3},{2,0},{3,1},{4,6},{5,7},{6,4},{7,5},{8,10},{9,11},{10,... | collective-permute-start | bytes 589832 | tf_op jit(solution)/shard_map/ppermute | solution.py:365
  42.5 26.9 %copy-start = (f32[384,8]{1,0:T(8,128)S(1)}, f32[384,8]{1,0:T(8,128)}, u32[]{:S(2)}) copy-start(f32[384,8]{1,0:T(8,128)} %get-tuple-element.21.slots) | copy-start | bytes 36868
  42.5 1.6 %collective-permute-start.10 = (f32[576,128]{1,0:T(8,128)S(1)}, f32[576,128]{1,0:T(8,128)S(1)}, u32[]{:S(2)}, u32[]{:S(2)}) collective-permute-start(f32[576,128]{1,0:T(8,128)S(1)} %score.1.mine), channel_id=1, source_target_pairs={{0,1},{1,0},{2,3},{3,2},{4,5},{5,4},{6,7},{7,6},{8,9},{9,8},{10,11... | collective-permute-start | bytes 884744 | tf_op jit(solution)/shard_map/ppermute | solution.py:365
  52.0 26.8 %copy-start.2 = (bf16[1024,256]{1,0:T(8,128)(2,1)S(1)}, bf16[1024,256]{1,0:T(8,128)(2,1)}, u32[]{:S(2)}) copy-start(bf16[1024,256]{1,0:T(8,128)(2,1)} %volume.1) | copy-start | bytes 1572868
  52.0 26.8 %copy-start.4 = (bf16[8,128,128]{2,1,0:T(8,128)(2,1)S(1)}, bf16[8,128,128]{2,1,0:T(8,128)(2,1)}, u32[]{:S(2)}) copy-start(bf16[8,128,128]{2,1,0:T(8,128)(2,1)} %interp.1) | copy-start | bytes 786436
  52.1 7.8 %collective-permute-start.12 = (bf16[768,128]{1,0:T(8,128)(2,1)S(1)}, bf16[768,128]{1,0:T(8,128)(2,1)S(1)}, u32[]{:S(2)}, u32[]{:S(2)}) collective-permute-start(bf16[768,128]{1,0:T(8,128)(2,1)S(1)} %get-tuple-element.34), channel_id=1, source_target_pairs={{0,2},{1,3},{2,0},{3,1},{4,6},{5,7},{6,4},{7,5},{8,10},{9,11},{10,... | collective-permute-start | bytes 589832 | tf_op jit(solution)/shard_map/ppermute | solution.py:365
  53.7 10.4 %collective-permute-start.14 = (bf16[768,128]{1,0:T(8,128)(2,1)S(1)}, bf16[768,128]{1,0:T(8,128)(2,1)S(1)}, u32[]{:S(2)}, u32[]{:S(2)}) collective-permute-start(bf16[768,128]{1,0:T(8,128)(2,1)S(1)} %get-tuple-element.36), channel_id=1, source_target_pairs={{0,2},{1,3},{2,0},{3,1},{4,6},{5,7},{6,4},{7,5},{8,10},{9,11},{10,... | collective-permute-start | bytes 589832 | tf_op jit(solution)/shard_map/ppermute | solution.py:365
  54.1 14.1 %collective-permute-start.16 = (bf16[768,128]{1,0:T(8,128)(2,1)S(1)}, bf16[768,128]{1,0:T(8,128)(2,1)S(1)}, u32[]{:S(2)}, u32[]{:S(2)}) collective-permute-start(bf16[768,128]{1,0:T(8,128)(2,1)S(1)} %get-tuple-element.38), channel_id=1, source_target_pairs={{0,2},{1,3},{2,0},{3,1},{4,6},{5,7},{6,4},{7,5},{8,10},{9,11},{10,... | collective-permute-start | bytes 589832 | tf_op jit(solution)/shard_map/ppermute | solution.py:365
  55.7 16.0 %collective-permute-start.11 = (bf16[768,128]{1,0:T(8,128)(2,1)S(1)}, bf16[768,128]{1,0:T(8,128)(2,1)S(1)}, u32[]{:S(2)}, u32[]{:S(2)}) collective-permute-start(bf16[768,128]{1,0:T(8,128)(2,1)S(1)} %get-tuple-element.32), channel_id=1, source_target_pairs={{0,2},{1,3},{2,0},{3,1},{4,6},{5,7},{6,4},{7,5},{8,10},{9,11},{10,... | collective-permute-start | bytes 589832 | tf_op jit(solution)/shard_map/ppermute | solution.py:365
  59.9 11.8 %collective-permute-start.13 = (bf16[768,128]{1,0:T(8,128)(2,1)S(1)}, bf16[768,128]{1,0:T(8,128)(2,1)S(1)}, u32[]{:S(2)}, u32[]{:S(2)}) collective-permute-start(bf16[768,128]{1,0:T(8,128)(2,1)S(1)} %add_convert_fusion.2), channel_id=1, source_target_pairs={{0,8},{1,9},{2,10},{3,11},{4,12},{5,13},{6,14},{7,15},{8,0},{9,1},... | collective-permute-start | bytes 589832 | tf_op jit(solution)/shard_map/ppermute | solution.py:365
  64.1 13.0 %collective-permute-start.15 = (bf16[768,128]{1,0:T(8,128)(2,1)S(1)}, bf16[768,128]{1,0:T(8,128)(2,1)S(1)}, u32[]{:S(2)}, u32[]{:S(2)}) collective-permute-start(bf16[768,128]{1,0:T(8,128)(2,1)S(1)} %add_convert_fusion.1), channel_id=1, source_target_pairs={{0,12},{1,13},{2,14},{3,15},{4,0},{5,1},{6,2},{7,3},{8,4},{9,5},{1... | collective-permute-start | bytes 589832 | tf_op jit(solution)/shard_map/ppermute | solution.py:365
  68.4 8.8 %collective-permute-start.17 = (bf16[768,128]{1,0:T(8,128)(2,1)S(1)}, bf16[768,128]{1,0:T(8,128)(2,1)S(1)}, u32[]{:S(2)}, u32[]{:S(2)}) collective-permute-start(bf16[768,128]{1,0:T(8,128)(2,1)S(1)} %add_convert_fusion), channel_id=1, source_target_pairs={{0,4},{1,5},{2,6},{3,7},{4,8},{5,9},{6,10},{7,11},{8,12},{9,13},{1... | collective-permute-start | bytes 589832 | tf_op jit(solution)/shard_map/ppermute | solution.py:365
  77.3 1.5 %collective-permute-start.18 = (f32[384,128]{1,0:T(8,128)S(1)}, f32[384,128]{1,0:T(8,128)S(1)}, u32[]{:S(2)}, u32[]{:S(2)}) collective-permute-start(f32[384,128]{1,0:T(8,128)S(1)} %get-tuple-element.40), channel_id=1, source_target_pairs={{0,1},{1,0},{2,3},{3,2},{4,5},{5,4},{6,7},{7,6},{8,9},{9,8},{10,11... | collective-permute-start | bytes 589832 | tf_op jit(solution)/shard_map/ppermute | solution.py:365

commit v5 on v4

--- a/solution.py
+++ b/solution.py
@@ -289,32 +289,39 @@
             rest[1 + i * ny + ky][...] = placed[start : start + rows, :].astype(BF16)
 
 
-def adjoint_kernel(place, slots, volume, interp, keep, other, new_map):
-    core = lax.axis_index("img") & 1
-    cap = keep.shape[0]
-    mine, theirs = keep[...], other[...]
-    left = jnp.where(core == 0, mine, theirs)
-    right = jnp.where(core == 0, theirs, mine)
-    real, imag = split_halves(left, right)
-    value = jnp.concatenate([real, imag], axis=0)
-    which = slots[:, 1:2]
-    which = jnp.concatenate([which, which], axis=0)
+def interpolate_back(value, slots, interp, core):
+    which = jnp.broadcast_to(slots[:, 1:2], value.shape)
     tables = range(interp.shape[0])
-    matrix = jnp.concatenate([interp[t] for t in tables], axis=0)
+    blank = jnp.zeros((HALF, BW), BF16)
+    matrix = []
+    for t in tables:
+        half = jnp.where(core == 0, interp[t][:HALF], interp[t][HALF:])
+        matrix += [jnp.concatenate(pair, axis=1) for pair in ((half, blank), (blank, half))]
+    matrix = jnp.concatenate(matrix, axis=0)
     high = value.astype(BF16).astype(F32)
-    out = jnp.zeros((2 * cap, BW), F32)
+    out = jnp.zeros((value.shape[0], 2 * BW), F32)
     for part in (high, value - high):
         chosen = [jnp.where(which == float(t), part, 0.0).astype(BF16) for t in tables]
         out = out + dot(jnp.concatenate(chosen, axis=1), matrix)
-    out = jnp.concatenate([out[:cap], out[cap:]], axis=1)
-    depth = volume.shape[0]
-    spread = jnp.where(
-        iota((depth, cap), 0) == place[0:1, :].astype(jnp.int32), 1.0, 0.0
+    return out
+
+
+def own_half_kernel(place, slots, interp, keep, half, spread):
+    core = lax.axis_index("img") & 1
+    half[...] = interpolate_back(keep[...], slots, interp, core)
+    spread[...] = jnp.where(
+        iota(spread.shape, 0) == place[0:1, :].astype(jnp.int32), 1.0, 0.0
     ).astype(BF16)
+
+
+def adjoint_kernel(slots, volume, interp, half, spread, other, new_map):
+    core = lax.axis_index("img") & 1
+    out = half[...] + interpolate_back(other[...], slots, interp, 1 - core)
     high = out.astype(BF16)
     rest = (out - high.astype(F32)).astype(BF16)
+    hot = spread[...]
     new_map[...] = volume[...].astype(F32) + dot(
-        jnp.concatenate([spread, spread], axis=1), jnp.concatenate([high, rest], axis=0)
+        jnp.concatenate([hot, hot], axis=1), jnp.concatenate([high, rest], axis=0)
     )
 
 
@@ -474,17 +481,31 @@
     evidence = outs[0][0, :count]
     parts = {kz: outs[1 + ny * i : 1 + ny * (i + 1)] for i, kz in enumerate(order)}
     moved = {kz: [to(parts[kz][ky], along_y(ky)) for ky in range(1, ny)] for kz in order}
-    summed = {}
+    crossed = {}
     for kz in order:
-        summed[kz] = parts[kz][0].astype(F32)
+        total = parts[kz][0].astype(F32)
         for part in moved[kz]:
-            summed[kz] = summed[kz] + part.astype(F32)
-    final = summed[0]
-    for kz in near[::-1]:
-        final = final + to(summed[kz].astype(BF16), along_z(kz)).astype(F32)
-    sum_keep = final[:cap]
-    sum_other = to(final[cap:], core_pairs)
-
+            total = total + part.astype(F32)
+        crossed[kz] = to(total.astype(BF16), along_z(kz)) if kz else total
+
+    def total_of(span):
+        total = crossed[0][span]
+        for kz in near[::-1]:
+            total = total + crossed[kz][span].astype(F32)
+        return total
+
+    sum_other = to(total_of(slice(cap, rows)), core_pairs)
+    sum_keep = total_of(slice(0, cap))
+
+    half, spread = call(
+        own_half_kernel,
+        [VMEM] * 4,
+        [struct((cap, 2 * BW), F32), struct((volume.shape[0], cap), BF16)],
+        [],
+        10**9,
+        2 * 10**6,
+        "own_half",
+    )(place, slots, interp, sum_keep)
     (new_map,) = call(
         adjoint_kernel,
         [VMEM] * 6,
@@ -493,7 +514,7 @@
         10**9,
         2 * 10**6,
         "adjoint",
-    )(place, slots, volume, interp, sum_keep, sum_other)
+    )(slots, volume, interp, half, spread, sum_other)
     return (new_map, evidence)
 
 

time: 82.3 us -> 81.9 us (level)
  waiting for transfers between devices: 29.6 us -> 28.5 us
    ppermute x19, waiting for transfers between devices: 29.6 us -> 28.5 us  [to(): return lax.ppermute(array, 'img', pairs)]
    pallas_call x0 -> x1, Pallas kernels: none -> 0.98 us  [per_device(): call(own_half_kernel, [VMEM] * 4, [struct((cap, 2 * BW), F32), struct((vo...]
  transfers between devices with their start and end apart: 19 -> 19, of which waited for: 11 -> 10; matrix products, arithmetic and copies ran while one was open for 5% -> 5% of each run, Pallas kernels for 4% -> 6%
where the time goes in v5:
time: 81.9 us; the launch traced here: 81.7 us
  waiting for transfers between devices  28.5 us (35%)
  Pallas kernels  27.3 us (33%)
  starting transfers between devices  20.8 us (25%)
  other arithmetic  2.46 us (3%)
  local copies, waits for them, and re-layouts  1.64 us (2%)
  between operations  0.89 us (1%)
    ppermute x19, waiting for transfers between devices, to(): return lax.ppermute(array, 'img', pairs)  28.5 us
    ppermute x19, starting transfers between devices, to(): return lax.ppermute(array, 'img', pairs)  20.8 us
    pallas_call x1, Pallas kernels, per_device(): call(functools.partial(score_kernel, [moves for _, moves in pieces]), [SM...  8.23 us
    pallas_call x1, Pallas kernels, per_device(): call(functools.partial(back_kernel, ny, rows, order), [SMEM] + [VMEM] * 6...  7.89 us
    pallas_call x1, Pallas kernels, per_device(): call(slice_kernel, [ANY] * 5, [struct((cap, 8), F32), struct((cap, BW), B...  3.66 us
    pallas_call x1, Pallas kernels, per_device(): call(adjoint_kernel, [VMEM] * 6, [struct(volume.shape, F32)], [], 10 ** 9...  2.88 us
    pallas_call x1, Pallas kernels, per_device(): call(weigh_kernel, [VMEM] * 3, [struct((count, KB * BW), BF16), struct((c...  2.12 us
    mul x1, other arithmetic, per_device(): sine = jnp.sin(angles) * jnp.where(lane < HALF, -1.0, 1.0)  1.92 us
  transfers between devices with their start and end apart: 19, of which 10 were waited for; matrix products, arithmetic and copies ran while one was open for 5% of the time, Pallas kernels for 6%

profile of v5, /device:TPU:0, one launch (start us, length us, event | category | flops | bytes accessed | tf_op | source)
XLA Modules:
  0.0 81.7 jit_solution(13567455116343419111)
XLA Ops:
  0.7 3.7 %own_slices.1 = (f32[384,8]{1,0:T(8,128)}, bf16[384,128]{1,0:T(8,128)(2,1)}, bf16[384,128]{1,0:T(8,128)(2,1)}) custom-call(s32[32,128]{1,0:T(8,128)} %bitcast.15, s32[32,128]{1,0:T(8,128)} %bitcast.20, s32[32,128]{1,0:T(8,128)} %bitcast.21, bf16[1024,256]{1,0:T(8,128)(2,1)} %volume.1, bf16[8,128,128]{2,1,0:T(8,128)(2,1)} %interp.3), custom_call_target="tpu_custom_call" | custom-call | flops 1000000000 | bytes 1000000 | tf_op jit(solution)/shard_map/own_slices/pallas_call | solution.py:376
  4.3 0.0 copy-start.5
  4.3 0.5 collective-permute-start
  4.9 0.9 %constant_dynamic-update-slice_fusion.1 = bf16[768,128]{1,0:T(8,128)(2,1)S(1)} fusion(bf16[384,128]{1,0:T(8,128)(2,1)} %get-tuple-element.24), kind=kLoop, calls=%fused_computation.15 | loop fusion | bytes 196608
  5.8 0.2 collective-permute-done
  6.0 5.0 %collective-permute-start.1 = (bf16[768,128]{1,0:T(8,128)(2,1)S(1)}, bf16[768,128]{1,0:T(8,128)(2,1)S(1)}, u32[]{:S(2)}, u32[]{:S(2)}) collective-permute-start(bf16[768,128]{1,0:T(8,128)(2,1)S(1)} %constant_dynamic-update-slice_fusion.rest_0_), channel_id=1, source_target_pairs={{0,12},{1,13},{2,14},{3,15},{4,0},{5,1},{6,2},{7,3},{8,4},{9,5},{1... | collective-permute-start | bytes 589832 | tf_op jit(solution)/shard_map/ppermute | solution.py:372
  11.0 0.0 collective-permute-start.6
  11.0 1.0 %collective-permute-start.8 = (bf16[768,128]{1,0:T(8,128)(2,1)S(1)}, bf16[768,128]{1,0:T(8,128)(2,1)S(1)}, u32[]{:S(2)}, u32[]{:S(2)}) collective-permute-start(bf16[768,128]{1,0:T(8,128)(2,1)S(1)} %constant_dynamic-update-slice_fusion.rest_0_), channel_id=1, source_target_pairs={{0,8},{1,9},{2,10},{3,11},{4,12},{5,13},{6,14},{7,15},{8,0},{9,1},... | collective-permute-start | bytes 589832 | tf_op jit(solution)/shard_map/ppermute | solution.py:372
  12.1 1.5 %collective-permute-start.4 = (bf16[768,128]{1,0:T(8,128)(2,1)S(1)}, bf16[768,128]{1,0:T(8,128)(2,1)S(1)}, u32[]{:S(2)}, u32[]{:S(2)}) collective-permute-start(bf16[768,128]{1,0:T(8,128)(2,1)S(1)} %constant_dynamic-update-slice_fusion.rest_0_), channel_id=1, source_target_pairs={{0,2},{1,3},{2,0},{3,1},{4,6},{5,7},{6,4},{7,5},{8,10},{9,11},{10,... | collective-permute-start | bytes 589832 | tf_op jit(solution)/shard_map/ppermute | solution.py:372
  13.6 0.0 copy-done.7
  13.6 0.1 copy.12.group
  13.7 0.0 collective-permute-start.2
  13.7 2.1 %weigh.1 = (bf16[64,8192]{1,0:T(8,128)(2,1)S(1)}, bf16[64,8192]{1,0:T(8,128)(2,1)S(1)}, bf16[16,8192]{1,0:T(8,128)(2,1)S(1)}) custom-call(bf16[64,16384]{1,0:T(8,128)(2,1)S(1)} %copy-done.1, s32[64,1]{1,0:T(8,128)S(1)} %copy.12.group, f32[8,8192]{1,0:T(8,128)S(1)} %copy-done.3), custom_call_target="tpu_custom_call" | custom-call | flops 1000000000 | bytes 4000000 | tf_op jit(solution)/shard_map/weigh/pallas_call | solution.py:418
  15.9 0.0 copy-start.6
  15.9 0.0 collective-permute-done.2
  15.9 0.5 collective-permute-start.3
  16.4 0.1 maximum_convert_fusion.group
  16.5 0.0 collective-permute-done.1.rest_2_
  16.5 1.4 %collective-permute-start.5 = (bf16[768,128]{1,0:T(8,128)(2,1)S(1)}, bf16[768,128]{1,0:T(8,128)(2,1)S(1)}, u32[]{:S(2)}, u32[]{:S(2)}) collective-permute-start(bf16[768,128]{1,0:T(8,128)(2,1)S(1)} %collective-permute-done.1.rest_2_), channel_id=1, source_target_pairs={{0,2},{1,3},{2,0},{3,1},{4,6},{5,7},{6,4},{7,5},{8,10},{9,11},{10,... | collective-permute-start | bytes 589832 | tf_op jit(solution)/shard_map/ppermute | solution.py:372
  17.9 3.7 %collective-permute-done.6.rest_4_ = bf16[768,128]{1,0:T(8,128)(2,1)S(1)} collective-permute-done((bf16[768,128]{1,0:T(8,128)(2,1)S(1)}, bf16[768,128]{1,0:T(8,128)(2,1)S(1)}, u32[]{:S(2)}, u32[]{:S(2)}) %collective-permute-start.6) | collective-permute-done | bytes 196640 | tf_op jit(solution)/shard_map/ppermute | solution.py:372
  21.5 1.5 %collective-permute-start.7 = (bf16[768,128]{1,0:T(8,128)(2,1)S(1)}, bf16[768,128]{1,0:T(8,128)(2,1)S(1)}, u32[]{:S(2)}, u32[]{:S(2)}) collective-permute-start(bf16[768,128]{1,0:T(8,128)(2,1)S(1)} %collective-permute-done.6.rest_4_), channel_id=1, source_target_pairs={{0,2},{1,3},{2,0},{3,1},{4,6},{5,7},{6,4},{7,5},{8,10},{9,11},{10,... | collective-permute-start | bytes 589832 | tf_op jit(solution)/shard_map/ppermute | solution.py:372
  23.0 5.0 %collective-permute-done.8.rest_6_ = bf16[768,128]{1,0:T(8,128)(2,1)S(1)} collective-permute-done((bf16[768,128]{1,0:T(8,128)(2,1)S(1)}, bf16[768,128]{1,0:T(8,128)(2,1)S(1)}, u32[]{:S(2)}, u32[]{:S(2)}) %collective-permute-start.8) | collective-permute-done | bytes 196640 | tf_op jit(solution)/shard_map/ppermute | solution.py:372
  28.1 1.5 %collective-permute-start.9 = (bf16[768,128]{1,0:T(8,128)(2,1)S(1)}, bf16[768,128]{1,0:T(8,128)(2,1)S(1)}, u32[]{:S(2)}, u32[]{:S(2)}) collective-permute-start(bf16[768,128]{1,0:T(8,128)(2,1)S(1)} %collective-permute-done.8.rest_6_), channel_id=1, source_target_pairs={{0,2},{1,3},{2,0},{3,1},{4,6},{5,7},{6,4},{7,5},{8,10},{9,11},{10,... | collective-permute-start | bytes 589832 | tf_op jit(solution)/shard_map/ppermute | solution.py:372
  29.6 1.6 %target.1 = s32[32,128]{1,0:T(8,128)S(1)} custom-call(s32[32,128]{1,0:T(8,128)S(1)} %bitcast.16), custom_call_target="tpu_custom_call" | custom-call | flops 1000000000 | bytes 1000000 | tf_op jit(solution)/shard_map/target/pallas_call | solution.py:407
  31.2 0.1 broadcast_multiply_fusion.1
  31.2 0.1 broadcast_multiply_fusion
  31.3 1.9 %sine_multiply_fusion = (f32[64,9,128]{2,1,0:T(8,128)S(1)}, f32[64,9,128]{2,1,0:T(8,128)S(1)}) fusion(f32[128]{0:T(128)S(1)} %compare_select_fusion, f32[64,9]{1,0:T(8,128)S(1)} %broadcast_multiply_fusion, f32[9,128]{1,0:T(8,128)S(1)} %broadcast_multiply_fusion.1), kind=kLoop, calls=%fused_computation | loop fusion | flops 221184 | bytes 597248 | tf_op jit(solution)/shard_map/mul | solution.py:451
  33.2 0.0 collective-permute-done.4.rest_1_
  33.2 0.0 collective-permute-done.5.rest_3_
  33.2 0.0 collective-permute-done.7.rest_5_
  33.3 0.9 %collective-permute-done.9.rest_7_ = bf16[768,128]{1,0:T(8,128)(2,1)S(1)} collective-permute-done((bf16[768,128]{1,0:T(8,128)(2,1)S(1)}, bf16[768,128]{1,0:T(8,128)(2,1)S(1)}, u32[]{:S(2)}, u32[]{:S(2)}) %collective-permute-start.9) | collective-permute-done | bytes 196640 | tf_op jit(solution)/shard_map/ppermute | solution.py:372
  34.2 0.0 collective-permute-done.3.other
  34.2 8.2 %score.1.mine = f32[576,128]{1,0:T(8,128)S(1)} custom-call(s32[4096]{0:T(1024)S(1)} %bitcast.17, s32[1,128]{1,0:T(1,128)S(1)} %maximum_convert_fusion.group, f32[64,9,128]{2,1,0:T(8,128)S(1)} %get-tuple-element.47.cosine, f32[64,9,128]{2,1,0:T(8,128)S(1)} %get-tuple-element.46.sine, bf16[64,8192]{1,0:T(8,128)(2,1)S(1)} %get-tuple-element.30.keep, ...), custom_call_target="tpu_custom_call" | custom-call | flops 4000000000 | bytes 10000000 | tf_op jit(solution)/shard_map/score/pallas_call | solution.py:453
  42.4 0.0 copy-start
  42.4 0.1 collective-permute-start.10
  42.5 1.6 %collective-permute-done.10.theirs = f32[576,128]{1,0:T(8,128)S(1)} collective-permute-done((f32[576,128]{1,0:T(8,128)S(1)}, f32[576,128]{1,0:T(8,128)S(1)}, u32[]{:S(2)}, u32[]{:S(2)}) %collective-permute-start.10) | collective-permute-done | bytes 294944 | tf_op jit(solution)/shard_map/ppermute | solution.py:372
  44.1 7.9 %back.1 = (f32[1,128]{1,0:T(1,128)S(1)}, bf16[768,128]{1,0:T(8,128)(2,1)S(1)}, bf16[768,128]{1,0:T(8,128)(2,1)S(1)}, bf16[768,128]{1,0:T(8,128)(2,1)S(1)}, bf16[...) custom-call(s32[4096]{0:T(1024)S(1)} %bitcast.18, ...), custom_call_target="tpu_custom_call" | custom-call | flops 4000000000 | bytes 10000000 | tf_op jit(solution)/shard_map/back/pallas_call | solution.py:471
  52.0 0.0 copy-start.4
  52.0 1.6 %collective-permute-start.12 = (bf16[768,128]{1,0:T(8,128)(2,1)S(1)}, bf16[768,128]{1,0:T(8,128)(2,1)S(1)}, u32[]{:S(2)}, u32[]{:S(2)}) collective-permute-start(bf16[768,128]{1,0:T(8,128)(2,1)S(1)} %get-tuple-element.36), channel_id=1, source_target_pairs={{0,2},{1,3},{2,0},{3,1},{4,6},{5,7},{6,4},{7,5},{8,10},{9,11},{10,... | collective-permute-start | bytes 589832 | tf_op jit(solution)/shard_map/ppermute | solution.py:372
  53.6 0.1 copy.11
  53.7 0.6 collective-permute-start.14
  54.2 1.5 %collective-permute-start.16 = (bf16[768,128]{1,0:T(8,128)(2,1)S(1)}, bf16[768,128]{1,0:T(8,128)(2,1)S(1)}, u32[]{:S(2)}, u32[]{:S(2)}) collective-permute-start(bf16[768,128]{1,0:T(8,128)(2,1)S(1)} %get-tuple-element.40), channel_id=1, source_target_pairs={{0,2},{1,3},{2,0},{3,1},{4,6},{5,7},{6,4},{7,5},{8,10},{9,11},{10,... | collective-permute-start | bytes 589832 | tf_op jit(solution)/shard_map/ppermute | solution.py:372
  55.7 0.5 collective-permute-start.11
  56.2 3.6 %collective-permute-done.12 = bf16[768,128]{1,0:T(8,128)(2,1)S(1)} collective-permute-done((bf16[768,128]{1,0:T(8,128)(2,1)S(1)}, bf16[768,128]{1,0:T(8,128)(2,1)S(1)}, u32[]{:S(2)}, u32[]{:S(2)}) %collective-permute-start.12) | collective-permute-done | bytes 196640 | tf_op jit(solution)/shard_map/ppermute | solution.py:372
  59.8 0.1 add_convert_fusion.2
  59.9 0.1 collective-permute-start.13
  59.9 4.1 %collective-permute-done.14 = bf16[768,128]{1,0:T(8,128)(2,1)S(1)} collective-permute-done((bf16[768,128]{1,0:T(8,128)(2,1)S(1)}, bf16[768,128]{1,0:T(8,128)(2,1)S(1)}, u32[]{:S(2)}, u32[]{:S(2)}) %collective-permute-start.14) | collective-permute-done | bytes 196640 | tf_op jit(solution)/shard_map/ppermute | solution.py:372
  64.0 0.1 add_convert_fusion.1
  64.1 2.4 %collective-permute-start.15 = (bf16[768,128]{1,0:T(8,128)(2,1)S(1)}, bf16[768,128]{1,0:T(8,128)(2,1)S(1)}, u32[]{:S(2)}, u32[]{:S(2)}) collective-permute-start(bf16[768,128]{1,0:T(8,128)(2,1)S(1)} %add_convert_fusion.1), channel_id=1, source_target_pairs={{0,12},{1,13},{2,14},{3,15},{4,0},{5,1},{6,2},{7,3},{8,4},{9,5},{1... | collective-permute-start | bytes 589832 | tf_op jit(solution)/shard_map/ppermute | solution.py:372
  66.5 1.8 %collective-permute-done.16 = bf16[768,128]{1,0:T(8,128)(2,1)S(1)} collective-permute-done((bf16[768,128]{1,0:T(8,128)(2,1)S(1)}, bf16[768,128]{1,0:T(8,128)(2,1)S(1)}, u32[]{:S(2)}, u32[]{:S(2)}) %collective-permute-start.16) | collective-permute-done | bytes 196640 | tf_op jit(solution)/shard_map/ppermute | solution.py:372
  68.2 0.1 add_convert_fusion
  68.3 1.0 %collective-permute-start.17 = (bf16[768,128]{1,0:T(8,128)(2,1)S(1)}, bf16[768,128]{1,0:T(8,128)(2,1)S(1)}, u32[]{:S(2)}, u32[]{:S(2)}) collective-permute-start(bf16[768,128]{1,0:T(8,128)(2,1)S(1)} %add_convert_fusion), channel_id=1, source_target_pairs={{0,4},{1,5},{2,6},{3,7},{4,8},{5,9},{6,10},{7,11},{8,12},{9,13},{1... | collective-permute-start | bytes 589832 | tf_op jit(solution)/shard_map/ppermute | solution.py:372
  69.3 2.3 %collective-permute-done.11 = bf16[768,128]{1,0:T(8,128)(2,1)S(1)} collective-permute-done((bf16[768,128]{1,0:T(8,128)(2,1)S(1)}, bf16[768,128]{1,0:T(8,128)(2,1)S(1)}, u32[]{:S(2)}, u32[]{:S(2)}) %collective-permute-start.11) | collective-permute-done | bytes 196640 | tf_op jit(solution)/shard_map/ppermute | solution.py:372
  71.6 0.1 convert_add_fusion
  71.7 0.0 collective-permute-done.13
  71.7 5.4 %collective-permute-done.15 = bf16[768,128]{1,0:T(8,128)(2,1)S(1)} collective-permute-done((bf16[768,128]{1,0:T(8,128)(2,1)S(1)}, bf16[768,128]{1,0:T(8,128)(2,1)S(1)}, u32[]{:S(2)}, u32[]{:S(2)}) %collective-permute-start.15) | collective-permute-done | bytes 196640 | tf_op jit(solution)/shard_map/ppermute | solution.py:372
  77.1 0.0 collective-permute-done.17
  77.1 0.1 fusion.2
  77.2 0.0 copy-start.2
  77.2 0.1 collective-permute-start.18
  77.3 0.5 slice_bitcast_fusion
  77.8 1.0 %own_half.1 = (f32[384,256]{1,0:T(8,128)S(1)}, bf16[1024,384]{1,0:T(8,128)(2,1)S(1)}) custom-call(f32[8,384]{1,0:T(8,128)S(1)} %bitcast.14, f32[384,8]{1,0:T(8,128)S(1)} %copy-done, bf16[8,128,128]{2,1,0:T(8,128)(2,1)S(1)} %copy-done.4, f32[384,128]{1,0:T(8,128)S(1)} %get-tuple-element.45.keep), custom_call_target="tpu_custom_call" | custom-call | flops 1000000000 | bytes 2000000 | tf_op jit(solution)/shard_map/own_half/pallas_call | solution.py:500
  78.8 0.0 collective-permute-done.18.other
  78.8 2.9 %adjoint.1 = f32[1024,256]{1,0:T(8,128)} custom-call(f32[384,8]{1,0:T(8,128)S(1)} %copy-done, bf16[1024,256]{1,0:T(8,128)(2,1)S(1)} %copy-done.2, bf16[8,128,128]{2,1,0:T(8,128)(2,1)S(1)} %copy-done.4, f32[384,256]{1,0:T(8,128)S(1)} %get-tuple-element.41.half, bf16[1024,384]{1,0:T(8,128)(2,1)S(1)} %get-tuple-element.42.spread, ...), custom_call_target="tpu_custom_call" | custom-call | flops 1000000000 | bytes 2000000 | tf_op jit(solution)/shard_map/adjoint/pallas_call | solution.py:509
  (16 shorter events, 0.1 us)
Async XLA Ops:
  0.6 12.9 %copy-start.7 = (s32[64]{0:T(128)S(1)}, s32[64]{0:T(128)}, u32[]{:S(2)}) copy-start(s32[64]{0:T(128)} %param.10) | copy-start | bytes 772
  0.6 13.1 %copy-start.1 = (bf16[64,16384]{1,0:T(8,128)(2,1)S(1)}, bf16[64,16384]{1,0:T(8,128)(2,1)}, u32[]{:S(2)}) copy-start(bf16[64,16384]{1,0:T(8,128)(2,1)} %images) | copy-start | bytes 6291460
  0.7 13.1 %copy-start.3 = (f32[8,8192]{1,0:T(8,128)S(1)}, f32[8,8192]{1,0:T(8,128)}, u32[]{:S(2)}) copy-start(f32[8,8192]{1,0:T(8,128)} %ctf.1) | copy-start | bytes 786436
  4.3 25.2 %copy-start.5 = (s32[4096,1]{0,1:T(1,128)S(1)}, s32[4096,1]{0,1:T(1,128)}, u32[]{:S(2)}) copy-start(s32[4096,1]{0,1:T(1,128)} %param.13) | copy-start | bytes 49156
  4.3 1.7 %collective-permute-start = (bf16[384,128]{1,0:T(8,128)(2,1)}, bf16[384,128]{1,0:T(8,128)(2,1)S(1)}, u32[]{:S(2)}, u32[]{:S(2)}) collective-permute-start(bf16[384,128]{1,0:T(8,128)(2,1)} %get-tuple-element.25), channel_id=1, source_target_pairs={{0,1},{1,0},{2,3},{3,2},{4,5},{5,4},{6,7},{7,6},{8,9},{9,8},{10,11... | collective-permute-start | bytes 294920 | tf_op jit(solution)/shard_map/ppermute | solution.py:372
  6.0 10.5 %collective-permute-start.1 = (bf16[768,128]{1,0:T(8,128)(2,1)S(1)}, bf16[768,128]{1,0:T(8,128)(2,1)S(1)}, u32[]{:S(2)}, u32[]{:S(2)}) collective-permute-start(bf16[768,128]{1,0:T(8,128)(2,1)S(1)} %constant_dynamic-update-slice_fusion.rest_0_), channel_id=1, source_target_pairs={{0,12},{1,13},{2,14},{3,15},{4,0},{5,1},{6,2},{7,3},{8,4},{9,5},{1... | collective-permute-start | bytes 589832 | tf_op jit(solution)/shard_map/ppermute | solution.py:372
  11.0 10.5 %collective-permute-start.6 = (bf16[768,128]{1,0:T(8,128)(2,1)S(1)}, bf16[768,128]{1,0:T(8,128)(2,1)S(1)}, u32[]{:S(2)}, u32[]{:S(2)}) collective-permute-start(bf16[768,128]{1,0:T(8,128)(2,1)S(1)} %constant_dynamic-update-slice_fusion.rest_0_), channel_id=1, source_target_pairs={{0,4},{1,5},{2,6},{3,7},{4,8},{5,9},{6,10},{7,11},{8,12},{9,13},{1... | collective-permute-start | bytes 589832 | tf_op jit(solution)/shard_map/ppermute | solution.py:372
  11.0 17.0 %collective-permute-start.8 = (bf16[768,128]{1,0:T(8,128)(2,1)S(1)}, bf16[768,128]{1,0:T(8,128)(2,1)S(1)}, u32[]{:S(2)}, u32[]{:S(2)}) collective-permute-start(bf16[768,128]{1,0:T(8,128)(2,1)S(1)} %constant_dynamic-update-slice_fusion.rest_0_), channel_id=1, source_target_pairs={{0,8},{1,9},{2,10},{3,11},{4,12},{5,13},{6,14},{7,15},{8,0},{9,1},... | collective-permute-start | bytes 589832 | tf_op jit(solution)/shard_map/ppermute | solution.py:372
  12.1 21.2 %collective-permute-start.4 = (bf16[768,128]{1,0:T(8,128)(2,1)S(1)}, bf16[768,128]{1,0:T(8,128)(2,1)S(1)}, u32[]{:S(2)}, u32[]{:S(2)}) collective-permute-start(bf16[768,128]{1,0:T(8,128)(2,1)S(1)} %constant_dynamic-update-slice_fusion.rest_0_), channel_id=1, source_target_pairs={{0,2},{1,3},{2,0},{3,1},{4,6},{5,7},{6,4},{7,5},{8,10},{9,11},{10,... | collective-permute-start | bytes 589832 | tf_op jit(solution)/shard_map/ppermute | solution.py:372
  13.7 2.2 %collective-permute-start.2 = (f32[1,64]{1,0:T(1,128)S(1)}, f32[1,64]{1,0:T(1,128)S(1)}, u32[]{:S(2)}, u32[]{:S(2)}) collective-permute-start(f32[1,64]{1,0:T(1,128)S(1)} %convert_bitcast_fusion.2), channel_id=1, source_target_pairs={{0,1},{1,0},{2,3},{3,2},{4,5},{5,4},{6,7},{7,6},{8,9},{9,8},{10,11... | collective-permute-start | bytes 776 | tf_op jit(solution)/shard_map/ppermute | solution.py:372
  15.9 15.3 %copy-start.6 = (s32[9,2]{0,1:T(2,128)S(1)}, s32[9,2]{0,1:T(2,128)}, u32[]{:S(2)}) copy-start(s32[9,2]{0,1:T(2,128)} %param.11) | copy-start | bytes 220
  15.9 18.3 %collective-permute-start.3 = (bf16[64,8192]{1,0:T(8,128)(2,1)S(1)}, bf16[64,8192]{1,0:T(8,128)(2,1)S(1)}, u32[]{:S(2)}, u32[]{:S(2)}) collective-permute-start(bf16[64,8192]{1,0:T(8,128)(2,1)S(1)} %get-tuple-element.31), channel_id=1, source_target_pairs={{0,1},{1,0},{2,3},{3,2},{4,5},{5,4},{6,7},{7,6},{8,9},{9,8},{10,11... | collective-permute-start | bytes 3145736 | tf_op jit(solution)/shard_map/ppermute | solution.py:372
  16.5 16.7 %collective-permute-start.5 = (bf16[768,128]{1,0:T(8,128)(2,1)S(1)}, bf16[768,128]{1,0:T(8,128)(2,1)S(1)}, u32[]{:S(2)}, u32[]{:S(2)}) collective-permute-start(bf16[768,128]{1,0:T(8,128)(2,1)S(1)} %collective-permute-done.1.rest_2_), channel_id=1, source_target_pairs={{0,2},{1,3},{2,0},{3,1},{4,6},{5,7},{6,4},{7,5},{8,10},{9,11},{10,... | collective-permute-start | bytes 589832 | tf_op jit(solution)/shard_map/ppermute | solution.py:372
  21.5 11.7 %collective-permute-start.7 = (bf16[768,128]{1,0:T(8,128)(2,1)S(1)}, bf16[768,128]{1,0:T(8,128)(2,1)S(1)}, u32[]{:S(2)}, u32[]{:S(2)}) collective-permute-start(bf16[768,128]{1,0:T(8,128)(2,1)S(1)} %collective-permute-done.6.rest_4_), channel_id=1, source_target_pairs={{0,2},{1,3},{2,0},{3,1},{4,6},{5,7},{6,4},{7,5},{8,10},{9,11},{10,... | collective-permute-start | bytes 589832 | tf_op jit(solution)/shard_map/ppermute | solution.py:372
  28.1 6.1 %collective-permute-start.9 = (bf16[768,128]{1,0:T(8,128)(2,1)S(1)}, bf16[768,128]{1,0:T(8,128)(2,1)S(1)}, u32[]{:S(2)}, u32[]{:S(2)}) collective-permute-start(bf16[768,128]{1,0:T(8,128)(2,1)S(1)} %collective-permute-done.8.rest_6_), channel_id=1, source_target_pairs={{0,2},{1,3},{2,0},{3,1},{4,6},{5,7},{6,4},{7,5},{8,10},{9,11},{10,... | collective-permute-start | bytes 589832 | tf_op jit(solution)/shard_map/ppermute | solution.py:372
  42.4 11.2 %copy-start = (f32[384,8]{1,0:T(8,128)S(1)}, f32[384,8]{1,0:T(8,128)}, u32[]{:S(2)}) copy-start(f32[384,8]{1,0:T(8,128)} %get-tuple-element.23.slots) | copy-start | bytes 36868
  42.4 1.6 %collective-permute-start.10 = (f32[576,128]{1,0:T(8,128)S(1)}, f32[576,128]{1,0:T(8,128)S(1)}, u32[]{:S(2)}, u32[]{:S(2)}) collective-permute-start(f32[576,128]{1,0:T(8,128)S(1)} %score.1.mine), channel_id=1, source_target_pairs={{0,1},{1,0},{2,3},{3,2},{4,5},{5,4},{6,7},{7,6},{8,9},{9,8},{10,11... | collective-permute-start | bytes 884744 | tf_op jit(solution)/shard_map/ppermute | solution.py:372
  52.0 25.8 %copy-start.4 = (bf16[8,128,128]{2,1,0:T(8,128)(2,1)S(1)}, bf16[8,128,128]{2,1,0:T(8,128)(2,1)}, u32[]{:S(2)}) copy-start(bf16[8,128,128]{2,1,0:T(8,128)(2,1)} %interp.3) | copy-start | bytes 786436
  52.0 7.8 %collective-permute-start.12 = (bf16[768,128]{1,0:T(8,128)(2,1)S(1)}, bf16[768,128]{1,0:T(8,128)(2,1)S(1)}, u32[]{:S(2)}, u32[]{:S(2)}) collective-permute-start(bf16[768,128]{1,0:T(8,128)(2,1)S(1)} %get-tuple-element.36), channel_id=1, source_target_pairs={{0,2},{1,3},{2,0},{3,1},{4,6},{5,7},{6,4},{7,5},{8,10},{9,11},{10,... | collective-permute-start | bytes 589832 | tf_op jit(solution)/shard_map/ppermute | solution.py:372
  53.7 10.4 %collective-permute-start.14 = (bf16[768,128]{1,0:T(8,128)(2,1)S(1)}, bf16[768,128]{1,0:T(8,128)(2,1)S(1)}, u32[]{:S(2)}, u32[]{:S(2)}) collective-permute-start(bf16[768,128]{1,0:T(8,128)(2,1)S(1)} %get-tuple-element.38), channel_id=1, source_target_pairs={{0,2},{1,3},{2,0},{3,1},{4,6},{5,7},{6,4},{7,5},{8,10},{9,11},{10,... | collective-permute-start | bytes 589832 | tf_op jit(solution)/shard_map/ppermute | solution.py:372
  54.2 14.0 %collective-permute-start.16 = (bf16[768,128]{1,0:T(8,128)(2,1)S(1)}, bf16[768,128]{1,0:T(8,128)(2,1)S(1)}, u32[]{:S(2)}, u32[]{:S(2)}) collective-permute-start(bf16[768,128]{1,0:T(8,128)(2,1)S(1)} %get-tuple-element.40), channel_id=1, source_target_pairs={{0,2},{1,3},{2,0},{3,1},{4,6},{5,7},{6,4},{7,5},{8,10},{9,11},{10,... | collective-permute-start | bytes 589832 | tf_op jit(solution)/shard_map/ppermute | solution.py:372
  55.7 15.9 %collective-permute-start.11 = (bf16[768,128]{1,0:T(8,128)(2,1)S(1)}, bf16[768,128]{1,0:T(8,128)(2,1)S(1)}, u32[]{:S(2)}, u32[]{:S(2)}) collective-permute-start(bf16[768,128]{1,0:T(8,128)(2,1)S(1)} %get-tuple-element.34), channel_id=1, source_target_pairs={{0,2},{1,3},{2,0},{3,1},{4,6},{5,7},{6,4},{7,5},{8,10},{9,11},{10,... | collective-permute-start | bytes 589832 | tf_op jit(solution)/shard_map/ppermute | solution.py:372
  59.9 11.8 %collective-permute-start.13 = (bf16[768,128]{1,0:T(8,128)(2,1)S(1)}, bf16[768,128]{1,0:T(8,128)(2,1)S(1)}, u32[]{:S(2)}, u32[]{:S(2)}) collective-permute-start(bf16[768,128]{1,0:T(8,128)(2,1)S(1)} %add_convert_fusion.2), channel_id=1, source_target_pairs={{0,8},{1,9},{2,10},{3,11},{4,12},{5,13},{6,14},{7,15},{8,0},{9,1},... | collective-permute-start | bytes 589832 | tf_op jit(solution)/shard_map/ppermute | solution.py:372
  64.1 13.0 %collective-permute-start.15 = (bf16[768,128]{1,0:T(8,128)(2,1)S(1)}, bf16[768,128]{1,0:T(8,128)(2,1)S(1)}, u32[]{:S(2)}, u32[]{:S(2)}) collective-permute-start(bf16[768,128]{1,0:T(8,128)(2,1)S(1)} %add_convert_fusion.1), channel_id=1, source_target_pairs={{0,12},{1,13},{2,14},{3,15},{4,0},{5,1},{6,2},{7,3},{8,4},{9,5},{1... | collective-permute-start | bytes 589832 | tf_op jit(solution)/shard_map/ppermute | solution.py:372
  68.3 8.8 %collective-permute-start.17 = (bf16[768,128]{1,0:T(8,128)(2,1)S(1)}, bf16[768,128]{1,0:T(8,128)(2,1)S(1)}, u32[]{:S(2)}, u32[]{:S(2)}) collective-permute-start(bf16[768,128]{1,0:T(8,128)(2,1)S(1)} %add_convert_fusion), channel_id=1, source_target_pairs={{0,4},{1,5},{2,6},{3,7},{4,8},{5,9},{6,10},{7,11},{8,12},{9,13},{1... | collective-permute-start | bytes 589832 | tf_op jit(solution)/shard_map/ppermute | solution.py:372
  77.2 1.6 %copy-start.2 = (bf16[1024,256]{1,0:T(8,128)(2,1)S(1)}, bf16[1024,256]{1,0:T(8,128)(2,1)}, u32[]{:S(2)}) copy-start(bf16[1024,256]{1,0:T(8,128)(2,1)} %volume.1) | copy-start | bytes 1572868
  77.2 1.6 %collective-permute-start.18 = (f32[384,128]{1,0:T(8,128)S(1)}, f32[384,128]{1,0:T(8,128)S(1)}, u32[]{:S(2)}, u32[]{:S(2)}) collective-permute-start(f32[384,128]{1,0:T(8,128)S(1)} %get-tuple-element.44), channel_id=1, source_target_pairs={{0,1},{1,0},{2,3},{3,2},{4,5},{5,4},{6,7},{7,6},{8,9},{9,8},{10,11... | collective-permute-start | bytes 589832 | tf_op jit(solution)/shard_map/ppermute | solution.py:372

commit v6 on v5

--- a/solution.py
+++ b/solution.py
@@ -14,6 +14,7 @@
 HALF = BW // 2
 BLOCKS = R * KB
 GROUP = 4
+PARTS = 4
 
 F32 = jnp.float32
 BF16 = jnp.bfloat16
@@ -314,15 +315,25 @@
     ).astype(BF16)
 
 
-def adjoint_kernel(slots, volume, interp, half, spread, other, new_map):
+def adjoint_kernel(slots, volume, interp, half, spread, other, new_map, held, sent):
     core = lax.axis_index("img") & 1
     out = half[...] + interpolate_back(other[...], slots, interp, 1 - core)
     high = out.astype(BF16)
     rest = (out - high.astype(F32)).astype(BF16)
-    hot = spread[...]
-    new_map[...] = volume[...].astype(F32) + dot(
-        jnp.concatenate([hot, hot], axis=1), jnp.concatenate([high, rest], axis=0)
-    )
+    sums = jnp.concatenate([high, rest], axis=0)
+    size = volume.shape[0] // PARTS
+    copies = []
+    for part in range(PARTS):
+        rows = slice(part * size, (part + 1) * size)
+        hot = spread[rows, :]
+        held[rows, :] = volume[rows, :].astype(F32) + dot(
+            jnp.concatenate([hot, hot], axis=1), sums
+        )
+        copy = pltpu.make_async_copy(held.at[rows, :], new_map.at[rows, :], sent.at[part])
+        copy.start()
+        copies.append(copy)
+    for copy in copies:
+        copy.wait()
 
 
 SMEM = pl.BlockSpec(memory_space=pltpu.SMEM)
@@ -330,11 +341,11 @@
 ANY = pl.BlockSpec(memory_space=pl.ANY)
 
 
-def call(kernel, in_specs, out_shapes, scratch, flops, touched, name, limit=40):
+def call(kernel, in_specs, out_shapes, scratch, flops, touched, name, limit=40, out=VMEM):
     return pl.pallas_call(
         kernel,
         in_specs=in_specs,
-        out_specs=[VMEM] * len(out_shapes),
+        out_specs=[out] * len(out_shapes),
         out_shape=out_shapes,
         scratch_shapes=scratch,
         compiler_params=pltpu.CompilerParams(vmem_limit_bytes=limit * 1024 * 1024),
@@ -510,10 +521,12 @@
         adjoint_kernel,
         [VMEM] * 6,
         [struct(volume.shape, F32)],
-        [],
+        [pltpu.VMEM(volume.shape, F32), pltpu.SemaphoreType.DMA((PARTS,))],
         10**9,
         2 * 10**6,
         "adjoint",
+        40,
+        ANY,
     )(slots, volume, interp, half, spread, sum_other)
     return (new_map, evidence)
 

time: 81.9 us -> 81.6 us (level)
  no operation moved by 1% of the time
where the time goes in v6:
time: 81.6 us; the launch traced here: 81.4 us
  waiting for transfers between devices  28.5 us (35%)
  Pallas kernels  27.1 us (33%)
  starting transfers between devices  20.8 us (25%)
  other arithmetic  2.46 us (3%)
  local copies, waits for them, and re-layouts  1.64 us (2%)
  between operations  0.89 us (1%)
    ppermute x19, waiting for transfers between devices, to(): return lax.ppermute(array, 'img', pairs)  28.5 us
    ppermute x19, starting transfers between devices, to(): return lax.ppermute(array, 'img', pairs)  20.8 us
    pallas_call x1, Pallas kernels, per_device(): call(functools.partial(score_kernel, [moves for _, moves in pieces]), [SM...  8.25 us
    pallas_call x1, Pallas kernels, per_device(): call(functools.partial(back_kernel, ny, rows, order), [SMEM] + [VMEM] * 6...  7.89 us
    pallas_call x1, Pallas kernels, per_device(): call(slice_kernel, [ANY] * 5, [struct((cap, 8), F32), struct((cap, BW), B...  3.66 us
    pallas_call x1, Pallas kernels, per_device(): call(adjoint_kernel, [VMEM] * 6, [struct(volume.shape, F32)], [pltpu.VMEM...  2.65 us
    pallas_call x1, Pallas kernels, per_device(): call(weigh_kernel, [VMEM] * 3, [struct((count, KB * BW), BF16), struct((c...  2.12 us
    mul x1, other arithmetic, per_device(): sine = jnp.sin(angles) * jnp.where(lane < HALF, -1.0, 1.0)  1.92 us
  transfers between devices with their start and end apart: 19, of which 10 were waited for; matrix products, arithmetic and copies ran while one was open for 5% of the time, Pallas kernels for 6%

profile of v6, /device:TPU:0, one launch (start us, length us, event | category | flops | bytes accessed | tf_op | source)
XLA Modules:
  0.0 81.4 jit_solution(6222506118642765604)
XLA Ops:
  0.7 3.7 %own_slices.1 = (f32[384,8]{1,0:T(8,128)}, bf16[384,128]{1,0:T(8,128)(2,1)}, bf16[384,128]{1,0:T(8,128)(2,1)}) custom-call(s32[32,128]{1,0:T(8,128)} %bitcast.15, s32[32,128]{1,0:T(8,128)} %bitcast.20, s32[32,128]{1,0:T(8,128)} %bitcast.21, bf16[1024,256]{1,0:T(8,128)(2,1)} %volume.1, bf16[8,128,128]{2,1,0:T(8,128)(2,1)} %interp.3), custom_call_target="tpu_custom_call" | custom-call | flops 1000000000 | bytes 1000000 | tf_op jit(solution)/shard_map/own_slices/pallas_call | solution.py:387
  4.3 0.0 copy-start.5
  4.3 0.5 collective-permute-start
  4.9 0.9 %constant_dynamic-update-slice_fusion.1 = bf16[768,128]{1,0:T(8,128)(2,1)S(1)} fusion(bf16[384,128]{1,0:T(8,128)(2,1)} %get-tuple-element.24), kind=kLoop, calls=%fused_computation.15 | loop fusion | bytes 196608
  5.8 0.2 collective-permute-done
  6.0 5.0 %collective-permute-start.1 = (bf16[768,128]{1,0:T(8,128)(2,1)S(1)}, bf16[768,128]{1,0:T(8,128)(2,1)S(1)}, u32[]{:S(2)}, u32[]{:S(2)}) collective-permute-start(bf16[768,128]{1,0:T(8,128)(2,1)S(1)} %constant_dynamic-update-slice_fusion.rest_0_), channel_id=1, source_target_pairs={{0,12},{1,13},{2,14},{3,15},{4,0},{5,1},{6,2},{7,3},{8,4},{9,5},{1... | collective-permute-start | bytes 589832 | tf_op jit(solution)/shard_map/ppermute | solution.py:383
  11.0 0.0 collective-permute-start.6
  11.0 1.0 %collective-permute-start.8 = (bf16[768,128]{1,0:T(8,128)(2,1)S(1)}, bf16[768,128]{1,0:T(8,128)(2,1)S(1)}, u32[]{:S(2)}, u32[]{:S(2)}) collective-permute-start(bf16[768,128]{1,0:T(8,128)(2,1)S(1)} %constant_dynamic-update-slice_fusion.rest_0_), channel_id=1, source_target_pairs={{0,8},{1,9},{2,10},{3,11},{4,12},{5,13},{6,14},{7,15},{8,0},{9,1},... | collective-permute-start | bytes 589832 | tf_op jit(solution)/shard_map/ppermute | solution.py:383
  12.1 1.5 %collective-permute-start.4 = (bf16[768,128]{1,0:T(8,128)(2,1)S(1)}, bf16[768,128]{1,0:T(8,128)(2,1)S(1)}, u32[]{:S(2)}, u32[]{:S(2)}) collective-permute-start(bf16[768,128]{1,0:T(8,128)(2,1)S(1)} %constant_dynamic-update-slice_fusion.rest_0_), channel_id=1, source_target_pairs={{0,2},{1,3},{2,0},{3,1},{4,6},{5,7},{6,4},{7,5},{8,10},{9,11},{10,... | collective-permute-start | bytes 589832 | tf_op jit(solution)/shard_map/ppermute | solution.py:383
  13.6 0.1 copy.12.group
  13.7 0.0 collective-permute-start.2
  13.7 2.1 %weigh.1 = (bf16[64,8192]{1,0:T(8,128)(2,1)S(1)}, bf16[64,8192]{1,0:T(8,128)(2,1)S(1)}, bf16[16,8192]{1,0:T(8,128)(2,1)S(1)}) custom-call(bf16[64,16384]{1,0:T(8,128)(2,1)S(1)} %copy-done.1, s32[64,1]{1,0:T(8,128)S(1)} %copy.12.group, f32[8,8192]{1,0:T(8,128)S(1)} %copy-done.3), custom_call_target="tpu_custom_call" | custom-call | flops 1000000000 | bytes 4000000 | tf_op jit(solution)/shard_map/weigh/pallas_call | solution.py:429
  15.9 0.0 copy-start.6
  15.9 0.0 collective-permute-done.2
  15.9 0.5 collective-permute-start.3
  16.4 0.1 maximum_convert_fusion.group
  16.5 0.0 collective-permute-done.1.rest_2_
  16.5 1.4 %collective-permute-start.5 = (bf16[768,128]{1,0:T(8,128)(2,1)S(1)}, bf16[768,128]{1,0:T(8,128)(2,1)S(1)}, u32[]{:S(2)}, u32[]{:S(2)}) collective-permute-start(bf16[768,128]{1,0:T(8,128)(2,1)S(1)} %collective-permute-done.1.rest_2_), channel_id=1, source_target_pairs={{0,2},{1,3},{2,0},{3,1},{4,6},{5,7},{6,4},{7,5},{8,10},{9,11},{10,... | collective-permute-start | bytes 589832 | tf_op jit(solution)/shard_map/ppermute | solution.py:383
  17.9 3.7 %collective-permute-done.6.rest_4_ = bf16[768,128]{1,0:T(8,128)(2,1)S(1)} collective-permute-done((bf16[768,128]{1,0:T(8,128)(2,1)S(1)}, bf16[768,128]{1,0:T(8,128)(2,1)S(1)}, u32[]{:S(2)}, u32[]{:S(2)}) %collective-permute-start.6) | collective-permute-done | bytes 196640 | tf_op jit(solution)/shard_map/ppermute | solution.py:383
  21.5 1.5 %collective-permute-start.7 = (bf16[768,128]{1,0:T(8,128)(2,1)S(1)}, bf16[768,128]{1,0:T(8,128)(2,1)S(1)}, u32[]{:S(2)}, u32[]{:S(2)}) collective-permute-start(bf16[768,128]{1,0:T(8,128)(2,1)S(1)} %collective-permute-done.6.rest_4_), channel_id=1, source_target_pairs={{0,2},{1,3},{2,0},{3,1},{4,6},{5,7},{6,4},{7,5},{8,10},{9,11},{10,... | collective-permute-start | bytes 589832 | tf_op jit(solution)/shard_map/ppermute | solution.py:383
  23.0 5.0 %collective-permute-done.8.rest_6_ = bf16[768,128]{1,0:T(8,128)(2,1)S(1)} collective-permute-done((bf16[768,128]{1,0:T(8,128)(2,1)S(1)}, bf16[768,128]{1,0:T(8,128)(2,1)S(1)}, u32[]{:S(2)}, u32[]{:S(2)}) %collective-permute-start.8) | collective-permute-done | bytes 196640 | tf_op jit(solution)/shard_map/ppermute | solution.py:383
  28.1 1.5 %collective-permute-start.9 = (bf16[768,128]{1,0:T(8,128)(2,1)S(1)}, bf16[768,128]{1,0:T(8,128)(2,1)S(1)}, u32[]{:S(2)}, u32[]{:S(2)}) collective-permute-start(bf16[768,128]{1,0:T(8,128)(2,1)S(1)} %collective-permute-done.8.rest_6_), channel_id=1, source_target_pairs={{0,2},{1,3},{2,0},{3,1},{4,6},{5,7},{6,4},{7,5},{8,10},{9,11},{10,... | collective-permute-start | bytes 589832 | tf_op jit(solution)/shard_map/ppermute | solution.py:383
  29.6 1.6 %target.1 = s32[32,128]{1,0:T(8,128)S(1)} custom-call(s32[32,128]{1,0:T(8,128)S(1)} %bitcast.16), custom_call_target="tpu_custom_call" | custom-call | flops 1000000000 | bytes 1000000 | tf_op jit(solution)/shard_map/target/pallas_call | solution.py:418
  31.2 0.1 broadcast_multiply_fusion.1
  31.2 0.1 broadcast_multiply_fusion
  31.3 1.9 %sine_multiply_fusion = (f32[64,9,128]{2,1,0:T(8,128)S(1)}, f32[64,9,128]{2,1,0:T(8,128)S(1)}) fusion(f32[128]{0:T(128)S(1)} %compare_select_fusion, f32[64,9]{1,0:T(8,128)S(1)} %broadcast_multiply_fusion, f32[9,128]{1,0:T(8,128)S(1)} %broadcast_multiply_fusion.1), kind=kLoop, calls=%fused_computation | loop fusion | flops 221184 | bytes 597248 | tf_op jit(solution)/shard_map/mul | solution.py:462
  33.2 0.0 collective-permute-done.4.rest_1_
  33.2 0.0 collective-permute-done.5.rest_3_
  33.2 0.0 collective-permute-done.7.rest_5_
  33.3 0.9 %collective-permute-done.9.rest_7_ = bf16[768,128]{1,0:T(8,128)(2,1)S(1)} collective-permute-done((bf16[768,128]{1,0:T(8,128)(2,1)S(1)}, bf16[768,128]{1,0:T(8,128)(2,1)S(1)}, u32[]{:S(2)}, u32[]{:S(2)}) %collective-permute-start.9) | collective-permute-done | bytes 196640 | tf_op jit(solution)/shard_map/ppermute | solution.py:383
  34.2 0.0 collective-permute-done.3.other
  34.2 8.2 %score.1.mine = f32[576,128]{1,0:T(8,128)S(1)} custom-call(s32[4096]{0:T(1024)S(1)} %bitcast.17, s32[1,128]{1,0:T(1,128)S(1)} %maximum_convert_fusion.group, f32[64,9,128]{2,1,0:T(8,128)S(1)} %get-tuple-element.47.cosine, f32[64,9,128]{2,1,0:T(8,128)S(1)} %get-tuple-element.46.sine, bf16[64,8192]{1,0:T(8,128)(2,1)S(1)} %get-tuple-element.30.keep, ...), custom_call_target="tpu_custom_call" | custom-call | flops 4000000000 | bytes 10000000 | tf_op jit(solution)/shard_map/score/pallas_call | solution.py:464
  42.4 0.0 copy-start
  42.5 0.1 collective-permute-start.10
  42.5 1.6 %collective-permute-done.10.theirs = f32[576,128]{1,0:T(8,128)S(1)} collective-permute-done((f32[576,128]{1,0:T(8,128)S(1)}, f32[576,128]{1,0:T(8,128)S(1)}, u32[]{:S(2)}, u32[]{:S(2)}) %collective-permute-start.10) | collective-permute-done | bytes 294944 | tf_op jit(solution)/shard_map/ppermute | solution.py:383
  44.1 7.9 %back.1 = (f32[1,128]{1,0:T(1,128)S(1)}, bf16[768,128]{1,0:T(8,128)(2,1)S(1)}, bf16[768,128]{1,0:T(8,128)(2,1)S(1)}, bf16[768,128]{1,0:T(8,128)(2,1)S(1)}, bf16[...) custom-call(s32[4096]{0:T(1024)S(1)} %bitcast.18, ...), custom_call_target="tpu_custom_call" | custom-call | flops 4000000000 | bytes 10000000 | tf_op jit(solution)/shard_map/back/pallas_call | solution.py:482
  52.0 0.0 copy-start.4
  52.0 1.6 %collective-permute-start.12 = (bf16[768,128]{1,0:T(8,128)(2,1)S(1)}, bf16[768,128]{1,0:T(8,128)(2,1)S(1)}, u32[]{:S(2)}, u32[]{:S(2)}) collective-permute-start(bf16[768,128]{1,0:T(8,128)(2,1)S(1)} %get-tuple-element.36), channel_id=1, source_target_pairs={{0,2},{1,3},{2,0},{3,1},{4,6},{5,7},{6,4},{7,5},{8,10},{9,11},{10,... | collective-permute-start | bytes 589832 | tf_op jit(solution)/shard_map/ppermute | solution.py:383
  53.6 0.0 copy-done
  53.6 0.1 copy.11
  53.7 0.6 collective-permute-start.14
  54.2 1.5 %collective-permute-start.16 = (bf16[768,128]{1,0:T(8,128)(2,1)S(1)}, bf16[768,128]{1,0:T(8,128)(2,1)S(1)}, u32[]{:S(2)}, u32[]{:S(2)}) collective-permute-start(bf16[768,128]{1,0:T(8,128)(2,1)S(1)} %get-tuple-element.40), channel_id=1, source_target_pairs={{0,2},{1,3},{2,0},{3,1},{4,6},{5,7},{6,4},{7,5},{8,10},{9,11},{10,... | collective-permute-start | bytes 589832 | tf_op jit(solution)/shard_map/ppermute | solution.py:383
  55.7 0.5 collective-permute-start.11
  56.3 3.6 %collective-permute-done.12 = bf16[768,128]{1,0:T(8,128)(2,1)S(1)} collective-permute-done((bf16[768,128]{1,0:T(8,128)(2,1)S(1)}, bf16[768,128]{1,0:T(8,128)(2,1)S(1)}, u32[]{:S(2)}, u32[]{:S(2)}) %collective-permute-start.12) | collective-permute-done | bytes 196640 | tf_op jit(solution)/shard_map/ppermute | solution.py:383
  59.8 0.1 add_convert_fusion.2
  59.9 0.1 collective-permute-start.13
  60.0 4.1 %collective-permute-done.14 = bf16[768,128]{1,0:T(8,128)(2,1)S(1)} collective-permute-done((bf16[768,128]{1,0:T(8,128)(2,1)S(1)}, bf16[768,128]{1,0:T(8,128)(2,1)S(1)}, u32[]{:S(2)}, u32[]{:S(2)}) %collective-permute-start.14) | collective-permute-done | bytes 196640 | tf_op jit(solution)/shard_map/ppermute | solution.py:383
  64.0 0.1 add_convert_fusion.1
  64.1 2.4 %collective-permute-start.15 = (bf16[768,128]{1,0:T(8,128)(2,1)S(1)}, bf16[768,128]{1,0:T(8,128)(2,1)S(1)}, u32[]{:S(2)}, u32[]{:S(2)}) collective-permute-start(bf16[768,128]{1,0:T(8,128)(2,1)S(1)} %add_convert_fusion.1), channel_id=1, source_target_pairs={{0,12},{1,13},{2,14},{3,15},{4,0},{5,1},{6,2},{7,3},{8,4},{9,5},{1... | collective-permute-start | bytes 589832 | tf_op jit(solution)/shard_map/ppermute | solution.py:383
  66.5 1.8 %collective-permute-done.16 = bf16[768,128]{1,0:T(8,128)(2,1)S(1)} collective-permute-done((bf16[768,128]{1,0:T(8,128)(2,1)S(1)}, bf16[768,128]{1,0:T(8,128)(2,1)S(1)}, u32[]{:S(2)}, u32[]{:S(2)}) %collective-permute-start.16) | collective-permute-done | bytes 196640 | tf_op jit(solution)/shard_map/ppermute | solution.py:383
  68.2 0.1 add_convert_fusion
  68.3 1.0 %collective-permute-start.17 = (bf16[768,128]{1,0:T(8,128)(2,1)S(1)}, bf16[768,128]{1,0:T(8,128)(2,1)S(1)}, u32[]{:S(2)}, u32[]{:S(2)}) collective-permute-start(bf16[768,128]{1,0:T(8,128)(2,1)S(1)} %add_convert_fusion), channel_id=1, source_target_pairs={{0,4},{1,5},{2,6},{3,7},{4,8},{5,9},{6,10},{7,11},{8,12},{9,13},{1... | collective-permute-start | bytes 589832 | tf_op jit(solution)/shard_map/ppermute | solution.py:383
  69.3 2.3 %collective-permute-done.11 = bf16[768,128]{1,0:T(8,128)(2,1)S(1)} collective-permute-done((bf16[768,128]{1,0:T(8,128)(2,1)S(1)}, bf16[768,128]{1,0:T(8,128)(2,1)S(1)}, u32[]{:S(2)}, u32[]{:S(2)}) %collective-permute-start.11) | collective-permute-done | bytes 196640 | tf_op jit(solution)/shard_map/ppermute | solution.py:383
  71.7 0.1 convert_add_fusion
  71.7 0.0 collective-permute-done.13
  71.7 5.4 %collective-permute-done.15 = bf16[768,128]{1,0:T(8,128)(2,1)S(1)} collective-permute-done((bf16[768,128]{1,0:T(8,128)(2,1)S(1)}, bf16[768,128]{1,0:T(8,128)(2,1)S(1)}, u32[]{:S(2)}, u32[]{:S(2)}) %collective-permute-start.15) | collective-permute-done | bytes 196640 | tf_op jit(solution)/shard_map/ppermute | solution.py:383
  77.1 0.0 collective-permute-done.17
  77.1 0.1 fusion.2
  77.2 0.0 copy-start.2
  77.2 0.1 collective-permute-start.18
  77.3 0.5 slice_bitcast_fusion
  77.8 1.0 %own_half.1 = (f32[384,256]{1,0:T(8,128)S(1)}, bf16[1024,384]{1,0:T(8,128)(2,1)S(1)}) custom-call(f32[8,384]{1,0:T(8,128)S(1)} %bitcast.14, f32[384,8]{1,0:T(8,128)S(1)} %copy-done, bf16[8,128,128]{2,1,0:T(8,128)(2,1)S(1)} %copy-done.4, f32[384,128]{1,0:T(8,128)S(1)} %get-tuple-element.45.keep), custom_call_target="tpu_custom_call" | custom-call | flops 1000000000 | bytes 2000000 | tf_op jit(solution)/shard_map/own_half/pallas_call | solution.py:511
  78.8 0.0 collective-permute-done.18.other
  78.8 2.7 %adjoint.1 = f32[1024,256]{1,0:T(8,128)} custom-call(f32[384,8]{1,0:T(8,128)S(1)} %copy-done, bf16[1024,256]{1,0:T(8,128)(2,1)S(1)} %copy-done.2, bf16[8,128,128]{2,1,0:T(8,128)(2,1)S(1)} %copy-done.4, f32[384,256]{1,0:T(8,128)S(1)} %get-tuple-element.41.half, bf16[1024,384]{1,0:T(8,128)(2,1)S(1)} %get-tuple-element.42.spread, ...), custom_call_target="tpu_custom_call" | custom-call | flops 1000000000 | bytes 2000000 | tf_op jit(solution)/shard_map/adjoint/pallas_call | solution.py:520
  (16 shorter events, 0.1 us)
Async XLA Ops:
  0.6 12.9 %copy-start.7 = (s32[64]{0:T(128)S(1)}, s32[64]{0:T(128)}, u32[]{:S(2)}) copy-start(s32[64]{0:T(128)} %param.10) | copy-start | bytes 772
  0.6 13.1 %copy-start.1 = (bf16[64,16384]{1,0:T(8,128)(2,1)S(1)}, bf16[64,16384]{1,0:T(8,128)(2,1)}, u32[]{:S(2)}) copy-start(bf16[64,16384]{1,0:T(8,128)(2,1)} %images) | copy-start | bytes 6291460
  0.7 13.1 %copy-start.3 = (f32[8,8192]{1,0:T(8,128)S(1)}, f32[8,8192]{1,0:T(8,128)}, u32[]{:S(2)}) copy-start(f32[8,8192]{1,0:T(8,128)} %ctf.1) | copy-start | bytes 786436
  4.3 25.2 %copy-start.5 = (s32[4096,1]{0,1:T(1,128)S(1)}, s32[4096,1]{0,1:T(1,128)}, u32[]{:S(2)}) copy-start(s32[4096,1]{0,1:T(1,128)} %param.13) | copy-start | bytes 49156
  4.3 1.7 %collective-permute-start = (bf16[384,128]{1,0:T(8,128)(2,1)}, bf16[384,128]{1,0:T(8,128)(2,1)S(1)}, u32[]{:S(2)}, u32[]{:S(2)}) collective-permute-start(bf16[384,128]{1,0:T(8,128)(2,1)} %get-tuple-element.25), channel_id=1, source_target_pairs={{0,1},{1,0},{2,3},{3,2},{4,5},{5,4},{6,7},{7,6},{8,9},{9,8},{10,11... | collective-permute-start | bytes 294920 | tf_op jit(solution)/shard_map/ppermute | solution.py:383
  6.0 10.5 %collective-permute-start.1 = (bf16[768,128]{1,0:T(8,128)(2,1)S(1)}, bf16[768,128]{1,0:T(8,128)(2,1)S(1)}, u32[]{:S(2)}, u32[]{:S(2)}) collective-permute-start(bf16[768,128]{1,0:T(8,128)(2,1)S(1)} %constant_dynamic-update-slice_fusion.rest_0_), channel_id=1, source_target_pairs={{0,12},{1,13},{2,14},{3,15},{4,0},{5,1},{6,2},{7,3},{8,4},{9,5},{1... | collective-permute-start | bytes 589832 | tf_op jit(solution)/shard_map/ppermute | solution.py:383
  11.0 10.5 %collective-permute-start.6 = (bf16[768,128]{1,0:T(8,128)(2,1)S(1)}, bf16[768,128]{1,0:T(8,128)(2,1)S(1)}, u32[]{:S(2)}, u32[]{:S(2)}) collective-permute-start(bf16[768,128]{1,0:T(8,128)(2,1)S(1)} %constant_dynamic-update-slice_fusion.rest_0_), channel_id=1, source_target_pairs={{0,4},{1,5},{2,6},{3,7},{4,8},{5,9},{6,10},{7,11},{8,12},{9,13},{1... | collective-permute-start | bytes 589832 | tf_op jit(solution)/shard_map/ppermute | solution.py:383
  11.0 17.0 %collective-permute-start.8 = (bf16[768,128]{1,0:T(8,128)(2,1)S(1)}, bf16[768,128]{1,0:T(8,128)(2,1)S(1)}, u32[]{:S(2)}, u32[]{:S(2)}) collective-permute-start(bf16[768,128]{1,0:T(8,128)(2,1)S(1)} %constant_dynamic-update-slice_fusion.rest_0_), channel_id=1, source_target_pairs={{0,8},{1,9},{2,10},{3,11},{4,12},{5,13},{6,14},{7,15},{8,0},{9,1},... | collective-permute-start | bytes 589832 | tf_op jit(solution)/shard_map/ppermute | solution.py:383
  12.1 21.2 %collective-permute-start.4 = (bf16[768,128]{1,0:T(8,128)(2,1)S(1)}, bf16[768,128]{1,0:T(8,128)(2,1)S(1)}, u32[]{:S(2)}, u32[]{:S(2)}) collective-permute-start(bf16[768,128]{1,0:T(8,128)(2,1)S(1)} %constant_dynamic-update-slice_fusion.rest_0_), channel_id=1, source_target_pairs={{0,2},{1,3},{2,0},{3,1},{4,6},{5,7},{6,4},{7,5},{8,10},{9,11},{10,... | collective-permute-start | bytes 589832 | tf_op jit(solution)/shard_map/ppermute | solution.py:383
  13.7 2.2 %collective-permute-start.2 = (f32[1,64]{1,0:T(1,128)S(1)}, f32[1,64]{1,0:T(1,128)S(1)}, u32[]{:S(2)}, u32[]{:S(2)}) collective-permute-start(f32[1,64]{1,0:T(1,128)S(1)} %convert_bitcast_fusion.2), channel_id=1, source_target_pairs={{0,1},{1,0},{2,3},{3,2},{4,5},{5,4},{6,7},{7,6},{8,9},{9,8},{10,11... | collective-permute-start | bytes 776 | tf_op jit(solution)/shard_map/ppermute | solution.py:383
  15.9 15.3 %copy-start.6 = (s32[9,2]{0,1:T(2,128)S(1)}, s32[9,2]{0,1:T(2,128)}, u32[]{:S(2)}) copy-start(s32[9,2]{0,1:T(2,128)} %param.11) | copy-start | bytes 220
  15.9 18.3 %collective-permute-start.3 = (bf16[64,8192]{1,0:T(8,128)(2,1)S(1)}, bf16[64,8192]{1,0:T(8,128)(2,1)S(1)}, u32[]{:S(2)}, u32[]{:S(2)}) collective-permute-start(bf16[64,8192]{1,0:T(8,128)(2,1)S(1)} %get-tuple-element.31), channel_id=1, source_target_pairs={{0,1},{1,0},{2,3},{3,2},{4,5},{5,4},{6,7},{7,6},{8,9},{9,8},{10,11... | collective-permute-start | bytes 3145736 | tf_op jit(solution)/shard_map/ppermute | solution.py:383
  16.5 16.7 %collective-permute-start.5 = (bf16[768,128]{1,0:T(8,128)(2,1)S(1)}, bf16[768,128]{1,0:T(8,128)(2,1)S(1)}, u32[]{:S(2)}, u32[]{:S(2)}) collective-permute-start(bf16[768,128]{1,0:T(8,128)(2,1)S(1)} %collective-permute-done.1.rest_2_), channel_id=1, source_target_pairs={{0,2},{1,3},{2,0},{3,1},{4,6},{5,7},{6,4},{7,5},{8,10},{9,11},{10,... | collective-permute-start | bytes 589832 | tf_op jit(solution)/shard_map/ppermute | solution.py:383
  21.5 11.7 %collective-permute-start.7 = (bf16[768,128]{1,0:T(8,128)(2,1)S(1)}, bf16[768,128]{1,0:T(8,128)(2,1)S(1)}, u32[]{:S(2)}, u32[]{:S(2)}) collective-permute-start(bf16[768,128]{1,0:T(8,128)(2,1)S(1)} %collective-permute-done.6.rest_4_), channel_id=1, source_target_pairs={{0,2},{1,3},{2,0},{3,1},{4,6},{5,7},{6,4},{7,5},{8,10},{9,11},{10,... | collective-permute-start | bytes 589832 | tf_op jit(solution)/shard_map/ppermute | solution.py:383
  28.1 6.1 %collective-permute-start.9 = (bf16[768,128]{1,0:T(8,128)(2,1)S(1)}, bf16[768,128]{1,0:T(8,128)(2,1)S(1)}, u32[]{:S(2)}, u32[]{:S(2)}) collective-permute-start(bf16[768,128]{1,0:T(8,128)(2,1)S(1)} %collective-permute-done.8.rest_6_), channel_id=1, source_target_pairs={{0,2},{1,3},{2,0},{3,1},{4,6},{5,7},{6,4},{7,5},{8,10},{9,11},{10,... | collective-permute-start | bytes 589832 | tf_op jit(solution)/shard_map/ppermute | solution.py:383
  42.4 11.2 %copy-start = (f32[384,8]{1,0:T(8,128)S(1)}, f32[384,8]{1,0:T(8,128)}, u32[]{:S(2)}) copy-start(f32[384,8]{1,0:T(8,128)} %get-tuple-element.23.slots) | copy-start | bytes 36868
  42.5 1.6 %collective-permute-start.10 = (f32[576,128]{1,0:T(8,128)S(1)}, f32[576,128]{1,0:T(8,128)S(1)}, u32[]{:S(2)}, u32[]{:S(2)}) collective-permute-start(f32[576,128]{1,0:T(8,128)S(1)} %score.1.mine), channel_id=1, source_target_pairs={{0,1},{1,0},{2,3},{3,2},{4,5},{5,4},{6,7},{7,6},{8,9},{9,8},{10,11... | collective-permute-start | bytes 884744 | tf_op jit(solution)/shard_map/ppermute | solution.py:383
  52.0 25.8 %copy-start.4 = (bf16[8,128,128]{2,1,0:T(8,128)(2,1)S(1)}, bf16[8,128,128]{2,1,0:T(8,128)(2,1)}, u32[]{:S(2)}) copy-start(bf16[8,128,128]{2,1,0:T(8,128)(2,1)} %interp.3) | copy-start | bytes 786436
  52.0 7.8 %collective-permute-start.12 = (bf16[768,128]{1,0:T(8,128)(2,1)S(1)}, bf16[768,128]{1,0:T(8,128)(2,1)S(1)}, u32[]{:S(2)}, u32[]{:S(2)}) collective-permute-start(bf16[768,128]{1,0:T(8,128)(2,1)S(1)} %get-tuple-element.36), channel_id=1, source_target_pairs={{0,2},{1,3},{2,0},{3,1},{4,6},{5,7},{6,4},{7,5},{8,10},{9,11},{10,... | collective-permute-start | bytes 589832 | tf_op jit(solution)/shard_map/ppermute | solution.py:383
  53.7 10.4 %collective-permute-start.14 = (bf16[768,128]{1,0:T(8,128)(2,1)S(1)}, bf16[768,128]{1,0:T(8,128)(2,1)S(1)}, u32[]{:S(2)}, u32[]{:S(2)}) collective-permute-start(bf16[768,128]{1,0:T(8,128)(2,1)S(1)} %get-tuple-element.38), channel_id=1, source_target_pairs={{0,2},{1,3},{2,0},{3,1},{4,6},{5,7},{6,4},{7,5},{8,10},{9,11},{10,... | collective-permute-start | bytes 589832 | tf_op jit(solution)/shard_map/ppermute | solution.py:383
  54.2 14.0 %collective-permute-start.16 = (bf16[768,128]{1,0:T(8,128)(2,1)S(1)}, bf16[768,128]{1,0:T(8,128)(2,1)S(1)}, u32[]{:S(2)}, u32[]{:S(2)}) collective-permute-start(bf16[768,128]{1,0:T(8,128)(2,1)S(1)} %get-tuple-element.40), channel_id=1, source_target_pairs={{0,2},{1,3},{2,0},{3,1},{4,6},{5,7},{6,4},{7,5},{8,10},{9,11},{10,... | collective-permute-start | bytes 589832 | tf_op jit(solution)/shard_map/ppermute | solution.py:383
  55.7 15.9 %collective-permute-start.11 = (bf16[768,128]{1,0:T(8,128)(2,1)S(1)}, bf16[768,128]{1,0:T(8,128)(2,1)S(1)}, u32[]{:S(2)}, u32[]{:S(2)}) collective-permute-start(bf16[768,128]{1,0:T(8,128)(2,1)S(1)} %get-tuple-element.34), channel_id=1, source_target_pairs={{0,2},{1,3},{2,0},{3,1},{4,6},{5,7},{6,4},{7,5},{8,10},{9,11},{10,... | collective-permute-start | bytes 589832 | tf_op jit(solution)/shard_map/ppermute | solution.py:383
  59.9 11.8 %collective-permute-start.13 = (bf16[768,128]{1,0:T(8,128)(2,1)S(1)}, bf16[768,128]{1,0:T(8,128)(2,1)S(1)}, u32[]{:S(2)}, u32[]{:S(2)}) collective-permute-start(bf16[768,128]{1,0:T(8,128)(2,1)S(1)} %add_convert_fusion.2), channel_id=1, source_target_pairs={{0,8},{1,9},{2,10},{3,11},{4,12},{5,13},{6,14},{7,15},{8,0},{9,1},... | collective-permute-start | bytes 589832 | tf_op jit(solution)/shard_map/ppermute | solution.py:383
  64.1 13.0 %collective-permute-start.15 = (bf16[768,128]{1,0:T(8,128)(2,1)S(1)}, bf16[768,128]{1,0:T(8,128)(2,1)S(1)}, u32[]{:S(2)}, u32[]{:S(2)}) collective-permute-start(bf16[768,128]{1,0:T(8,128)(2,1)S(1)} %add_convert_fusion.1), channel_id=1, source_target_pairs={{0,12},{1,13},{2,14},{3,15},{4,0},{5,1},{6,2},{7,3},{8,4},{9,5},{1... | collective-permute-start | bytes 589832 | tf_op jit(solution)/shard_map/ppermute | solution.py:383
  68.3 8.8 %collective-permute-start.17 = (bf16[768,128]{1,0:T(8,128)(2,1)S(1)}, bf16[768,128]{1,0:T(8,128)(2,1)S(1)}, u32[]{:S(2)}, u32[]{:S(2)}) collective-permute-start(bf16[768,128]{1,0:T(8,128)(2,1)S(1)} %add_convert_fusion), channel_id=1, source_target_pairs={{0,4},{1,5},{2,6},{3,7},{4,8},{5,9},{6,10},{7,11},{8,12},{9,13},{1... | collective-permute-start | bytes 589832 | tf_op jit(solution)/shard_map/ppermute | solution.py:383
  77.2 1.6 %copy-start.2 = (bf16[1024,256]{1,0:T(8,128)(2,1)S(1)}, bf16[1024,256]{1,0:T(8,128)(2,1)}, u32[]{:S(2)}) copy-start(bf16[1024,256]{1,0:T(8,128)(2,1)} %volume.1) | copy-start | bytes 1572868
  77.2 1.6 %collective-permute-start.18 = (f32[384,128]{1,0:T(8,128)S(1)}, f32[384,128]{1,0:T(8,128)S(1)}, u32[]{:S(2)}, u32[]{:S(2)}) collective-permute-start(f32[384,128]{1,0:T(8,128)S(1)} %get-tuple-element.44), channel_id=1, source_target_pairs={{0,1},{1,0},{2,3},{3,2},{4,5},{5,4},{6,7},{7,6},{8,9},{9,8},{10,11... | collective-permute-start | bytes 589832 | tf_op jit(solution)/shard_map/ppermute | solution.py:383

commit v7 on v6

--- a/solution.py
+++ b/solution.py
@@ -256,7 +256,7 @@
     top = jnp.max(scores, axis=0, keepdims=True)
     exponent = jnp.exp(scores - top)
     total = jnp.sum(exponent, axis=0, keepdims=True)
-    evidence[...] = top + jnp.log(total)
+    evidence[...] = (top + jnp.log(total))[:, : evidence.shape[1]]
     weights = (exponent / total).astype(BF16)
     sublane = iota((8, BW), 0)
 
@@ -482,14 +482,14 @@
     outs = call(
         functools.partial(back_kernel, ny, rows, order),
         [SMEM] + [VMEM] * 6,
-        [struct((1, 2 * count), F32)]
+        [struct((1, count), F32)]
         + [struct((rows, BW), BF16)] * chips,
         [pltpu.VMEM((chips * rows + 16, BW), F32)],
         4 * 10**9,
         10**7,
         "back",
     )(target, partial, theirs, cosine, sine, weight_keep, weight_other)
-    evidence = outs[0][0, :count]
+    evidence = outs[0].reshape(count)
     parts = {kz: outs[1 + ny * i : 1 + ny * (i + 1)] for i, kz in enumerate(order)}
     moved = {kz: [to(parts[kz][ky], along_y(ky)) for ky in range(1, ny)] for kz in order}
     crossed = {}

time: 81.6 us -> 81.7 us (level)
  transfers between devices with their start and end apart: 19 -> 19, of which waited for: 10 -> 11; matrix products, arithmetic and copies ran while one was open for 5% -> 4% of each run, Pallas kernels for 6% -> 6%
where the time goes in v7:
time: 81.7 us; the launch traced here: 81.5 us
  waiting for transfers between devices  28.8 us (35%)
  Pallas kernels  27.6 us (34%)
  starting transfers between devices  20.7 us (25%)
  other arithmetic  2.45 us (3%)
  local copies, waits for them, and re-layouts  1.12 us (1%)
  between operations  0.86 us (1%)
    ppermute x19, waiting for transfers between devices, to(): return lax.ppermute(array, 'img', pairs)  28.8 us
    ppermute x19, starting transfers between devices, to(): return lax.ppermute(array, 'img', pairs)  20.7 us
    pallas_call x1, Pallas kernels, per_device(): call(functools.partial(back_kernel, ny, rows, order), [SMEM] + [VMEM] * 6...  8.28 us
    pallas_call x1, Pallas kernels, per_device(): call(functools.partial(score_kernel, [moves for _, moves in pieces]), [SM...  8.21 us
    pallas_call x1, Pallas kernels, per_device(): call(slice_kernel, [ANY] * 5, [struct((cap, 8), F32), struct((cap, BW), B...  3.66 us
    pallas_call x1, Pallas kernels, per_device(): call(adjoint_kernel, [VMEM] * 6, [struct(volume.shape, F32)], [pltpu.VMEM...  2.65 us
    pallas_call x1, Pallas kernels, per_device(): call(weigh_kernel, [VMEM] * 3, [struct((count, KB * BW), BF16), struct((c...  2.23 us
    mul x1, other arithmetic, per_device(): sine = jnp.sin(angles) * jnp.where(lane < HALF, -1.0, 1.0)  1.92 us
  transfers between devices with their start and end apart: 19, of which 11 were waited for; matrix products, arithmetic and copies ran while one was open for 4% of the time, Pallas kernels for 6%

profile of v7, /device:TPU:0, one launch (start us, length us, event | category | flops | bytes accessed | tf_op | source)
XLA Modules:
  0.0 81.5 jit_solution(1402119944593140890)
XLA Ops:
  0.6 0.0 copy-start.7
  0.6 0.0 copy-start.1
  0.7 0.0 copy-start.3
  0.7 3.7 %own_slices.1 = (f32[384,8]{1,0:T(8,128)}, bf16[384,128]{1,0:T(8,128)(2,1)}, bf16[384,128]{1,0:T(8,128)(2,1)}) custom-call(s32[32,128]{1,0:T(8,128)} %bitcast.14, s32[32,128]{1,0:T(8,128)} %bitcast.19, s32[32,128]{1,0:T(8,128)} %bitcast.20, bf16[1024,256]{1,0:T(8,128)(2,1)} %volume.1, bf16[8,128,128]{2,1,0:T(8,128)(2,1)} %interp.3), custom_call_target="tpu_custom_call" | custom-call | flops 1000000000 | bytes 1000000 | tf_op jit(solution)/shard_map/own_slices/pallas_call | solution.py:387
  4.3 0.0 copy-start.5
  4.3 0.5 collective-permute-start
  4.9 0.9 %constant_dynamic-update-slice_fusion.1 = bf16[768,128]{1,0:T(8,128)(2,1)S(1)} fusion(bf16[384,128]{1,0:T(8,128)(2,1)} %get-tuple-element.24), kind=kLoop, calls=%fused_computation.15 | loop fusion | bytes 196608
  5.8 0.2 collective-permute-done
  6.0 5.0 %collective-permute-start.1 = (bf16[768,128]{1,0:T(8,128)(2,1)S(1)}, bf16[768,128]{1,0:T(8,128)(2,1)S(1)}, u32[]{:S(2)}, u32[]{:S(2)}) collective-permute-start(bf16[768,128]{1,0:T(8,128)(2,1)S(1)} %constant_dynamic-update-slice_fusion.rest_0_), channel_id=1, source_target_pairs={{0,12},{1,13},{2,14},{3,15},{4,0},{5,1},{6,2},{7,3},{8,4},{9,5},{1... | collective-permute-start | bytes 589832 | tf_op jit(solution)/shard_map/ppermute | solution.py:383
  11.0 0.0 collective-permute-start.6
  11.0 1.0 %collective-permute-start.8 = (bf16[768,128]{1,0:T(8,128)(2,1)S(1)}, bf16[768,128]{1,0:T(8,128)(2,1)S(1)}, u32[]{:S(2)}, u32[]{:S(2)}) collective-permute-start(bf16[768,128]{1,0:T(8,128)(2,1)S(1)} %constant_dynamic-update-slice_fusion.rest_0_), channel_id=1, source_target_pairs={{0,8},{1,9},{2,10},{3,11},{4,12},{5,13},{6,14},{7,15},{8,0},{9,1},... | collective-permute-start | bytes 589832 | tf_op jit(solution)/shard_map/ppermute | solution.py:383
  12.1 1.5 %collective-permute-start.4 = (bf16[768,128]{1,0:T(8,128)(2,1)S(1)}, bf16[768,128]{1,0:T(8,128)(2,1)S(1)}, u32[]{:S(2)}, u32[]{:S(2)}) collective-permute-start(bf16[768,128]{1,0:T(8,128)(2,1)S(1)} %constant_dynamic-update-slice_fusion.rest_0_), channel_id=1, source_target_pairs={{0,2},{1,3},{2,0},{3,1},{4,6},{5,7},{6,4},{7,5},{8,10},{9,11},{10,... | collective-permute-start | bytes 589832 | tf_op jit(solution)/shard_map/ppermute | solution.py:383
  13.6 0.0 copy-done.7
  13.6 0.1 copy.12.group
  13.7 0.0 collective-permute-start.2
  13.7 0.0 copy-done.1
  13.7 2.2 %weigh.1 = (bf16[64,8192]{1,0:T(8,128)(2,1)S(1)}, bf16[64,8192]{1,0:T(8,128)(2,1)S(1)}, bf16[16,8192]{1,0:T(8,128)(2,1)S(1)}) custom-call(bf16[64,16384]{1,0:T(8,128)(2,1)S(1)} %copy-done.1, s32[64,1]{1,0:T(8,128)S(1)} %copy.12.group, f32[8,8192]{1,0:T(8,128)S(1)} %copy-done.3), custom_call_target="tpu_custom_call" | custom-call | flops 1000000000 | bytes 4000000 | tf_op jit(solution)/shard_map/weigh/pallas_call | solution.py:429
  16.0 0.0 copy-start.6
  16.0 0.0 collective-permute-done.2
  16.0 0.5 collective-permute-start.3
  16.5 0.1 maximum_convert_fusion.group
  16.6 0.0 collective-permute-done.1.rest_2_
  16.6 1.3 %collective-permute-start.5 = (bf16[768,128]{1,0:T(8,128)(2,1)S(1)}, bf16[768,128]{1,0:T(8,128)(2,1)S(1)}, u32[]{:S(2)}, u32[]{:S(2)}) collective-permute-start(bf16[768,128]{1,0:T(8,128)(2,1)S(1)} %collective-permute-done.1.rest_2_), channel_id=1, source_target_pairs={{0,2},{1,3},{2,0},{3,1},{4,6},{5,7},{6,4},{7,5},{8,10},{9,11},{10,... | collective-permute-start | bytes 589832 | tf_op jit(solution)/shard_map/ppermute | solution.py:383
  17.9 3.7 %collective-permute-done.6.rest_4_ = bf16[768,128]{1,0:T(8,128)(2,1)S(1)} collective-permute-done((bf16[768,128]{1,0:T(8,128)(2,1)S(1)}, bf16[768,128]{1,0:T(8,128)(2,1)S(1)}, u32[]{:S(2)}, u32[]{:S(2)}) %collective-permute-start.6) | collective-permute-done | bytes 196640 | tf_op jit(solution)/shard_map/ppermute | solution.py:383
  21.5 1.5 %collective-permute-start.7 = (bf16[768,128]{1,0:T(8,128)(2,1)S(1)}, bf16[768,128]{1,0:T(8,128)(2,1)S(1)}, u32[]{:S(2)}, u32[]{:S(2)}) collective-permute-start(bf16[768,128]{1,0:T(8,128)(2,1)S(1)} %collective-permute-done.6.rest_4_), channel_id=1, source_target_pairs={{0,2},{1,3},{2,0},{3,1},{4,6},{5,7},{6,4},{7,5},{8,10},{9,11},{10,... | collective-permute-start | bytes 589832 | tf_op jit(solution)/shard_map/ppermute | solution.py:383
  23.0 5.0 %collective-permute-done.8.rest_6_ = bf16[768,128]{1,0:T(8,128)(2,1)S(1)} collective-permute-done((bf16[768,128]{1,0:T(8,128)(2,1)S(1)}, bf16[768,128]{1,0:T(8,128)(2,1)S(1)}, u32[]{:S(2)}, u32[]{:S(2)}) %collective-permute-start.8) | collective-permute-done | bytes 196640 | tf_op jit(solution)/shard_map/ppermute | solution.py:383
  28.1 1.5 %collective-permute-start.9 = (bf16[768,128]{1,0:T(8,128)(2,1)S(1)}, bf16[768,128]{1,0:T(8,128)(2,1)S(1)}, u32[]{:S(2)}, u32[]{:S(2)}) collective-permute-start(bf16[768,128]{1,0:T(8,128)(2,1)S(1)} %collective-permute-done.8.rest_6_), channel_id=1, source_target_pairs={{0,2},{1,3},{2,0},{3,1},{4,6},{5,7},{6,4},{7,5},{8,10},{9,11},{10,... | collective-permute-start | bytes 589832 | tf_op jit(solution)/shard_map/ppermute | solution.py:383
  29.6 1.6 %target.1 = s32[32,128]{1,0:T(8,128)S(1)} custom-call(s32[32,128]{1,0:T(8,128)S(1)} %bitcast.15), custom_call_target="tpu_custom_call" | custom-call | flops 1000000000 | bytes 1000000 | tf_op jit(solution)/shard_map/target/pallas_call | solution.py:418
  31.2 0.1 broadcast_multiply_fusion.1
  31.2 0.1 broadcast_multiply_fusion
  31.3 1.9 %sine_multiply_fusion = (f32[64,9,128]{2,1,0:T(8,128)S(1)}, f32[64,9,128]{2,1,0:T(8,128)S(1)}) fusion(f32[128]{0:T(128)S(1)} %compare_select_fusion, f32[64,9]{1,0:T(8,128)S(1)} %broadcast_multiply_fusion, f32[9,128]{1,0:T(8,128)S(1)} %broadcast_multiply_fusion.1), kind=kLoop, calls=%fused_computation | loop fusion | flops 221184 | bytes 597248 | tf_op jit(solution)/shard_map/mul | solution.py:462
  33.2 0.0 collective-permute-done.4.rest_1_
  33.2 0.0 collective-permute-done.5.rest_3_
  33.2 0.0 collective-permute-done.7.rest_5_
  33.3 0.9 %collective-permute-done.9.rest_7_ = bf16[768,128]{1,0:T(8,128)(2,1)S(1)} collective-permute-done((bf16[768,128]{1,0:T(8,128)(2,1)S(1)}, bf16[768,128]{1,0:T(8,128)(2,1)S(1)}, u32[]{:S(2)}, u32[]{:S(2)}) %collective-permute-start.9) | collective-permute-done | bytes 196640 | tf_op jit(solution)/shard_map/ppermute | solution.py:383
  34.2 0.0 collective-permute-done.3.other
  34.2 8.2 %score.1.mine = f32[576,128]{1,0:T(8,128)S(1)} custom-call(s32[4096]{0:T(1024)S(1)} %bitcast.16, s32[1,128]{1,0:T(1,128)S(1)} %maximum_convert_fusion.group, f32[64,9,128]{2,1,0:T(8,128)S(1)} %get-tuple-element.47.cosine, f32[64,9,128]{2,1,0:T(8,128)S(1)} %get-tuple-element.46.sine, bf16[64,8192]{1,0:T(8,128)(2,1)S(1)} %get-tuple-element.30.keep, ...), custom_call_target="tpu_custom_call" | custom-call | flops 4000000000 | bytes 10000000 | tf_op jit(solution)/shard_map/score/pallas_call | solution.py:464
  42.4 0.1 collective-permute-start.10
  42.5 1.6 %collective-permute-done.10.theirs = f32[576,128]{1,0:T(8,128)S(1)} collective-permute-done((f32[576,128]{1,0:T(8,128)S(1)}, f32[576,128]{1,0:T(8,128)S(1)}, u32[]{:S(2)}, u32[]{:S(2)}) %collective-permute-start.10) | collective-permute-done | bytes 294944 | tf_op jit(solution)/shard_map/ppermute | solution.py:383
  44.0 8.3 %back.1 = (f32[1,64]{1,0:T(1,128)}, bf16[768,128]{1,0:T(8,128)(2,1)S(1)}, bf16[768,128]{1,0:T(8,128)(2,1)S(1)}, bf16[768,128]{1,0:T(8,128)(2,1)S(1)}, bf16[768,1...) custom-call(s32[4096]{0:T(1024)S(1)} %bitcast.17, ...), custom_call_target="tpu_custom_call" | custom-call | flops 4000000000 | bytes 10000000 | tf_op jit(solution)/shard_map/back/pallas_call | solution.py:482
  52.3 1.5 %collective-permute-start.12 = (bf16[768,128]{1,0:T(8,128)(2,1)S(1)}, bf16[768,128]{1,0:T(8,128)(2,1)S(1)}, u32[]{:S(2)}, u32[]{:S(2)}) collective-permute-start(bf16[768,128]{1,0:T(8,128)(2,1)S(1)} %get-tuple-element.36), channel_id=1, source_target_pairs={{0,2},{1,3},{2,0},{3,1},{4,6},{5,7},{6,4},{7,5},{8,10},{9,11},{10,... | collective-permute-start | bytes 589832 | tf_op jit(solution)/shard_map/ppermute | solution.py:383
  53.9 0.5 collective-permute-start.14
  54.4 1.5 %collective-permute-start.16 = (bf16[768,128]{1,0:T(8,128)(2,1)S(1)}, bf16[768,128]{1,0:T(8,128)(2,1)S(1)}, u32[]{:S(2)}, u32[]{:S(2)}) collective-permute-start(bf16[768,128]{1,0:T(8,128)(2,1)S(1)} %get-tuple-element.40), channel_id=1, source_target_pairs={{0,2},{1,3},{2,0},{3,1},{4,6},{5,7},{6,4},{7,5},{8,10},{9,11},{10,... | collective-permute-start | bytes 589832 | tf_op jit(solution)/shard_map/ppermute | solution.py:383
  55.9 0.5 collective-permute-start.11
  56.4 3.7 %collective-permute-done.12 = bf16[768,128]{1,0:T(8,128)(2,1)S(1)} collective-permute-done((bf16[768,128]{1,0:T(8,128)(2,1)S(1)}, bf16[768,128]{1,0:T(8,128)(2,1)S(1)}, u32[]{:S(2)}, u32[]{:S(2)}) %collective-permute-start.12) | collective-permute-done | bytes 196640 | tf_op jit(solution)/shard_map/ppermute | solution.py:383
  60.1 0.1 add_convert_fusion.2
  60.1 0.1 collective-permute-start.13
  60.2 4.1 %collective-permute-done.14 = bf16[768,128]{1,0:T(8,128)(2,1)S(1)} collective-permute-done((bf16[768,128]{1,0:T(8,128)(2,1)S(1)}, bf16[768,128]{1,0:T(8,128)(2,1)S(1)}, u32[]{:S(2)}, u32[]{:S(2)}) %collective-permute-start.14) | collective-permute-done | bytes 196640 | tf_op jit(solution)/shard_map/ppermute | solution.py:383
  64.3 0.1 add_convert_fusion.1
  64.4 2.4 %collective-permute-start.15 = (bf16[768,128]{1,0:T(8,128)(2,1)S(1)}, bf16[768,128]{1,0:T(8,128)(2,1)S(1)}, u32[]{:S(2)}, u32[]{:S(2)}) collective-permute-start(bf16[768,128]{1,0:T(8,128)(2,1)S(1)} %add_convert_fusion.1), channel_id=1, source_target_pairs={{0,12},{1,13},{2,14},{3,15},{4,0},{5,1},{6,2},{7,3},{8,4},{9,5},{1... | collective-permute-start | bytes 589832 | tf_op jit(solution)/shard_map/ppermute | solution.py:383
  66.7 1.8 %collective-permute-done.16 = bf16[768,128]{1,0:T(8,128)(2,1)S(1)} collective-permute-done((bf16[768,128]{1,0:T(8,128)(2,1)S(1)}, bf16[768,128]{1,0:T(8,128)(2,1)S(1)}, u32[]{:S(2)}, u32[]{:S(2)}) %collective-permute-start.16) | collective-permute-done | bytes 196640 | tf_op jit(solution)/shard_map/ppermute | solution.py:383
  68.5 0.1 add_convert_fusion
  68.6 1.1 %collective-permute-start.17 = (bf16[768,128]{1,0:T(8,128)(2,1)S(1)}, bf16[768,128]{1,0:T(8,128)(2,1)S(1)}, u32[]{:S(2)}, u32[]{:S(2)}) collective-permute-start(bf16[768,128]{1,0:T(8,128)(2,1)S(1)} %add_convert_fusion), channel_id=1, source_target_pairs={{0,4},{1,5},{2,6},{3,7},{4,8},{5,9},{6,10},{7,11},{8,12},{9,13},{1... | collective-permute-start | bytes 589832 | tf_op jit(solution)/shard_map/ppermute | solution.py:383
  69.7 2.2 %collective-permute-done.11 = bf16[768,128]{1,0:T(8,128)(2,1)S(1)} collective-permute-done((bf16[768,128]{1,0:T(8,128)(2,1)S(1)}, bf16[768,128]{1,0:T(8,128)(2,1)S(1)}, u32[]{:S(2)}, u32[]{:S(2)}) %collective-permute-start.11) | collective-permute-done | bytes 196640 | tf_op jit(solution)/shard_map/ppermute | solution.py:383
  72.0 0.0 collective-permute-done.13
  72.0 5.3 %collective-permute-done.15 = bf16[768,128]{1,0:T(8,128)(2,1)S(1)} collective-permute-done((bf16[768,128]{1,0:T(8,128)(2,1)S(1)}, bf16[768,128]{1,0:T(8,128)(2,1)S(1)}, u32[]{:S(2)}, u32[]{:S(2)}) %collective-permute-start.15) | collective-permute-done | bytes 196640 | tf_op jit(solution)/shard_map/ppermute | solution.py:383
  77.3 0.0 collective-permute-done.17
  77.3 0.1 fusion.2
  77.3 0.0 copy-start.2
  77.3 0.1 collective-permute-start.18
  77.4 0.1 copy.11
  77.5 1.0 %own_half.1 = (f32[384,256]{1,0:T(8,128)S(1)}, bf16[1024,384]{1,0:T(8,128)(2,1)S(1)}) custom-call(f32[8,384]{1,0:T(8,128)S(1)} %bitcast.13, f32[384,8]{1,0:T(8,128)S(1)} %copy-done, bf16[8,128,128]{2,1,0:T(8,128)(2,1)S(1)} %copy-done.4, f32[384,128]{1,0:T(8,128)S(1)} %get-tuple-element.45.keep), custom_call_target="tpu_custom_call" | custom-call | flops 1000000000 | bytes 2000000 | tf_op jit(solution)/shard_map/own_half/pallas_call | solution.py:511
  78.5 0.3 collective-permute-done.18.other
  78.9 2.7 %adjoint.1 = f32[1024,256]{1,0:T(8,128)} custom-call(f32[384,8]{1,0:T(8,128)S(1)} %copy-done, bf16[1024,256]{1,0:T(8,128)(2,1)S(1)} %copy-done.2, bf16[8,128,128]{2,1,0:T(8,128)(2,1)S(1)} %copy-done.4, f32[384,256]{1,0:T(8,128)S(1)} %get-tuple-element.41.half, bf16[1024,384]{1,0:T(8,128)(2,1)S(1)} %get-tuple-element.42.spread, ...), custom_call_target="tpu_custom_call" | custom-call | flops 1000000000 | bytes 2000000 | tf_op jit(solution)/shard_map/adjoint/pallas_call | solution.py:520
  (15 shorter events, 0.1 us)
Async XLA Ops:
  0.6 12.9 %copy-start.7 = (s32[64]{0:T(128)S(1)}, s32[64]{0:T(128)}, u32[]{:S(2)}) copy-start(s32[64]{0:T(128)} %param.10) | copy-start | bytes 772
  0.6 13.1 %copy-start.1 = (bf16[64,16384]{1,0:T(8,128)(2,1)S(1)}, bf16[64,16384]{1,0:T(8,128)(2,1)}, u32[]{:S(2)}) copy-start(bf16[64,16384]{1,0:T(8,128)(2,1)} %images) | copy-start | bytes 6291460
  0.7 13.1 %copy-start.3 = (f32[8,8192]{1,0:T(8,128)S(1)}, f32[8,8192]{1,0:T(8,128)}, u32[]{:S(2)}) copy-start(f32[8,8192]{1,0:T(8,128)} %ctf.1) | copy-start | bytes 786436
  4.3 25.2 %copy-start.5 = (s32[4096,1]{0,1:T(1,128)S(1)}, s32[4096,1]{0,1:T(1,128)}, u32[]{:S(2)}) copy-start(s32[4096,1]{0,1:T(1,128)} %param.13) | copy-start | bytes 49156
  4.3 1.7 %collective-permute-start = (bf16[384,128]{1,0:T(8,128)(2,1)}, bf16[384,128]{1,0:T(8,128)(2,1)S(1)}, u32[]{:S(2)}, u32[]{:S(2)}) collective-permute-start(bf16[384,128]{1,0:T(8,128)(2,1)} %get-tuple-element.25), channel_id=1, source_target_pairs={{0,1},{1,0},{2,3},{3,2},{4,5},{5,4},{6,7},{7,6},{8,9},{9,8},{10,11... | collective-permute-start | bytes 294920 | tf_op jit(solution)/shard_map/ppermute | solution.py:383
  6.0 10.6 %collective-permute-start.1 = (bf16[768,128]{1,0:T(8,128)(2,1)S(1)}, bf16[768,128]{1,0:T(8,128)(2,1)S(1)}, u32[]{:S(2)}, u32[]{:S(2)}) collective-permute-start(bf16[768,128]{1,0:T(8,128)(2,1)S(1)} %constant_dynamic-update-slice_fusion.rest_0_), channel_id=1, source_target_pairs={{0,12},{1,13},{2,14},{3,15},{4,0},{5,1},{6,2},{7,3},{8,4},{9,5},{1... | collective-permute-start | bytes 589832 | tf_op jit(solution)/shard_map/ppermute | solution.py:383
  11.0 10.5 %collective-permute-start.6 = (bf16[768,128]{1,0:T(8,128)(2,1)S(1)}, bf16[768,128]{1,0:T(8,128)(2,1)S(1)}, u32[]{:S(2)}, u32[]{:S(2)}) collective-permute-start(bf16[768,128]{1,0:T(8,128)(2,1)S(1)} %constant_dynamic-update-slice_fusion.rest_0_), channel_id=1, source_target_pairs={{0,4},{1,5},{2,6},{3,7},{4,8},{5,9},{6,10},{7,11},{8,12},{9,13},{1... | collective-permute-start | bytes 589832 | tf_op jit(solution)/shard_map/ppermute | solution.py:383
  11.0 17.0 %collective-permute-start.8 = (bf16[768,128]{1,0:T(8,128)(2,1)S(1)}, bf16[768,128]{1,0:T(8,128)(2,1)S(1)}, u32[]{:S(2)}, u32[]{:S(2)}) collective-permute-start(bf16[768,128]{1,0:T(8,128)(2,1)S(1)} %constant_dynamic-update-slice_fusion.rest_0_), channel_id=1, source_target_pairs={{0,8},{1,9},{2,10},{3,11},{4,12},{5,13},{6,14},{7,15},{8,0},{9,1},... | collective-permute-start | bytes 589832 | tf_op jit(solution)/shard_map/ppermute | solution.py:383
  12.1 21.2 %collective-permute-start.4 = (bf16[768,128]{1,0:T(8,128)(2,1)S(1)}, bf16[768,128]{1,0:T(8,128)(2,1)S(1)}, u32[]{:S(2)}, u32[]{:S(2)}) collective-permute-start(bf16[768,128]{1,0:T(8,128)(2,1)S(1)} %constant_dynamic-update-slice_fusion.rest_0_), channel_id=1, source_target_pairs={{0,2},{1,3},{2,0},{3,1},{4,6},{5,7},{6,4},{7,5},{8,10},{9,11},{10,... | collective-permute-start | bytes 589832 | tf_op jit(solution)/shard_map/ppermute | solution.py:383
  13.7 2.3 %collective-permute-start.2 = (f32[1,64]{1,0:T(1,128)S(1)}, f32[1,64]{1,0:T(1,128)S(1)}, u32[]{:S(2)}, u32[]{:S(2)}) collective-permute-start(f32[1,64]{1,0:T(1,128)S(1)} %convert_bitcast_fusion.2), channel_id=1, source_target_pairs={{0,1},{1,0},{2,3},{3,2},{4,5},{5,4},{6,7},{7,6},{8,9},{9,8},{10,11... | collective-permute-start | bytes 776 | tf_op jit(solution)/shard_map/ppermute | solution.py:383
  16.0 15.2 %copy-start.6 = (s32[9,2]{0,1:T(2,128)S(1)}, s32[9,2]{0,1:T(2,128)}, u32[]{:S(2)}) copy-start(s32[9,2]{0,1:T(2,128)} %param.11) | copy-start | bytes 220
  16.0 18.2 %collective-permute-start.3 = (bf16[64,8192]{1,0:T(8,128)(2,1)S(1)}, bf16[64,8192]{1,0:T(8,128)(2,1)S(1)}, u32[]{:S(2)}, u32[]{:S(2)}) collective-permute-start(bf16[64,8192]{1,0:T(8,128)(2,1)S(1)} %get-tuple-element.31), channel_id=1, source_target_pairs={{0,1},{1,0},{2,3},{3,2},{4,5},{5,4},{6,7},{7,6},{8,9},{9,8},{10,11... | collective-permute-start | bytes 3145736 | tf_op jit(solution)/shard_map/ppermute | solution.py:383
  16.6 16.6 %collective-permute-start.5 = (bf16[768,128]{1,0:T(8,128)(2,1)S(1)}, bf16[768,128]{1,0:T(8,128)(2,1)S(1)}, u32[]{:S(2)}, u32[]{:S(2)}) collective-permute-start(bf16[768,128]{1,0:T(8,128)(2,1)S(1)} %collective-permute-done.1.rest_2_), channel_id=1, source_target_pairs={{0,2},{1,3},{2,0},{3,1},{4,6},{5,7},{6,4},{7,5},{8,10},{9,11},{10,... | collective-permute-start | bytes 589832 | tf_op jit(solution)/shard_map/ppermute | solution.py:383
  21.5 11.7 %collective-permute-start.7 = (bf16[768,128]{1,0:T(8,128)(2,1)S(1)}, bf16[768,128]{1,0:T(8,128)(2,1)S(1)}, u32[]{:S(2)}, u32[]{:S(2)}) collective-permute-start(bf16[768,128]{1,0:T(8,128)(2,1)S(1)} %collective-permute-done.6.rest_4_), channel_id=1, source_target_pairs={{0,2},{1,3},{2,0},{3,1},{4,6},{5,7},{6,4},{7,5},{8,10},{9,11},{10,... | collective-permute-start | bytes 589832 | tf_op jit(solution)/shard_map/ppermute | solution.py:383
  28.1 6.1 %collective-permute-start.9 = (bf16[768,128]{1,0:T(8,128)(2,1)S(1)}, bf16[768,128]{1,0:T(8,128)(2,1)S(1)}, u32[]{:S(2)}, u32[]{:S(2)}) collective-permute-start(bf16[768,128]{1,0:T(8,128)(2,1)S(1)} %collective-permute-done.8.rest_6_), channel_id=1, source_target_pairs={{0,2},{1,3},{2,0},{3,1},{4,6},{5,7},{6,4},{7,5},{8,10},{9,11},{10,... | collective-permute-start | bytes 589832 | tf_op jit(solution)/shard_map/ppermute | solution.py:383
  42.4 1.6 %collective-permute-start.10 = (f32[576,128]{1,0:T(8,128)S(1)}, f32[576,128]{1,0:T(8,128)S(1)}, u32[]{:S(2)}, u32[]{:S(2)}) collective-permute-start(f32[576,128]{1,0:T(8,128)S(1)} %score.1.mine), channel_id=1, source_target_pairs={{0,1},{1,0},{2,3},{3,2},{4,5},{5,4},{6,7},{7,6},{8,9},{9,8},{10,11... | collective-permute-start | bytes 884744 | tf_op jit(solution)/shard_map/ppermute | solution.py:383
  52.3 25.1 %copy-start = (f32[384,8]{1,0:T(8,128)S(1)}, f32[384,8]{1,0:T(8,128)}, u32[]{:S(2)}) copy-start(f32[384,8]{1,0:T(8,128)} %get-tuple-element.23.slots) | copy-start | bytes 36868
  52.3 25.2 %copy-start.4 = (bf16[8,128,128]{2,1,0:T(8,128)(2,1)S(1)}, bf16[8,128,128]{2,1,0:T(8,128)(2,1)}, u32[]{:S(2)}) copy-start(bf16[8,128,128]{2,1,0:T(8,128)(2,1)} %interp.3) | copy-start | bytes 786436
  52.3 7.7 %collective-permute-start.12 = (bf16[768,128]{1,0:T(8,128)(2,1)S(1)}, bf16[768,128]{1,0:T(8,128)(2,1)S(1)}, u32[]{:S(2)}, u32[]{:S(2)}) collective-permute-start(bf16[768,128]{1,0:T(8,128)(2,1)S(1)} %get-tuple-element.36), channel_id=1, source_target_pairs={{0,2},{1,3},{2,0},{3,1},{4,6},{5,7},{6,4},{7,5},{8,10},{9,11},{10,... | collective-permute-start | bytes 589832 | tf_op jit(solution)/shard_map/ppermute | solution.py:383
  53.9 10.4 %collective-permute-start.14 = (bf16[768,128]{1,0:T(8,128)(2,1)S(1)}, bf16[768,128]{1,0:T(8,128)(2,1)S(1)}, u32[]{:S(2)}, u32[]{:S(2)}) collective-permute-start(bf16[768,128]{1,0:T(8,128)(2,1)S(1)} %get-tuple-element.38), channel_id=1, source_target_pairs={{0,2},{1,3},{2,0},{3,1},{4,6},{5,7},{6,4},{7,5},{8,10},{9,11},{10,... | collective-permute-start | bytes 589832 | tf_op jit(solution)/shard_map/ppermute | solution.py:383
  54.4 14.1 %collective-permute-start.16 = (bf16[768,128]{1,0:T(8,128)(2,1)S(1)}, bf16[768,128]{1,0:T(8,128)(2,1)S(1)}, u32[]{:S(2)}, u32[]{:S(2)}) collective-permute-start(bf16[768,128]{1,0:T(8,128)(2,1)S(1)} %get-tuple-element.40), channel_id=1, source_target_pairs={{0,2},{1,3},{2,0},{3,1},{4,6},{5,7},{6,4},{7,5},{8,10},{9,11},{10,... | collective-permute-start | bytes 589832 | tf_op jit(solution)/shard_map/ppermute | solution.py:383
  55.9 16.0 %collective-permute-start.11 = (bf16[768,128]{1,0:T(8,128)(2,1)S(1)}, bf16[768,128]{1,0:T(8,128)(2,1)S(1)}, u32[]{:S(2)}, u32[]{:S(2)}) collective-permute-start(bf16[768,128]{1,0:T(8,128)(2,1)S(1)} %get-tuple-element.34), channel_id=1, source_target_pairs={{0,2},{1,3},{2,0},{3,1},{4,6},{5,7},{6,4},{7,5},{8,10},{9,11},{10,... | collective-permute-start | bytes 589832 | tf_op jit(solution)/shard_map/ppermute | solution.py:383
  60.1 11.8 %collective-permute-start.13 = (bf16[768,128]{1,0:T(8,128)(2,1)S(1)}, bf16[768,128]{1,0:T(8,128)(2,1)S(1)}, u32[]{:S(2)}, u32[]{:S(2)}) collective-permute-start(bf16[768,128]{1,0:T(8,128)(2,1)S(1)} %add_convert_fusion.2), channel_id=1, source_target_pairs={{0,8},{1,9},{2,10},{3,11},{4,12},{5,13},{6,14},{7,15},{8,0},{9,1},... | collective-permute-start | bytes 589832 | tf_op jit(solution)/shard_map/ppermute | solution.py:383
  64.4 12.9 %collective-permute-start.15 = (bf16[768,128]{1,0:T(8,128)(2,1)S(1)}, bf16[768,128]{1,0:T(8,128)(2,1)S(1)}, u32[]{:S(2)}, u32[]{:S(2)}) collective-permute-start(bf16[768,128]{1,0:T(8,128)(2,1)S(1)} %add_convert_fusion.1), channel_id=1, source_target_pairs={{0,12},{1,13},{2,14},{3,15},{4,0},{5,1},{6,2},{7,3},{8,4},{9,5},{1... | collective-permute-start | bytes 589832 | tf_op jit(solution)/shard_map/ppermute | solution.py:383
  68.6 8.7 %collective-permute-start.17 = (bf16[768,128]{1,0:T(8,128)(2,1)S(1)}, bf16[768,128]{1,0:T(8,128)(2,1)S(1)}, u32[]{:S(2)}, u32[]{:S(2)}) collective-permute-start(bf16[768,128]{1,0:T(8,128)(2,1)S(1)} %add_convert_fusion), channel_id=1, source_target_pairs={{0,4},{1,5},{2,6},{3,7},{4,8},{5,9},{6,10},{7,11},{8,12},{9,13},{1... | collective-permute-start | bytes 589832 | tf_op jit(solution)/shard_map/ppermute | solution.py:383
  77.3 1.5 %copy-start.2 = (bf16[1024,256]{1,0:T(8,128)(2,1)S(1)}, bf16[1024,256]{1,0:T(8,128)(2,1)}, u32[]{:S(2)}) copy-start(bf16[1024,256]{1,0:T(8,128)(2,1)} %volume.1) | copy-start | bytes 1572868
  77.3 1.5 %collective-permute-start.18 = (f32[384,128]{1,0:T(8,128)S(1)}, f32[384,128]{1,0:T(8,128)S(1)}, u32[]{:S(2)}, u32[]{:S(2)}) collective-permute-start(f32[384,128]{1,0:T(8,128)S(1)} %get-tuple-element.44), channel_id=1, source_target_pairs={{0,1},{1,0},{2,3},{3,2},{4,5},{5,4},{6,7},{7,6},{8,9},{9,8},{10,11... | collective-permute-start | bytes 589832 | tf_op jit(solution)/shard_map/ppermute | solution.py:383
